TPU v7x, 512 devices: a whole 4x4x16 slice. The times are simulated.
512 devices in a mesh: offset: 8 (over y_lo, x), slab: 64 (over y_hi, z, core).
Axes of the slice: x: 4, y: 4 (y_hi: 2, y_lo: 2; y = y_hi * 2 + y_lo), z: 16, core: 2. Of those that a mesh axis runs over, the one named last changes fastest.
Arguments:
- traces: bfloat16 [8, 8192, 256], P('offset', 'slab'), may hold values from -6 to 6
- centre_ids: int32 [8, 8192, 1], P('offset', 'slab'), may hold values from 0 to 63; in each aligned block of 128 rows (0 to 127, 128 to 255, ..., all dimensions but the last counted through in order) at most 6 rows name the same one
- midpoint_bins: int32 [8, 8192], P('offset', 'slab'), may hold values from 0 to 15
- ray_times: float32 [8, 64, 7, 16, 256], P('offset', 'slab'), may hold values from 16 to 240
- ray_amps: float32 [8, 64, 7, 16, 256], P('offset', 'slab'), may hold values from 0.2 to 2
- beam_lateral: float32 [8, 64, 7, 16], P('offset'), may hold values from 0 to 128
- footprint: int32 [64, 7, 2], replicated, may hold values from 0 to 128, as said below
Outputs:
- image: float32 [256, 8192], P('offset', 'slab')
Inputs may be any that keep to these rules, and one draw needn't show every extreme that they name: `centre_ids`: within the rows of one device no centre is named by more than 6 rows. footprint[c, w, 0] is below 64 and footprint[c, w, 1] above it; at w = 3, a centre's own slab, they are 0 and 128.
All inputs are finite; a program needn't handle non-finite values.
Results may differ from a plain program's by a relative error of at most 0.0049.
Values may be sent and summed in bfloat16 or wider, within the bound.
No kernel may reach another device: no remote copies, remote signals or barrier semaphores. Data moves between devices by JAX's collectives and lax.ppermute only.
A program may use at most 64 MiB of HBM per device.

v0:
```python
import math

import jax
import jax.numpy as jnp
from jax import lax
from jax.sharding import PartitionSpec as P

NT = 256
NF = 64
KLO = 8
P_SIZE = 16
BINS = 16
CAP = 6
WIN = 7
XW = 128


two_pi = 2.0 * math.pi
slow_step = 0.25
width_scale = 200.0


def shifted(shard, axis, by):
    count = lax.axis_size(axis)
    pairs = [(i, i + by) for i in range(count) if 0 <= i + by < count]
    return lax.ppermute(shard, axis, pairs)


def dft_table():
    sample = jnp.arange(NT, dtype=jnp.int32)[:, None]
    bin_index = jnp.arange(NF, dtype=jnp.int32)[None, :] + KLO
    turns = (sample * bin_index % NT).astype(jnp.float32) * (two_pi / NT)
    return jnp.concatenate([jnp.cos(turns), -jnp.sin(turns)], axis=1)


def omegas():
    return (jnp.arange(NF, dtype=jnp.int32) + KLO).astype(jnp.float32) * (two_pi / NT)


def slowness():
    return (
        jnp.arange(P_SIZE, dtype=jnp.int32).astype(jnp.float32) - (P_SIZE - 1) / 2.0
    ) * slow_step


def beam_blocks(beams, times_in, amps_in, lateral, first_col, end_col):
    freq = omegas()
    phase = freq[None, :, None] * times_in[:, None, :]
    depth = times_in.shape[1]
    u_block = jnp.stack(
        [amps_in[:, None, :] * jnp.cos(phase), -amps_in[:, None, :] * jnp.sin(phase)]
    )
    u_block = u_block.reshape(2 * P_SIZE * NF, depth).astype(jnp.bfloat16)
    col_index = jnp.arange(XW, dtype=jnp.int32)
    inside = ((col_index >= first_col) & (col_index < end_col)).astype(jnp.float32)
    columns = col_index.astype(jnp.float32)
    gauss = jnp.exp(
        -((columns[None, None, :] - lateral[:, None, None]) ** 2)
        * freq[None, :, None]
        / width_scale
    )
    gauss = gauss * inside[None, None, :] / math.sqrt(P_SIZE * NF)
    beam_re = beams[:, :NF].astype(jnp.float32)[:, :, None]
    beam_im = beams[:, NF:].astype(jnp.float32)[:, :, None]
    v_block = (
        jnp.stack([beam_re * gauss, beam_im * gauss])
        .reshape(2 * P_SIZE * NF, XW)
        .astype(jnp.bfloat16)
    )
    return lax.dot_general(
        u_block, v_block, (((0,), (0,)), ((), ())), preferred_element_type=jnp.float32
    )


def shards(traces, centre_ids, midpoint_bins, ray_times, ray_amps, beam_lateral, footprint):
    my_slab = lax.axis_index("slab")
    slab_count = lax.axis_size("slab")
    half_win = (WIN - 1) // 2
    centre_of = centre_ids[0, :, 0]
    one_hot = (centre_of[:, None] == jnp.arange(slab_count, dtype=jnp.int32)[None, :]).astype(
        jnp.int32
    )
    slot_rank = jnp.sum((jnp.cumsum(one_hot, axis=0) - 1) * one_hot, axis=1)
    target_row = centre_of * CAP + slot_rank
    samples = jnp.zeros((slab_count * CAP, NT), jnp.bfloat16).at[target_row].set(traces[0])
    places = (midpoint_bins[0].astype(jnp.float32) - (BINS - 1) / 2.0).astype(jnp.bfloat16)
    place_slots = jnp.zeros((slab_count * CAP,), jnp.bfloat16).at[target_row].set(places)
    arrived, arrived_place = (
        lax.all_to_all(
            samples.reshape(slab_count, CAP, NT), "slab", split_axis=0, concat_axis=0, tiled=True
        ),
        lax.all_to_all(
            place_slots.reshape(slab_count, CAP), "slab", split_axis=0, concat_axis=0, tiled=True
        ),
    )
    spectrum = jnp.dot(
        arrived.reshape(slab_count * CAP, NT).astype(jnp.float32),
        dft_table(),
        precision=lax.Precision.HIGHEST,
    )
    position = arrived_place.reshape(slab_count * CAP).astype(jnp.float32)
    phase = omegas()[None, None, :] * slowness()[None, :, None] * position[:, None, None]
    cosine = jnp.cos(phase)
    sine_part = jnp.sin(phase)
    spec_re = spectrum[:, None, :NF]
    spec_im = spectrum[:, None, NF:]
    beam_re = jnp.sum(spec_re * cosine + spec_im * sine_part, axis=0)
    beam_im = jnp.sum(spec_im * cosine - spec_re * sine_part, axis=0)
    scale = 1.0 / math.sqrt(NT * traces.shape[1])
    beams = (jnp.concatenate([beam_re, beam_im], axis=1) * scale).astype(jnp.bfloat16)
    depth = ray_times.shape[4]
    partial_image = jnp.zeros((depth, XW), jnp.float32)
    lateral_own = lax.dynamic_index_in_dim(beam_lateral[0], my_slab, 0, keepdims=False)
    foot_own = lax.dynamic_index_in_dim(footprint, my_slab, 0, keepdims=False)
    for window in range(WIN):
        step_by = window - half_win
        contrib = beam_blocks(
            beams,
            ray_times[0, 0, window],
            ray_amps[0, 0, window],
            lateral_own[window],
            foot_own[window, 0],
            foot_own[window, 1],
        )
        if step_by == 0:
            partial_image = partial_image + contrib
        else:
            partial_image = partial_image + shifted(contrib, "slab", step_by)
    return lax.psum_scatter(partial_image, "offset", scatter_dimension=0, tiled=True)


def solution(mesh):
    return jax.shard_map(
        shards,
        mesh=mesh,
        in_specs=(
            P("offset", "slab", None),
            P("offset", "slab", None),
            P("offset", "slab"),
            P("offset", "slab", None, None, None),
            P("offset", "slab", None, None, None),
            P("offset", None, None, None),
            P(),
        ),
        out_specs=P("offset", "slab"),
        check_vma=False,
    )
```

profile of v0, /device:TPU:32, one launch (start us, length us, event | category | flops | bytes accessed | tf_op | source)
XLA Modules:
  0.0 180.1 jit_solution(13763766085595332829)
XLA Ops:
  6.5 0.7 convert_bitcast_fusion
  7.2 0.7 fusion.92
  8.2 0.8 select_reduce_fusion
  9.0 0.7 fusion.94
  9.7 1.3 scatter_custom_fusion.1
  11.0 0.8 all_to_all.12
  11.8 18.4 %all-to-all-start.1 = ((bf16[64,1,6]{2,1,0:T(2,128)(2,1)}), bf16[64,1,6]{2,1,0:T(2,128)(2,1)S(1)}, u32[]{:S(2)}, u32[]{:S(2)}) async-start(bf16[64,1,6]{2,1,0:T(2,128)(2,1)} %all_to_all.12), calls=%async_computation.1 | async-start | bytes 65536 | tf_op jit(solution)/shard_map/all_to_all | solution.py:92
  30.2 0.8 constant_dynamic-slice_fusion
  31.1 0.7 fusion.117
  31.9 0.6 slice_bitcast_fusion.6
  33.1 0.7 broadcast_multiply_fusion
  33.7 2.6 %and_convert_fusion.2 = (f32[128]{0:T(128)S(1)}, f32[128]{0:T(128)S(1)}) fusion(s32[]{:T(128)} %bitcast.34, s32[]{:T(128)} %bitcast.33, s32[]{:T(128)} %bitcast.28, s32[]{:T(128)} %bitcast.27), kind=kLoop, calls=%fused_computation.184 | loop fusion | flops 1024 | bytes 1040 | tf_op jit(solution)/shard_map/convert_element_type | solution.py:55
  36.3 2.6 %and_convert_fusion = (f32[128]{0:T(128)S(1)}, f32[128]{0:T(128)S(1)}) fusion(s32[]{:T(128)} %bitcast.46, s32[]{:T(128)} %bitcast.45, s32[]{:T(128)} %bitcast.40, s32[]{:T(128)} %bitcast.39), kind=kLoop, calls=%fused_computation.182 | loop fusion | flops 1024 | bytes 1040 | tf_op jit(solution)/shard_map/convert_element_type | solution.py:55
  39.2 0.7 multiply_negate_fusion.3
  39.9 2.5 %and_convert_fusion.4 = (f32[128]{0:T(128)S(1)}, f32[128]{0:T(128)S(1)}) fusion(s32[]{:T(128)} %bitcast.22, s32[]{:T(128)} %bitcast.21, s32[]{:T(128)} %bitcast.16, s32[]{:T(128)} %bitcast.15), kind=kLoop, calls=%fused_computation.186 | loop fusion | flops 1024 | bytes 1040 | tf_op jit(solution)/shard_map/convert_element_type | solution.py:55
  42.4 1.1 scatter_custom_fusion
  43.5 0.8 reshape.749
  44.3 15.2 %all-to-all-start = ((bf16[64,6,256]{2,1,0:T(8,128)(2,1)}), bf16[64,6,256]{2,1,0:T(8,128)(2,1)S(1)}, u32[]{:S(2)}, u32[]{:S(2)}) async-start(bf16[64,6,256]{2,1,0:T(8,128)(2,1)} %reshape.749), calls=%async_computation | async-start | bytes 524288 | tf_op jit(solution)/shard_map/all_to_all | solution.py:89
  59.7 1.3 and_convert_fusion.6
  61.1 4.2 %fusion.9 = (bf16[1,16,64,256]{3,2,1,0:T(8,128)(2,1)S(1)}, bf16[1,16,64,256]{3,2,1,0:T(8,128)(2,1)S(1)}) fusion(f32[16,256]{1,0:T(8,128)S(1)} %get-tuple-element.27, f32[64]{0:T(128)S(1)} %convert_multiply_fusion.2, f32[16,256]{1,0:T(8,128)S(1)} %get-tuple-element.144, f32[16,256]{1,0:T(8,128)S(1)} %get-tuple-element.36), kind=kLoop, calls=%fused_computation.34 | loop fusion | flops 1310720 | bytes 1097984 | tf_op jit(solution)/shard_map/convert.27
  65.3 24.7 %fusion.21 = (bf16[1,16,64,256]{3,2,1,0:T(8,128)(2,1)S(1)}, bf16[1,16,64,256]{3,2,1,0:T(8,128)(2,1)S(1)}, bf16[1,16,64,256]{3,2,1,0:T(8,128)(2,1)}, bf16[1,16,64...) fusion(f32[16,256]{1,0:T(8,128)S(1)} %get-tuple-element.23, ...), kind=kLoop, calls=%fused_computation.46 | loop fusion | flops 7864320 | bytes 6586624 | tf_op jit(solution)/shard_map/convert.15
  91.0 6.9 %fusion.5 = (f32[16,64]{1,0:T(8,128)S(1)}, f32[16,64]{1,0:T(8,128)S(1)}) fusion(f32[384,64]{0,1:T(8,128)S(1)} %get-tuple-element.15, f32[384]{0:T(512)S(1)} %reshape.751, f32[16,64]{1,0:T(8,128)S(1)} %copy-done.26, f32[384,64]{0,1:T(8,128)S(1)} %get-tuple-element.14), kind=kLoop, calls=%fused_computation.9 | loop fusion | flops 3536896 | bytes 210432 | tf_op jit(solution)/shard_map/reduce_sum | solution.py:107
  98.1 1.6 multiply_convert_fusion.1
  100.2 1.3 collective-permute-start
  102.1 2.4 %collective-permute-start.1 = (f32[256,128]{1,0:T(8,128)S(1)}, f32[256,128]{1,0:T(8,128)S(1)}, u32[]{:S(2)}, u32[]{:S(2)}) collective-permute-start(f32[256,128]{1,0:T(8,128)S(1)} %convolution_bitcast_fusion.5), channel_id=1, source_target_pairs={{2,0},{3,1},{4,2},{5,3},{6,4},{7,5},{8,6},{9,7},{10,8},{11,9},{12,... | collective-permute-start | bytes 393224 | tf_op jit(solution)/shard_map/ppermute | solution.py:26
  105.0 1.9 %collective-permute-start.2 = (f32[256,128]{1,0:T(8,128)S(1)}, f32[256,128]{1,0:T(8,128)S(1)}, u32[]{:S(2)}, u32[]{:S(2)}) collective-permute-start(f32[256,128]{1,0:T(8,128)S(1)} %convolution_bitcast_fusion.4), channel_id=1, source_target_pairs={{1,0},{2,1},{3,2},{4,3},{5,4},{6,5},{7,6},{8,7},{9,8},{10,9},{11,1... | collective-permute-start | bytes 393224 | tf_op jit(solution)/shard_map/ppermute | solution.py:26
  107.4 2.7 %collective-permute-start.3 = (f32[256,128]{1,0:T(8,128)S(1)}, f32[256,128]{1,0:T(8,128)S(1)}, u32[]{:S(2)}, u32[]{:S(2)}) collective-permute-start(f32[256,128]{1,0:T(8,128)S(1)} %convolution_bitcast_fusion.2), channel_id=1, source_target_pairs={{0,1},{1,2},{2,3},{3,4},{4,5},{5,6},{6,7},{7,8},{8,9},{9,10},{10,1... | collective-permute-start | bytes 393224 | tf_op jit(solution)/shard_map/ppermute | solution.py:26
  110.6 3.6 %collective-permute-start.4 = (f32[256,128]{1,0:T(8,128)S(1)}, f32[256,128]{1,0:T(8,128)S(1)}, u32[]{:S(2)}, u32[]{:S(2)}) collective-permute-start(f32[256,128]{1,0:T(8,128)S(1)} %convolution_bitcast_fusion.1), channel_id=1, source_target_pairs={{0,2},{1,3},{2,4},{3,5},{4,6},{5,7},{6,8},{7,9},{8,10},{9,11},{10,... | collective-permute-start | bytes 393224 | tf_op jit(solution)/shard_map/ppermute | solution.py:26
  114.8 5.7 %collective-permute-start.5 = (f32[256,128]{1,0:T(8,128)S(1)}, f32[256,128]{1,0:T(8,128)S(1)}, u32[]{:S(2)}, u32[]{:S(2)}) collective-permute-start(f32[256,128]{1,0:T(8,128)S(1)} %convolution_bitcast_fusion), channel_id=1, source_target_pairs={{0,3},{1,4},{2,5},{3,6},{4,7},{5,8},{6,9},{7,10},{8,11},{9,12},{10... | collective-permute-start | bytes 393224 | tf_op jit(solution)/shard_map/ppermute | solution.py:26
  120.6 4.1 %collective-permute-done.5 = f32[256,128]{1,0:T(8,128)S(1)} collective-permute-done((f32[256,128]{1,0:T(8,128)S(1)}, f32[256,128]{1,0:T(8,128)S(1)}, u32[]{:S(2)}, u32[]{:S(2)}) %collective-permute-start.5) | collective-permute-done | bytes 131104 | tf_op jit(solution)/shard_map/ppermute | solution.py:26
  124.6 1.1 add_add_fusion
  125.8 47.5 %reduce-scatter.2.cloned.1.call-done = f32[32,128]{1,0:T(8,128)} async-done(((f32[256,128]{1,0:T(8,128)}), f32[32,128]{1,0:T(8,128)}) %reduce-scatter.2.cloned.1.call-update) | async-done | bytes 16400 | tf_op jit(solution)/shard_map/reduce_scatter | solution.py:129
  (85 shorter events, 5.5 us)
Async XLA Ops:
  6.5 35.9 %copy-start = (bf16[1,128,256]{2,1,0:T(8,128)(2,1)S(1)}, bf16[1,128,256]{2,1,0:T(8,128)(2,1)}, u32[]{:S(2)}) copy-start(bf16[1,128,256]{2,1,0:T(8,128)(2,1)} %param.7) | copy-start | bytes 196612
  6.5 25.3 %copy-start.10 = (f32[1,1,7,16,256]{4,3,2,1,0:T(8,128)S(1)}, f32[1,1,7,16,256]{4,3,2,1,0:T(8,128)}, u32[]{:S(2)}) copy-start(f32[1,1,7,16,256]{4,3,2,1,0:T(8,128)} %param.11) | copy-start | bytes 344068
  6.5 25.3 %copy-start.11 = (f32[1,1,7,16,256]{4,3,2,1,0:T(8,128)S(1)}, f32[1,1,7,16,256]{4,3,2,1,0:T(8,128)}, u32[]{:S(2)}) copy-start(f32[1,1,7,16,256]{4,3,2,1,0:T(8,128)} %param.10) | copy-start | bytes 344068
  11.8 32.5 %all-to-all-start.1 = ((bf16[64,1,6]{2,1,0:T(2,128)(2,1)}), bf16[64,1,6]{2,1,0:T(2,128)(2,1)S(1)}, u32[]{:S(2)}, u32[]{:S(2)}) async-start(bf16[64,1,6]{2,1,0:T(2,128)(2,1)} %all_to_all.12), calls=%async_computation.1 | async-start | bytes 65536 | tf_op jit(solution)/shard_map/all_to_all | solution.py:92
  30.2 8.6 %copy-start.18 = (f32[1,64,7,16]{1,3,2,0:T(8,128)S(1)}, f32[1,64,7,16]{1,3,2,0:T(8,128)}, u32[]{:S(2)}) copy-start(f32[1,64,7,16]{1,3,2,0:T(8,128)} %param.12) | copy-start | bytes 86020
  44.3 45.9 %all-to-all-start = ((bf16[64,6,256]{2,1,0:T(8,128)(2,1)}), bf16[64,6,256]{2,1,0:T(8,128)(2,1)S(1)}, u32[]{:S(2)}, u32[]{:S(2)}) async-start(bf16[64,6,256]{2,1,0:T(8,128)(2,1)} %reshape.749), calls=%async_computation | async-start | bytes 524288 | tf_op jit(solution)/shard_map/all_to_all | solution.py:89
  59.5 113.7 %reduce-scatter.2.cloned.1.call-start = ((), (), s32[]{:S(2)}) async-start(), calls=%async_computation.3 | async-start | bytes 147456 | tf_op jit(solution)/shard_map/reduce_scatter | solution.py:129
  61.0 4.2 %copy-start.12 = (f32[16,256]{1,0:T(8,128)S(1)}, f32[16,256]{1,0:T(8,128)}, u32[]{:S(2)}) copy-start(f32[16,256]{1,0:T(8,128)} %get-tuple-element.142) | copy-start | bytes 49156
  61.0 4.2 %copy-start.13 = (f32[16,256]{1,0:T(8,128)S(1)}, f32[16,256]{1,0:T(8,128)}, u32[]{:S(2)}) copy-start(f32[16,256]{1,0:T(8,128)} %get-tuple-element.143) | copy-start | bytes 49156
  61.0 4.2 %copy-start.14 = (f32[16,256]{1,0:T(8,128)S(1)}, f32[16,256]{1,0:T(8,128)}, u32[]{:S(2)}) copy-start(f32[16,256]{1,0:T(8,128)} %get-tuple-element.145) | copy-start | bytes 49156
  61.0 4.2 %copy-start.15 = (f32[16,256]{1,0:T(8,128)S(1)}, f32[16,256]{1,0:T(8,128)}, u32[]{:S(2)}) copy-start(f32[16,256]{1,0:T(8,128)} %get-tuple-element.146) | copy-start | bytes 49156
  61.0 4.2 %copy-start.16 = (f32[16,256]{1,0:T(8,128)S(1)}, f32[16,256]{1,0:T(8,128)}, u32[]{:S(2)}) copy-start(f32[16,256]{1,0:T(8,128)} %get-tuple-element.147) | copy-start | bytes 49156
  61.1 4.2 %copy-start.17 = (f32[16,256]{1,0:T(8,128)S(1)}, f32[16,256]{1,0:T(8,128)}, u32[]{:S(2)}) copy-start(f32[16,256]{1,0:T(8,128)} %get-tuple-element.148) | copy-start | bytes 49156
  91.0 7.1 %copy-start.19 = (f32[16,128]{1,0:T(8,128)S(1)}, f32[16,128]{1,0:T(8,128)}, u32[]{:S(2)}) copy-start(f32[16,128]{1,0:T(8,128)} %get-tuple-element.133) | copy-start | bytes 24580
  91.0 7.1 %copy-start.20 = (f32[16,128]{1,0:T(8,128)S(1)}, f32[16,128]{1,0:T(8,128)}, u32[]{:S(2)}) copy-start(f32[16,128]{1,0:T(8,128)} %get-tuple-element.134) | copy-start | bytes 24580
  91.0 7.1 %copy-start.21 = (f32[16,128]{1,0:T(8,128)S(1)}, f32[16,128]{1,0:T(8,128)}, u32[]{:S(2)}) copy-start(f32[16,128]{1,0:T(8,128)} %get-tuple-element.135) | copy-start | bytes 24580
  91.0 7.1 %copy-start.22 = (f32[16,128]{1,0:T(8,128)S(1)}, f32[16,128]{1,0:T(8,128)}, u32[]{:S(2)}) copy-start(f32[16,128]{1,0:T(8,128)} %get-tuple-element.136) | copy-start | bytes 24580
  91.0 7.1 %copy-start.23 = (f32[16,128]{1,0:T(8,128)S(1)}, f32[16,128]{1,0:T(8,128)}, u32[]{:S(2)}) copy-start(f32[16,128]{1,0:T(8,128)} %get-tuple-element.137) | copy-start | bytes 24580
  91.0 7.1 %copy-start.24 = (f32[16,128]{1,0:T(8,128)S(1)}, f32[16,128]{1,0:T(8,128)}, u32[]{:S(2)}) copy-start(f32[16,128]{1,0:T(8,128)} %get-tuple-element.138) | copy-start | bytes 24580
  91.0 7.1 %copy-start.25 = (f32[16,128]{1,0:T(8,128)S(1)}, f32[16,128]{1,0:T(8,128)}, u32[]{:S(2)}) copy-start(f32[16,128]{1,0:T(8,128)} %get-tuple-element.139) | copy-start | bytes 24580
  100.2 14.5 %collective-permute-start = (f32[256,128]{1,0:T(8,128)S(1)}, f32[256,128]{1,0:T(8,128)S(1)}, u32[]{:S(2)}, u32[]{:S(2)}) collective-permute-start(f32[256,128]{1,0:T(8,128)S(1)} %convolution_bitcast_fusion.6), channel_id=1, source_target_pairs={{3,0},{4,1},{5,2},{6,3},{7,4},{8,5},{9,6},{10,7},{11,8},{12,9},{13... | collective-permute-start | bytes 393224 | tf_op jit(solution)/shard_map/ppermute | solution.py:26
  101.6 2.9 %copy-start.6 = (bf16[1,16,64,256]{3,2,1,0:T(8,128)(2,1)S(1)}, bf16[1,16,64,256]{3,2,1,0:T(8,128)(2,1)}, u32[]{:S(2)}) copy-start(bf16[1,16,64,256]{3,2,1,0:T(8,128)(2,1)} %get-tuple-element.125) | copy-start | bytes 1572868
  101.6 2.9 %copy-start.7 = (bf16[1,16,64,256]{3,2,1,0:T(8,128)(2,1)S(1)}, bf16[1,16,64,256]{3,2,1,0:T(8,128)(2,1)}, u32[]{:S(2)}) copy-start(bf16[1,16,64,256]{3,2,1,0:T(8,128)(2,1)} %get-tuple-element.126) | copy-start | bytes 1572868
  102.1 18.5 %collective-permute-start.1 = (f32[256,128]{1,0:T(8,128)S(1)}, f32[256,128]{1,0:T(8,128)S(1)}, u32[]{:S(2)}, u32[]{:S(2)}) collective-permute-start(f32[256,128]{1,0:T(8,128)S(1)} %convolution_bitcast_fusion.5), channel_id=1, source_target_pairs={{2,0},{3,1},{4,2},{5,3},{6,4},{7,5},{8,6},{9,7},{10,8},{11,9},{12,... | collective-permute-start | bytes 393224 | tf_op jit(solution)/shard_map/ppermute | solution.py:26
  104.5 2.4 %copy-start.4 = (bf16[1,16,64,256]{3,2,1,0:T(8,128)(2,1)S(1)}, bf16[1,16,64,256]{3,2,1,0:T(8,128)(2,1)}, u32[]{:S(2)}) copy-start(bf16[1,16,64,256]{3,2,1,0:T(8,128)(2,1)} %get-tuple-element.127) | copy-start | bytes 1572868
  105.0 15.6 %collective-permute-start.2 = (f32[256,128]{1,0:T(8,128)S(1)}, f32[256,128]{1,0:T(8,128)S(1)}, u32[]{:S(2)}, u32[]{:S(2)}) collective-permute-start(f32[256,128]{1,0:T(8,128)S(1)} %convolution_bitcast_fusion.4), channel_id=1, source_target_pairs={{1,0},{2,1},{3,2},{4,3},{5,4},{6,5},{7,6},{8,7},{9,8},{10,9},{11,1... | collective-permute-start | bytes 393224 | tf_op jit(solution)/shard_map/ppermute | solution.py:26
  106.9 3.2 %copy-start.2 = (bf16[1,16,64,256]{3,2,1,0:T(8,128)(2,1)S(1)}, bf16[1,16,64,256]{3,2,1,0:T(8,128)(2,1)}, u32[]{:S(2)}) copy-start(bf16[1,16,64,256]{3,2,1,0:T(8,128)(2,1)} %get-tuple-element.129) | copy-start | bytes 1572868
  106.9 3.2 %copy-start.3 = (bf16[1,16,64,256]{3,2,1,0:T(8,128)(2,1)S(1)}, bf16[1,16,64,256]{3,2,1,0:T(8,128)(2,1)}, u32[]{:S(2)}) copy-start(bf16[1,16,64,256]{3,2,1,0:T(8,128)(2,1)} %get-tuple-element.130) | copy-start | bytes 1572868
  107.4 13.1 %collective-permute-start.3 = (f32[256,128]{1,0:T(8,128)S(1)}, f32[256,128]{1,0:T(8,128)S(1)}, u32[]{:S(2)}, u32[]{:S(2)}) collective-permute-start(f32[256,128]{1,0:T(8,128)S(1)} %convolution_bitcast_fusion.2), channel_id=1, source_target_pairs={{0,1},{1,2},{2,3},{3,4},{4,5},{5,6},{6,7},{7,8},{8,9},{9,10},{10,1... | collective-permute-start | bytes 393224 | tf_op jit(solution)/shard_map/ppermute | solution.py:26
  110.1 4.2 %copy-start.1 = (bf16[1,16,64,256]{3,2,1,0:T(8,128)(2,1)S(1)}, bf16[1,16,64,256]{3,2,1,0:T(8,128)(2,1)}, u32[]{:S(2)}) copy-start(bf16[1,16,64,256]{3,2,1,0:T(8,128)(2,1)} %get-tuple-element.132) | copy-start | bytes 1572868
  110.6 9.9 %collective-permute-start.4 = (f32[256,128]{1,0:T(8,128)S(1)}, f32[256,128]{1,0:T(8,128)S(1)}, u32[]{:S(2)}, u32[]{:S(2)}) collective-permute-start(f32[256,128]{1,0:T(8,128)S(1)} %convolution_bitcast_fusion.1), channel_id=1, source_target_pairs={{0,2},{1,3},{2,4},{3,5},{4,6},{5,7},{6,8},{7,9},{8,10},{9,11},{10,... | collective-permute-start | bytes 393224 | tf_op jit(solution)/shard_map/ppermute | solution.py:26
  114.8 9.8 %collective-permute-start.5 = (f32[256,128]{1,0:T(8,128)S(1)}, f32[256,128]{1,0:T(8,128)S(1)}, u32[]{:S(2)}, u32[]{:S(2)}) collective-permute-start(f32[256,128]{1,0:T(8,128)S(1)} %convolution_bitcast_fusion), channel_id=1, source_target_pairs={{0,3},{1,4},{2,5},{3,6},{4,7},{5,8},{6,9},{7,10},{8,11},{9,12},{10... | collective-permute-start | bytes 393224 | tf_op jit(solution)/shard_map/ppermute | solution.py:26
  (4 other events, 6.8 us)
Sparse Core Ops, SparseCore 0:
  125.9 47.2 reduce-scatter.1
where the time goes:
time: 181 us; the launch traced here: 180 us
  other arithmetic  51.5 us (28%)
  waiting for transfers between devices  51.5 us (28%)
  starting transfers between devices  51.4 us (28%)
  between operations  14 us (8%)
  local copies, waits for them, and re-layouts  7.12 us (4%)
  matrix products  4.47 us (2%)
    reduce_scatter x1, waiting for transfers between devices, shards(): lax.psum_scatter(partial_image, 'offset', scatter_dimension=0, tiled=True)  47.5 us
    another operation x3, other arithmetic  30.4 us
    all_to_all x1, starting transfers between devices, shards(): lax.all_to_all(place_slots.reshape(slab_count, CAP), 'slab', split_axis=0...  18.4 us
    ppermute x6, starting transfers between devices, shifted(): return lax.ppermute(shard, axis, pairs)  17.6 us
    all_to_all x1, starting transfers between devices, shards(): lax.all_to_all(samples.reshape(slab_count, CAP, NT), 'slab', split_axis=0...  15.2 us
    convert_element_type x4, other arithmetic, beam_blocks(): ((col_index >= first_col) & (col_index < end_col)).astype(jnp.float32)  8.87 us
    reduce_sum x1, other arithmetic, shards(): beam_re = jnp.sum(spec_re * cosine + spec_im * sine_part, axis=0)  6.88 us
    ppermute x6, waiting for transfers between devices, shifted(): return lax.ppermute(shard, axis, pairs)  4.07 us
  transfers between devices with their start and end apart: 9, of which 2 were waited for; matrix products, arithmetic and copies ran while one was open for 26% of the time, Pallas kernels for 0%

commit v1 on v0

v1 whole, which is shorter than its diff:
```python
import math

import jax
import jax.numpy as jnp
import numpy as np
from jax import lax
from jax.experimental import pallas as pl
from jax.experimental.pallas import tpu as pltpu
from jax.sharding import PartitionSpec as P

NT = 256
NF = 64
KLO = 8
P_SIZE = 16
BINS = 16
CAP = 6
WIN = 7
XW = 128
ROWS = 8
LANES = 128
HALF = (WIN - 1) // 2
KEEP = HALF + 1

two_pi = 2.0 * math.pi
slow_step = 0.25
width_scale = 200.0
omega_step = two_pi / NT

f32 = jnp.float32
bf16 = jnp.bfloat16


def dft_tables():
    sample = np.arange(NT)[:, None]
    turns = (sample * (np.arange(NF)[None, :] + KLO) % NT) * (two_pi / NT)
    table = np.concatenate([np.cos(turns), -np.sin(turns)], axis=1).astype(np.float32)
    high = table.astype(bf16)
    low = (table - high.astype(np.float32)).astype(bf16)
    return high, low


def slant_tables():
    freq = (np.arange(NF) + KLO) * omega_step
    slow = (np.arange(P_SIZE) - (P_SIZE - 1) / 2.0) * slow_step
    place = np.arange(BINS) - (BINS - 1) / 2.0
    phase = place[:, None, None] * freq[None, :, None] * slow[None, None, :]
    phase = phase.reshape(BINS, NF * P_SIZE)
    spread = np.arange(2 * NF)[:, None] % NF == np.arange(NF * P_SIZE)[None, :] // P_SIZE
    return (
        np.cos(phase).astype(np.float32),
        np.sin(phase).astype(np.float32),
        spread.astype(np.float32).astype(bf16),
    )


def iota(shape, dim):
    return lax.broadcasted_iota(jnp.int32, shape, dim)


def dot(a, b):
    return jnp.dot(a, b, preferred_element_type=f32)


def route_kernel(ids_ref, bins_ref, traces_ref, high_ref, low_ref, out_ref):
    count = traces_ref.shape[0]
    square = (count, count)
    row, col = iota(square, 0), iota(square, 1)
    ids_down = jnp.broadcast_to(ids_ref[...], square)
    ids_across = jnp.sum(jnp.where(row == col, ids_down, 0).astype(f32), axis=0, keepdims=True)
    ids_across = ids_across.astype(jnp.int32)
    same = ids_down == ids_across
    rank_across = jnp.sum(jnp.where(same & (row < col), 1.0, 0.0), axis=0, keepdims=True)
    rank_down = jnp.sum(jnp.where(same & (col < row), 1.0, 0.0), axis=1, keepdims=True)
    place_across = bins_ref[...].astype(f32) - (BINS - 1) / 2.0
    place_down = jnp.sum(jnp.where(row == col, place_across, 0.0), axis=1, keepdims=True)
    traces = traces_ref[...]
    spectrum = dot(traces, high_ref[...]) + dot(traces, low_ref[...])
    places = jnp.where(col == rank_down.astype(jnp.int32), place_down, 0.0)
    values = jnp.concatenate([spectrum, places], axis=1).astype(bf16)
    out_rows = out_ref.shape[0]
    slot = iota((out_rows, count), 0)
    place_row = slot % ROWS == CAP
    target = ids_across * ROWS + rank_across.astype(jnp.int32)
    pick = (slot == target) | (place_row & (slot // ROWS == ids_across))
    picked = dot(jnp.where(pick, 1.0, 0.0).astype(bf16), values)
    out_ref[...] = jnp.where(place_row, picked[:, LANES:], picked[:, :LANES]).astype(bf16)


def slant_stack(arrived, spread, cosine, sine, scale):
    rows = arrived.shape[0]
    full = arrived.astype(f32).reshape(rows // ROWS, ROWS, LANES)
    sub, lane = iota((rows // ROWS, ROWS, LANES), 1), iota((rows // ROWS, ROWS, LANES), 2)
    own = jnp.where(sub == lane, jnp.broadcast_to(full[:, CAP : CAP + 1, :], full.shape), 0.0)
    own = own.reshape(rows, LANES).astype(bf16)
    place = dot(own, jnp.ones((LANES, LANES), bf16))
    bin_place = iota((rows, LANES), 1).astype(f32) - (BINS - 1) / 2.0
    in_bin = jnp.where((place == bin_place) & (place != 0.0), 1.0, 0.0).astype(bf16)
    binned = lax.dot_general(
        in_bin, arrived, (((0,), (0,)), ((), ())), preferred_element_type=f32
    )[:BINS]
    real = iota((BINS, LANES), 1) < NF
    binned_re = jnp.where(real, binned, 0.0)
    binned_im = jnp.where(real, 0.0, binned)
    parts = []
    for part in (binned_re, binned_im):
        high = part.astype(bf16)
        parts += [high, (part - high.astype(f32)).astype(bf16)]
    wide = dot(jnp.concatenate(parts, axis=0), spread)
    wide_re = wide[:BINS] + wide[BINS : 2 * BINS]
    wide_im = wide[2 * BINS : 3 * BINS] + wide[3 * BINS :]
    beam_re = jnp.sum(wide_re * cosine + wide_im * sine, axis=0, keepdims=True)
    beam_im = jnp.sum(wide_im * cosine - wide_re * sine, axis=0, keepdims=True)
    return (
        (beam_re * scale).astype(bf16).astype(f32),
        (beam_im * scale).astype(bf16).astype(f32),
    )


def cos_sin_turns(turns):
    half = (turns - 0.5) * math.pi
    sq = half * half
    sin_of = 1.0 / 6227020800.0
    for divisor in (-39916800.0, 362880.0, -5040.0, 120.0, -6.0, 1.0):
        sin_of = sin_of * sq + 1.0 / divisor
    sin_of = sin_of * half
    cos_of = 1.0 / 479001600.0
    for divisor in (-3628800.0, 40320.0, -720.0, 24.0, -2.0, 1.0):
        cos_of = cos_of * sq + 1.0 / divisor
    return 2.0 * sin_of * sin_of - 1.0, -2.0 * sin_of * cos_of


def fill_u(u_ref, times, amps):
    cos_1, sin_1 = cos_sin_turns(times * (1.0 / NT))
    power = (cos_1, sin_1)

    def times_of(a, b):
        return a[0] * b[0] - a[1] * b[1], a[0] * b[1] + a[1] * b[0]

    one = power
    two = times_of(one, one)
    four = times_of(two, two)
    eight = times_of(four, four)
    start = (amps * eight[0], amps * eight[1])
    walk = [start]
    walk.append(times_of(start, one))
    walk.append(times_of(start, two))
    walk.append(times_of(walk[1], two))
    values = [(c, -s) for c, s in walk]
    factor = 2.0 * two[0]
    for j in range(NF):
        if j >= 4:
            values.append(
                tuple(factor * values[j - 2][i] - values[j - 4][i] for i in range(2))
            )
        group, inner = divmod(j, LANES // P_SIZE)
        for i in range(2):
            first = group * 2 * LANES + i * LANES + inner * P_SIZE
            u_ref[pl.ds(first, P_SIZE), :] = values[j][i].astype(bf16)


def migrate_kernel(
    core_ref, foot_ref, arrived_ref, lateral_ref, times_ref, amps_ref, spread_ref, cos_ref, sin_ref,
    keep_ref, give_ref, u_ref, v_ref, *, scale,
):
    core = core_ref[0]
    beam_re, beam_im = slant_stack(
        arrived_ref[...], spread_ref[...], cos_ref[...], sin_ref[...], scale
    )
    xs = iota((XW, LANES), 0)
    columns = xs.astype(f32)
    first_freq = (iota((XW, LANES), 1) // P_SIZE + KLO).astype(f32) * (omega_step / width_scale)
    group_freq = (LANES // P_SIZE) * omega_step / width_scale
    outputs, depth = keep_ref.shape[0], keep_ref.shape[2]

    def contribution(w):
        fill_u(u_ref, times_ref[w], amps_ref[w])
        away = columns - lateral_ref[pl.ds(w, 1), :]
        minus = -(away * away)
        inside = (xs >= foot_ref[w, 0]) & (xs < foot_ref[w, 1])
        gauss = jnp.where(inside, jnp.exp(minus * first_freq), 0.0) * (
            1.0 / math.sqrt(P_SIZE * NF)
        )
        ratio = jnp.exp(minus * group_freq)
        for group in range(NF * P_SIZE // LANES):
            lanes = slice(group * LANES, (group + 1) * LANES)
            v_ref[:, 2 * group * LANES : (2 * group + 1) * LANES] = (
                gauss * beam_re[:, lanes]
            ).astype(bf16)
            v_ref[:, (2 * group + 1) * LANES : (2 * group + 2) * LANES] = (
                gauss * beam_im[:, lanes]
            ).astype(bf16)
            gauss = gauss * ratio
        return dot(v_ref[...], u_ref[...]).T

    def give_step(q, carry):
        w = jnp.where(core == 0, KEEP + q, HALF - 1 - q)
        result = contribution(w).astype(bf16)
        for o in range(outputs):
            give_ref[o, q] = result[o * depth : (o + 1) * depth]
        return carry

    def keep_step(q, carry):
        w = jnp.where(core == 0, HALF - q, HALF + q)
        result = contribution(w)
        for o in range(outputs):
            keep_ref[o, q] = result[o * depth : (o + 1) * depth]
        return carry

    lax.fori_loop(0, HALF, give_step, 0)
    lax.fori_loop(0, KEEP, keep_step, 0)


def merge_kernel(keep_ref, taken_ref, out_ref):
    out_ref[:, :HALF] = (keep_ref[:, :HALF] + taken_ref[...].astype(f32)).astype(bf16)
    out_ref[:, HALF:] = keep_ref[:, HALF:].astype(bf16)


def total_kernel(parts_ref, *out_refs):
    for q, out_ref in enumerate(out_refs):
        total = parts_ref[0, q].astype(f32)
        for o in range(1, parts_ref.shape[0]):
            total = total + parts_ref[o, q].astype(f32)
        out_ref[...] = total


def vmem():
    return pl.BlockSpec(memory_space=pltpu.VMEM)


def smem():
    return pl.BlockSpec(memory_space=pltpu.SMEM)


def shards(traces, centre_ids, midpoint_bins, ray_times, ray_amps, beam_lateral, footprint):
    my_slab = lax.axis_index("slab")
    slabs = lax.axis_size("slab")
    offsets = lax.axis_size("offset")
    count = traces.shape[1]
    depth = ray_times.shape[4]
    part = depth // offsets
    high, low = dft_tables()
    routed = pl.pallas_call(
        route_kernel,
        out_shape=jax.ShapeDtypeStruct((slabs * ROWS, LANES), bf16),
        in_specs=[vmem()] * 5,
        out_specs=vmem(),
    )(centre_ids[0], midpoint_bins, traces[0], jnp.asarray(high), jnp.asarray(low))
    arrived = lax.all_to_all(
        routed.reshape(slabs, ROWS, LANES), "slab", split_axis=0, concat_axis=0, tiled=True
    ).reshape(slabs * ROWS, LANES)

    lateral = lax.dynamic_index_in_dim(beam_lateral[0], my_slab, 0, keepdims=False)
    lateral = jnp.tile(lateral, (1, LANES // P_SIZE))
    foot = lax.dynamic_index_in_dim(footprint, my_slab, 0, keepdims=False)
    core = (my_slab % 2).astype(jnp.int32).reshape(1)
    cosine, sine, spread = slant_tables()
    keep, give = pl.pallas_call(
        lambda *refs: migrate_kernel(*refs, scale=1.0 / math.sqrt(NT * count)),
        out_shape=(
            jax.ShapeDtypeStruct((offsets, KEEP, part, XW), f32),
            jax.ShapeDtypeStruct((offsets, HALF, part, XW), bf16),
        ),
        in_specs=[smem(), smem()] + [vmem()] * 7,
        out_specs=(vmem(), vmem()),
        scratch_shapes=[
            pltpu.VMEM((2 * P_SIZE * NF, depth), bf16),
            pltpu.VMEM((XW, 2 * P_SIZE * NF), bf16),
        ],
        compiler_params=pltpu.CompilerParams(vmem_limit_bytes=32 * 1024 * 1024),
    )(
        core, foot, arrived, lateral, ray_times[0, 0], ray_amps[0, 0],
        jnp.asarray(spread), jnp.asarray(cosine), jnp.asarray(sine),
    )
    swap = [(i, i ^ 1) for i in range(slabs)]
    taken = lax.ppermute(give, "slab", swap)
    merged = pl.pallas_call(
        merge_kernel,
        out_shape=jax.ShapeDtypeStruct((offsets, KEEP, part, XW), bf16),
        in_specs=[vmem()] * 2,
        out_specs=vmem(),
    )(keep, taken)
    parts = lax.all_to_all(merged, "offset", split_axis=0, concat_axis=0, tiled=True)
    totals = pl.pallas_call(
        total_kernel,
        out_shape=tuple(jax.ShapeDtypeStruct((part, XW), f32) for _ in range(KEEP)),
        in_specs=[vmem()],
        out_specs=tuple(vmem() for _ in range(KEEP)),
    )(parts)
    image = totals[0]
    for step in range(1, KEEP):
        pairs = [(i, i - step if i % 2 == 0 else i + step) for i in range(slabs)]
        pairs = [(i, j) for i, j in pairs if 0 <= j < slabs]
        image = image + lax.ppermute(totals[step], "slab", pairs)
    return image


def solution(mesh):
    return jax.shard_map(
        shards,
        mesh=mesh,
        in_specs=(
            P("offset", "slab", None),
            P("offset", "slab", None),
            P("offset", "slab"),
            P("offset", "slab", None, None, None),
            P("offset", "slab", None, None, None),
            P("offset", None, None, None),
            P(),
        ),
        out_specs=P("offset", "slab"),
        check_vma=False,
    )
```

time: 181 us -> 83.2 us (0.46)
  the two profiles are of different devices: /device:TPU:32 before, /device:TPU:24 now
where the time goes in v1:
time: 83.2 us; the launch traced here: 82.6 us
  starting transfers between devices  33.1 us (40%)
  waiting for transfers between devices  20.5 us (25%)
  blocking collectives  12 us (14%)
  Pallas kernels  11.5 us (14%)
  local copies, waits for them, and re-layouts  4.12 us (5%)
  other arithmetic  1.33 us (2%)
    all_to_all x1, starting transfers between devices, shards(): lax.all_to_all(routed.reshape(slabs, ROWS, LANES), 'slab', split_axis=0,...  18.8 us
    all_to_all x1, waiting for transfers between devices, shards(): lax.all_to_all(routed.reshape(slabs, ROWS, LANES), 'slab', split_axis=0,...  14.4 us
    ppermute x3, starting transfers between devices, shards(): image = image + lax.ppermute(totals[step], 'slab', pairs)  12.3 us
    all_to_all x1, blocking collectives, shards(): lax.all_to_all(merged, 'offset', split_axis=0, concat_axis=0, tiled=True)  12 us
    pallas_call x1, Pallas kernels, shards(): pl.pallas_call(lambda *refs: migrate_kernel(*refs, scale=1.0 / math.sqrt(...  6.07 us
    ppermute x3, waiting for transfers between devices, shards(): image = image + lax.ppermute(totals[step], 'slab', pairs)  4.71 us
    unnamed x21, local copies, waits for them, and re-layouts  2.94 us
    pallas_call x1, Pallas kernels, shards(): pl.pallas_call(route_kernel, out_shape=jax.ShapeDtypeStruct((slabs * ROWS...  2.05 us
  transfers between devices with their start and end apart: 5, of which 3 were waited for; matrix products, arithmetic and copies ran while one was open for 1% of the time, Pallas kernels for 0%

profile of v1, /device:TPU:24, one launch (start us, length us, event | category | flops | bytes accessed | tf_op | source)
XLA Modules:
  0.0 82.6 jit_solution(6305134207558173789)
XLA Ops:
  0.0 0.0 copy-start
  0.0 0.7 copy-done.9
  0.7 0.7 copy.14.ids_ref
  1.4 2.0 %shard_map.118 = bf16[512,128]{1,0:T(8,128)(2,1)} custom-call(s32[128,1]{1,0:T(8,128)} %copy.14.ids_ref, s32[1,128]{1,0:T(1,128)} %bins_ref.1, bf16[128,256]{1,0:T(8,128)(2,1)} %bitcast.13, bf16[256,128]{1,0:T(8,128)(2,1)} %constant.37.clone.high_ref, bf16[256,128]{1,0:T(8,128)(2,1)} %constant.38.clone.low_ref), custom_call_target="tpu_custom_call" | custom-call | tf_op jit(solution)/shard_map/pallas_call | solution.py:242
  3.4 18.8 %all-to-all-start = ((bf16[64,8,128]{2,1,0:T(8,128)(2,1)}), bf16[64,8,128]{2,1,0:T(8,128)(2,1)S(1)}, u32[]{:S(2)}, u32[]{:S(2)}) async-start(bf16[64,8,128]{2,1,0:T(8,128)(2,1)} %bitcast.12), calls=%async_computation | async-start | bytes 262144 | tf_op jit(solution)/shard_map/all_to_all | solution.py:248
  22.3 0.0 copy-start.8
  22.3 0.0 copy-start.5
  22.3 0.7 copy-done.8
  23.0 0.1 constant_dynamic-slice_fusion.1
  23.1 0.1 copy.13
  23.2 0.1 copy.16.refs_1_
  23.3 0.1 constant_dynamic-slice_fusion
  23.4 0.1 copy.17
  23.5 0.1 tile.13.refs_3_
  23.6 14.4 %all-to-all-done = bf16[64,8,128]{2,1,0:T(8,128)(2,1)S(1)} async-done(((bf16[64,8,128]{2,1,0:T(8,128)(2,1)}), bf16[64,8,128]{2,1,0:T(8,128)(2,1)S(1)}, u32[]{:S(2)}, u32[]{:S(2)}) %all-to-all-start) | async-done | bytes 131104 | tf_op jit(solution)/shard_map/all_to_all | solution.py:248
  38.0 0.0 copy-done.6
  38.0 0.0 copy-done.5
  38.0 6.1 %shard_map.119 = (f32[8,4,32,128]{3,2,1,0:T(8,128)S(1)}, bf16[8,3,32,128]{3,2,1,0:T(8,128)(2,1)S(1)}) custom-call(s32[1]{0:T(128)} %bitcast.refs_0_, s32[7,2]{1,0:T(8,128)S(1)} %copy.16.refs_1_, bf16[512,128]{1,0:T(8,128)(2,1)S(1)} %bitcast.9, f32[7,128]{1,0:T(8,128)S(1)} %tile.13.refs_3_, f32[7,16,256]{2,1,0:T(8,128)S(1)} %bitcast.10, ...), custom_call_target="tpu_custom_call" | custom-call | tf_op jit(solution)/shard_map/pallas_call | solution.py:257
  44.1 0.8 copy-done.1
  44.9 2.0 %collective-permute-start = (bf16[8,3,32,128]{3,2,1,0:T(8,128)(2,1)S(1)}, bf16[8,3,32,128]{3,2,1,0:T(8,128)(2,1)S(1)}, u32[]{:S(2)}, u32[]{:S(2)}) collective-permute-start(bf16[8,3,32,128]{3,2,1,0:T(8,128)(2,1)S(1)} %get-tuple-element.12), channel_id=1, source_target_pairs={{0,1},{1,0},{2,3},{3,2},{4,5},{5,4},{6,7},{7,6},{8,9},{9,8},{10,11... | collective-permute-start | bytes 589832 | tf_op jit(solution)/shard_map/ppermute | solution.py:275
  46.9 1.3 %collective-permute-done.taken_ref = bf16[8,3,32,128]{3,2,1,0:T(8,128)(2,1)S(1)} collective-permute-done((bf16[8,3,32,128]{3,2,1,0:T(8,128)(2,1)S(1)}, bf16[8,3,32,128]{3,2,1,0:T(8,128)(2,1)S(1)}, u32[]{:S(2)}, u32[]{:S(2)}) %collective-permute-start) | collective-permute-done | bytes 196640 | tf_op jit(solution)/shard_map/ppermute | solution.py:275
  48.2 0.7 copy-done.7
  48.9 1.8 %shard_map.120 = bf16[8,4,32,128]{3,2,1,0:T(8,128)(2,1)} custom-call(f32[8,4,32,128]{3,2,1,0:T(8,128)} %copy-done.1, bf16[8,3,32,128]{3,2,1,0:T(8,128)(2,1)} %copy-done.7), custom_call_target="tpu_custom_call" | custom-call | tf_op jit(solution)/shard_map/pallas_call | solution.py:276
  50.8 12.0 %all_to_all.10.parts_ref = bf16[8,4,32,128]{3,2,1,0:T(8,128)(2,1)} all-to-all(bf16[8,4,32,128]{3,2,1,0:T(8,128)(2,1)} %shard_map.120), channel_id=1, replica_groups=mesh['offset'=8,'slab'=64] {'offset'}, dimensions={0} | all-to-all | bytes 524288 | tf_op jit(solution)/shard_map/all_to_all | solution.py:282
  62.7 1.6 %shard_map.121 = (f32[32,128]{1,0:T(8,128)}, f32[32,128]{1,0:T(8,128)}, f32[32,128]{1,0:T(8,128)}, f32[32,128]{1,0:T(8,128)}) custom-call(bf16[8,4,32,128]{3,2,1,0:T(8,128)(2,1)} %all_to_all.10.parts_ref), custom_call_target="tpu_custom_call" | custom-call | tf_op jit(solution)/shard_map/pallas_call | solution.py:283
  64.3 1.9 %collective-permute-start.1 = (f32[32,128]{1,0:T(8,128)}, f32[32,128]{1,0:T(8,128)S(1)}, u32[]{:S(2)}, u32[]{:S(2)}) collective-permute-start(f32[32,128]{1,0:T(8,128)} %get-tuple-element.14), channel_id=1, source_target_pairs={{1,2},{2,1},{3,4},{4,3},{5,6},{6,5},{7,8},{8,7},{9,10},{10,9},{11,... | collective-permute-start | bytes 49160 | tf_op jit(solution)/shard_map/ppermute | solution.py:293
  66.2 5.3 %collective-permute-start.2 = (f32[32,128]{1,0:T(8,128)}, f32[32,128]{1,0:T(8,128)S(1)}, u32[]{:S(2)}, u32[]{:S(2)}) collective-permute-start(f32[32,128]{1,0:T(8,128)} %get-tuple-element.15), channel_id=1, source_target_pairs={{1,3},{2,0},{3,5},{4,2},{5,7},{6,4},{7,9},{8,6},{9,11},{10,8},{11,... | collective-permute-start | bytes 49160 | tf_op jit(solution)/shard_map/ppermute | solution.py:293
  71.5 5.1 %collective-permute-start.3 = (f32[32,128]{1,0:T(8,128)}, f32[32,128]{1,0:T(8,128)S(1)}, u32[]{:S(2)}, u32[]{:S(2)}) collective-permute-start(f32[32,128]{1,0:T(8,128)} %get-tuple-element.16), channel_id=1, source_target_pairs={{1,4},{3,6},{4,1},{5,8},{6,3},{7,10},{8,5},{9,12},{10,7},{11,14},{... | collective-permute-start | bytes 49160 | tf_op jit(solution)/shard_map/ppermute | solution.py:293
  76.6 0.0 collective-permute-done.1
  76.6 0.0 collective-permute-done.2
  76.6 4.7 %collective-permute-done.3 = f32[32,128]{1,0:T(8,128)S(1)} collective-permute-done((f32[32,128]{1,0:T(8,128)}, f32[32,128]{1,0:T(8,128)S(1)}, u32[]{:S(2)}, u32[]{:S(2)}) %collective-permute-start.3) | collective-permute-done | bytes 16416 | tf_op jit(solution)/shard_map/ppermute | solution.py:293
  81.3 1.3 %add_add_fusion = f32[32,128]{1,0:T(8,128)} fusion(f32[32,128]{1,0:T(8,128)S(1)} %collective-permute-done.3, f32[32,128]{1,0:T(8,128)S(1)} %collective-permute-done.2, f32[32,128]{1,0:T(8,128)} %get-tuple-element.13, f32[32,128]{1,0:T(8,128)S(1)} %collective-permute-done.1), kind=kLoop, calls=%fused_computation | loop fusion | flops 12288 | bytes 81920 | tf_op jit(solution)/shard_map/add | solution.py:293
  (12 shorter events, 0.0 us)
Async XLA Ops:
  0.0 23.3 %copy-start = (f32[1,64,7,16]{1,3,2,0:T(8,128)S(1)}, f32[1,64,7,16]{1,3,2,0:T(8,128)}, u32[]{:S(2)}) copy-start(f32[1,64,7,16]{1,3,2,0:T(8,128)} %param.17) | copy-start | bytes 86020
  0.0 0.7 copy-start.9
  1.4 36.6 %copy-start.6 = (f32[16,1024]{1,0:T(8,128)S(1)}, f32[16,1024]{1,0:T(8,128)}, u32[]{:S(2)}) copy-start(f32[16,1024]{1,0:T(8,128)} %constant.40.clone.refs_7_) | copy-start | bytes 196612
  3.4 34.6 %copy-start.2 = (bf16[128,1024]{1,0:T(8,128)(2,1)S(1)}, bf16[128,1024]{1,0:T(8,128)(2,1)}, u32[]{:S(2)}) copy-start(bf16[128,1024]{1,0:T(8,128)(2,1)} %constant.39.clone.refs_6_) | copy-start | bytes 786436
  3.4 34.6 %all-to-all-start = ((bf16[64,8,128]{2,1,0:T(8,128)(2,1)}), bf16[64,8,128]{2,1,0:T(8,128)(2,1)S(1)}, u32[]{:S(2)}, u32[]{:S(2)}) async-start(bf16[64,8,128]{2,1,0:T(8,128)(2,1)} %bitcast.12), calls=%async_computation | async-start | bytes 262144 | tf_op jit(solution)/shard_map/all_to_all | solution.py:248
  22.3 0.7 copy-start.8
  22.3 15.7 %copy-start.5 = (f32[16,1024]{1,0:T(8,128)S(1)}, f32[16,1024]{1,0:T(8,128)}, u32[]{:S(2)}) copy-start(f32[16,1024]{1,0:T(8,128)} %constant.41.clone.refs_8_) | copy-start | bytes 196612
  23.3 14.8 %copy-start.3 = (f32[1,1,7,16,256]{4,3,2,1,0:T(8,128)S(1)}, f32[1,1,7,16,256]{4,3,2,1,0:T(8,128)}, u32[]{:S(2)}) copy-start(f32[1,1,7,16,256]{4,3,2,1,0:T(8,128)} %param.15) | copy-start | bytes 344068
  23.3 14.8 %copy-start.4 = (f32[1,1,7,16,256]{4,3,2,1,0:T(8,128)S(1)}, f32[1,1,7,16,256]{4,3,2,1,0:T(8,128)}, u32[]{:S(2)}) copy-start(f32[1,1,7,16,256]{4,3,2,1,0:T(8,128)} %param.16) | copy-start | bytes 344068
  44.1 0.8 copy-start.1
  44.9 3.3 %collective-permute-start = (bf16[8,3,32,128]{3,2,1,0:T(8,128)(2,1)S(1)}, bf16[8,3,32,128]{3,2,1,0:T(8,128)(2,1)S(1)}, u32[]{:S(2)}, u32[]{:S(2)}) collective-permute-start(bf16[8,3,32,128]{3,2,1,0:T(8,128)(2,1)S(1)} %get-tuple-element.12), channel_id=1, source_target_pairs={{0,1},{1,0},{2,3},{3,2},{4,5},{5,4},{6,7},{7,6},{8,9},{9,8},{10,11... | collective-permute-start | bytes 589832 | tf_op jit(solution)/shard_map/ppermute | solution.py:275
  48.2 0.7 copy-start.7
  64.3 12.3 %collective-permute-start.1 = (f32[32,128]{1,0:T(8,128)}, f32[32,128]{1,0:T(8,128)S(1)}, u32[]{:S(2)}, u32[]{:S(2)}) collective-permute-start(f32[32,128]{1,0:T(8,128)} %get-tuple-element.14), channel_id=1, source_target_pairs={{1,2},{2,1},{3,4},{4,3},{5,6},{6,5},{7,8},{8,7},{9,10},{10,9},{11,... | collective-permute-start | bytes 49160 | tf_op jit(solution)/shard_map/ppermute | solution.py:293
  66.2 10.4 %collective-permute-start.2 = (f32[32,128]{1,0:T(8,128)}, f32[32,128]{1,0:T(8,128)S(1)}, u32[]{:S(2)}, u32[]{:S(2)}) collective-permute-start(f32[32,128]{1,0:T(8,128)} %get-tuple-element.15), channel_id=1, source_target_pairs={{1,3},{2,0},{3,5},{4,2},{5,7},{6,4},{7,9},{8,6},{9,11},{10,8},{11,... | collective-permute-start | bytes 49160 | tf_op jit(solution)/shard_map/ppermute | solution.py:293
  71.5 9.8 %collective-permute-start.3 = (f32[32,128]{1,0:T(8,128)}, f32[32,128]{1,0:T(8,128)S(1)}, u32[]{:S(2)}, u32[]{:S(2)}) collective-permute-start(f32[32,128]{1,0:T(8,128)} %get-tuple-element.16), channel_id=1, source_target_pairs={{1,4},{3,6},{4,1},{5,8},{6,3},{7,10},{8,5},{9,12},{10,7},{11,14},{... | collective-permute-start | bytes 49160 | tf_op jit(solution)/shard_map/ppermute | solution.py:293

commit v2 on v1

v2 whole, which is shorter than its diff:
```python
import math

import jax
import jax.numpy as jnp
import numpy as np
from jax import lax
from jax.experimental import pallas as pl
from jax.experimental.pallas import tpu as pltpu
from jax.sharding import Mesh
from jax.sharding import PartitionSpec as P

NT = 256
NF = 64
KLO = 8
P_SIZE = 16
BINS = 16
CAP = 6
WIN = 7
XW = 128
ROWS = 8
LANES = 128
HALF = (WIN - 1) // 2
GROUPS = P_SIZE * NF // LANES

two_pi = 2.0 * math.pi
slow_step = 0.25
width_scale = 200.0
omega_step = two_pi / NT

f32 = jnp.float32
bf16 = jnp.bfloat16


def dft_tables():
    sample = np.arange(NT)[:, None]
    turns = (sample * (np.arange(NF)[None, :] + KLO) % NT) * (two_pi / NT)
    table = np.concatenate([np.cos(turns), -np.sin(turns)], axis=1).astype(np.float32)
    high = table.astype(bf16)
    low = (table - high.astype(np.float32)).astype(bf16)
    return high, low


def slant_tables():
    freq = (np.arange(NF) + KLO) * omega_step
    slow = (np.arange(P_SIZE) - (P_SIZE - 1) / 2.0) * slow_step
    place = np.arange(BINS) - (BINS - 1) / 2.0
    phase = place[:, None, None] * freq[None, :, None] * slow[None, None, :]
    phase = phase.reshape(BINS, NF * P_SIZE)
    spread = np.arange(2 * NF)[:, None] % NF == np.arange(NF * P_SIZE)[None, :] // P_SIZE
    return (
        np.cos(phase).astype(np.float32),
        np.sin(phase).astype(np.float32),
        spread.astype(np.float32).astype(bf16),
    )


def iota(shape, dim):
    return lax.broadcasted_iota(jnp.int32, shape, dim)


def dot(a, b):
    return jnp.dot(a, b, preferred_element_type=f32)


def route_kernel(ids_ref, bins_ref, traces_ref, high_ref, low_ref, out_ref):
    count = traces_ref.shape[0]
    square = (count, count)
    row, col = iota(square, 0), iota(square, 1)
    ids_across = ids_ref[...]
    ids_down = jnp.sum(
        jnp.where(row == col, ids_across.astype(f32), 0.0), axis=1, keepdims=True
    )
    same = ids_down == ids_across.astype(f32)
    rank_across = jnp.sum(jnp.where(same & (row < col), 1.0, 0.0), axis=0, keepdims=True)
    rank_down = jnp.sum(jnp.where(same & (col < row), 1.0, 0.0), axis=1, keepdims=True)
    place_across = bins_ref[...].astype(f32) - (BINS - 1) / 2.0
    place_down = jnp.sum(jnp.where(row == col, place_across, 0.0), axis=1, keepdims=True)
    traces = traces_ref[...]
    spectrum = dot(traces, high_ref[...]) + dot(traces, low_ref[...])
    places = jnp.where(col == rank_down.astype(jnp.int32), place_down, 0.0)
    values = jnp.concatenate([spectrum, places], axis=1).astype(bf16)
    out_rows = out_ref.shape[0]
    slot = iota((out_rows, count), 0)
    place_row = slot % ROWS == CAP
    target = ids_across * ROWS + rank_across.astype(jnp.int32)
    pick = (slot == target) | (place_row & (slot // ROWS == ids_across))
    picked = dot(jnp.where(pick, 1.0, 0.0).astype(bf16), values)
    out_ref[...] = jnp.where(place_row, picked[:, LANES:], picked[:, :LANES]).astype(bf16)


def slant_stack(arrived, spread, cosine, sine, scale):
    rows = arrived.shape[0]
    full = arrived.astype(f32).reshape(rows // ROWS, ROWS, LANES)
    sub, lane = iota((rows // ROWS, ROWS, LANES), 1), iota((rows // ROWS, ROWS, LANES), 2)
    own = jnp.where(sub == lane, jnp.broadcast_to(full[:, CAP : CAP + 1, :], full.shape), 0.0)
    own = own.reshape(rows, LANES).astype(bf16)
    place = dot(own, jnp.ones((LANES, LANES), bf16))
    bin_place = iota((rows, LANES), 1).astype(f32) - (BINS - 1) / 2.0
    in_bin = jnp.where((place == bin_place) & (place != 0.0), 1.0, 0.0).astype(bf16)
    binned = lax.dot_general(
        in_bin, arrived, (((0,), (0,)), ((), ())), preferred_element_type=f32
    )[:BINS]
    real = iota((BINS, LANES), 1) < NF
    binned_re = jnp.where(real, binned, 0.0)
    binned_im = jnp.where(real, 0.0, binned)
    parts = []
    for part in (binned_re, binned_im):
        high = part.astype(bf16)
        parts += [high, (part - high.astype(f32)).astype(bf16)]
    wide = dot(jnp.concatenate(parts, axis=0), spread)
    wide_re = wide[:BINS] + wide[BINS : 2 * BINS]
    wide_im = wide[2 * BINS : 3 * BINS] + wide[3 * BINS :]
    beam_re = jnp.sum(wide_re * cosine + wide_im * sine, axis=0, keepdims=True)
    beam_im = jnp.sum(wide_im * cosine - wide_re * sine, axis=0, keepdims=True)
    return (
        (beam_re * scale).astype(bf16).astype(f32),
        (beam_im * scale).astype(bf16).astype(f32),
    )


def cos_sin_turns(turns):
    half = (turns - 0.5) * math.pi
    sq = half * half
    sin_of = 1.0 / 6227020800.0
    for divisor in (-39916800.0, 362880.0, -5040.0, 120.0, -6.0, 1.0):
        sin_of = sin_of * sq + 1.0 / divisor
    sin_of = sin_of * half
    cos_of = 1.0 / 479001600.0
    for divisor in (-3628800.0, 40320.0, -720.0, 24.0, -2.0, 1.0):
        cos_of = cos_of * sq + 1.0 / divisor
    return 2.0 * sin_of * sin_of - 1.0, -2.0 * sin_of * cos_of


def u_groups(u_ref, times, amps):
    def times_of(a, b):
        return a[0] * b[0] - a[1] * b[1], a[0] * b[1] + a[1] * b[0]

    one = cos_sin_turns(times * (1.0 / NT))
    two = times_of(one, one)
    four = times_of(two, two)
    eight = times_of(four, four)
    start = (amps * eight[0], amps * eight[1])
    walk = [start, times_of(start, one), times_of(start, two)]
    walk.append(times_of(walk[1], two))
    values = [(c, -s) for c, s in walk]
    factor = 2.0 * two[0]
    for j in range(NF):
        if j >= 4:
            values.append(
                tuple(factor * values[j - 2][i] - values[j - 4][i] for i in range(2))
            )
        group, inner = divmod(j, LANES // P_SIZE)
        for i in range(2):
            first = group * 2 * LANES + i * LANES + inner * P_SIZE
            u_ref[pl.ds(first, P_SIZE), :] = values[j][i].astype(bf16)
        if inner == LANES // P_SIZE - 1:
            yield


def v_groups(w, beam_re, beam_im, foot_ref, lateral_ref):
    xs = iota((XW, LANES), 0)
    freq = (iota((XW, LANES), 1) // P_SIZE + KLO).astype(f32) * (omega_step / width_scale)
    away = xs.astype(f32) - lateral_ref[pl.ds(w, 1), :]
    minus = -(away * away)
    inside = (xs >= foot_ref[w, 0]) & (xs < foot_ref[w, 1])
    gauss = jnp.where(inside, jnp.exp(minus * freq), 0.0) * (1.0 / math.sqrt(P_SIZE * NF))
    ratio = jnp.exp(minus * ((LANES // P_SIZE) * omega_step / width_scale))
    for group in range(GROUPS):
        lanes = slice(group * LANES, (group + 1) * LANES)
        yield jnp.concatenate(
            [(gauss * beam_re[:, lanes]).astype(bf16), (gauss * beam_im[:, lanes]).astype(bf16)],
            axis=1,
        )
        gauss = gauss * ratio


def contributions(windows, beams_of, foot_ref, lateral_ref, times_ref, amps_ref, u_ref, store):
    def u_of(i):
        return u_groups(u_ref.at[i], times_ref[windows[i]], amps_ref[windows[i]])

    for _ in u_of(0):
        pass
    beam_re, beam_im = beams_of()
    for i, w in enumerate(windows):
        following = u_of(i + 1) if i + 1 < len(windows) else iter(())
        total = None
        for group, v in enumerate(v_groups(w, beam_re, beam_im, foot_ref, lateral_ref)):
            part = dot(v, u_ref[i, pl.ds(group * 2 * LANES, 2 * LANES), :])
            total = part if total is None else total + part
            next(following, None)
        store(i, total.T)


def far_kernel(
    place_ref, foot_ref, arrived_ref, lateral_ref, times_ref, amps_ref, spread_ref, cos_ref,
    sin_ref, seam_ref, pair_ref, outer_ref, beam_ref, u_ref, *, scale,
):
    core, odd = place_ref[0], place_ref[1]

    def beams_of():
        beams = slant_stack(
            arrived_ref[...], spread_ref[...], cos_ref[...], sin_ref[...], scale
        )
        for i in range(2):
            beam_ref[i : i + 1] = beams[i]
        return beams

    def store(i, block):
        block = block.astype(bf16)
        if i < 3:
            seam_ref[i] = block
        else:
            pair_ref[i - 3] = block
        if i == 2:
            outer_ref[...] = block

    left, right = 1 - core, 5 - core
    to_seam, to_pair = jnp.where(odd == 0, left, right), jnp.where(odd == 0, right, left)
    windows = [to_seam, to_seam + 1, core * (WIN - 1), to_pair, to_pair + 1]
    contributions(windows, beams_of, foot_ref, lateral_ref, times_ref, amps_ref, u_ref, store)


def near_kernel(
    place_ref, foot_ref, beam_ref, lateral_ref, times_ref, amps_ref, near_ref, u_ref
):
    def store(i, block):
        near_ref[i] = block

    first = HALF - place_ref[0]
    contributions(
        [first, first + 1], lambda: (beam_ref[0:1], beam_ref[1:2]),
        foot_ref, lateral_ref, times_ref, amps_ref, u_ref, store,
    )


def merge_kernel(place_ref, near_ref, seam_ref, pair_ref, outer_ref, last_ref, out_ref):
    core = place_ref[0]
    cores, rows = 2, out_ref.shape[1]
    outer = outer_ref[...].astype(f32) + last_ref[...].astype(f32)
    for i in range(cores):
        total = near_ref[i] + seam_ref[i].astype(f32) + pair_ref[i].astype(f32)
        total = (total + jnp.where(core == i, outer, 0.0)).astype(bf16)
        for o in range(out_ref.shape[0] // cores):
            out_ref[o * cores + i] = total[o * rows : (o + 1) * rows]


def total_kernel(parts_ref, out_ref):
    total = parts_ref[0].astype(f32)
    for i in range(1, parts_ref.shape[0]):
        total = total + parts_ref[i].astype(f32)
    out_ref[...] = total


def vmem():
    return pl.BlockSpec(memory_space=pltpu.VMEM)


def smem():
    return pl.BlockSpec(memory_space=pltpu.SMEM)


def call(kernel, out_shape, in_specs, mib=None, scratch=(), flops=0):
    many = isinstance(out_shape, tuple)
    limit = None if mib is None else mib * 1024 * 1024
    return pl.pallas_call(
        kernel,
        out_shape=out_shape,
        in_specs=in_specs,
        out_specs=tuple(vmem() for _ in out_shape) if many else vmem(),
        scratch_shapes=scratch,
        compiler_params=pltpu.CompilerParams(vmem_limit_bytes=limit),
        cost_estimate=pl.CostEstimate(flops=flops, bytes_accessed=1 << 20, transcendentals=0),
    )


def struct(*shape):
    return jax.ShapeDtypeStruct(shape, bf16)


def struct32(*shape):
    return jax.ShapeDtypeStruct(shape, f32)


def shards(traces, centre_ids, midpoint_bins, ray_times, ray_amps, beam_lateral, footprint):
    slab_axes = ("chip", "core")
    my_slab = lax.axis_index(slab_axes)
    slabs = lax.axis_size(slab_axes)
    offsets = lax.axis_size("offset")
    count = traces.shape[1]
    depth = ray_times.shape[4]
    part = depth // offsets
    high, low = dft_tables()
    routed = call(route_kernel, struct(slabs * ROWS, LANES), [vmem()] * 5)(
        centre_ids.reshape(1, count), midpoint_bins, traces[0], jnp.asarray(high), jnp.asarray(low)
    )
    arrived = lax.all_to_all(
        routed.reshape(slabs, ROWS, LANES), slab_axes, split_axis=0, concat_axis=0, tiled=True
    ).reshape(slabs * ROWS, LANES)

    lateral = lax.dynamic_index_in_dim(beam_lateral[0], my_slab, 0, keepdims=False)
    lateral = jnp.tile(lateral, (1, LANES // P_SIZE))
    foot = lax.dynamic_index_in_dim(footprint, my_slab, 0, keepdims=False)
    u_rows = 2 * P_SIZE * NF
    place = jnp.stack([my_slab % 2, my_slab // 2 % 2]).astype(jnp.int32)
    cosine, sine, spread = slant_tables()
    to_seam, to_pair, to_outer, beams = call(
        lambda *refs: far_kernel(*refs, scale=1.0 / math.sqrt(NT * count)),
        (struct(3, depth, XW), struct(2, depth, XW), struct(depth, XW), struct32(2, NF * P_SIZE)),
        [smem()] * 2 + [vmem()] * 7,
        24,
        [pltpu.VMEM((WIN - 2, u_rows, depth), bf16)],
    )(
        place, foot, arrived, lateral, ray_times[0, 0], ray_amps[0, 0],
        jnp.asarray(spread), jnp.asarray(cosine), jnp.asarray(sine),
    )

    half = slabs // 2

    def chip_pairs(parity):
        pairs = [(i, i + 2 if i // 2 % 2 == parity else i - 2) for i in range(slabs)]
        return [(i, j) for i, j in pairs if 0 <= j < slabs]

    outward = [(i, i + 3 if i % 2 else i - 3) for i in range(slabs)]
    outward = [(i, j) for i, j in outward if 0 <= j < slabs and i not in (half - 1, half)]
    from_seam = lax.ppermute(to_seam, slab_axes, chip_pairs(1))
    from_pair = lax.ppermute(to_pair, slab_axes, chip_pairs(0))
    from_outer = lax.ppermute(to_outer, slab_axes, outward)
    near = call(
        near_kernel,
        struct32(2, depth, XW),
        [smem()] * 2 + [vmem()] * 4,
        24,
        [pltpu.VMEM((2, u_rows, depth), bf16)],
        flops=1 << 28,
    )(place, foot, beams, lateral, ray_times[0, 0], ray_amps[0, 0])
    last = lax.ppermute(from_seam[2], slab_axes, [(half - 2, half - 3), (half + 1, half + 2)])
    merged = call(merge_kernel, struct(2 * offsets, part, XW), [smem()] + [vmem()] * 5, 8)(
        place, near, from_seam, from_pair, from_outer, last
    )
    parts = lax.all_to_all(
        merged, ("offset", "core"), split_axis=0, concat_axis=0, tiled=True
    )
    return call(total_kernel, struct32(part, XW), [vmem()], 4)(parts)


def solution(mesh):
    offsets, slabs = mesh.devices.shape
    chips = Mesh(mesh.devices.reshape(offsets, slabs // 2, 2), ("offset", "chip", "core"))
    slab = ("chip", "core")
    return jax.shard_map(
        shards,
        mesh=chips,
        in_specs=(
            P("offset", slab, None),
            P("offset", slab, None),
            P("offset", slab),
            P("offset", slab, None, None, None),
            P("offset", slab, None, None, None),
            P("offset", None, None, None),
            P(),
        ),
        out_specs=P("offset", slab),
        check_vma=False,
    )
```

time: 83.2 us -> 69 us (0.83)
  the two profiles are of different devices: /device:TPU:24 before, /device:TPU:49 now
where the time goes in v2:
time: 69 us; the launch traced here: 68.6 us
  starting transfers between devices  28.3 us (41%)
  blocking collectives  16.9 us (24%)
  waiting for transfers between devices  14.5 us (21%)
  Pallas kernels  8.03 us (12%)
    all_to_all x1, starting transfers between devices, shards(): lax.all_to_all(routed.reshape(slabs, ROWS, LANES), slab_axes, split_axis=...  18.7 us
    all_to_all x1, blocking collectives, shards(): lax.all_to_all(merged, ('offset', 'core'), split_axis=0, concat_axis=0, t...  16.9 us
    all_to_all x1, waiting for transfers between devices, shards(): lax.all_to_all(routed.reshape(slabs, ROWS, LANES), slab_axes, split_axis=...  14.5 us
    ppermute x1, starting transfers between devices, shards(): from_pair = lax.ppermute(to_pair, slab_axes, chip_pairs(0))  3.76 us
    pallas_call x1, Pallas kernels, shards(): call(lambda *refs: far_kernel(*refs, scale=1.0 / math.sqrt(NT * count)),...  3.16 us
    ppermute x1, starting transfers between devices, shards(): from_outer = lax.ppermute(to_outer, slab_axes, outward)  2.98 us
    ppermute x1, starting transfers between devices, shards(): from_seam = lax.ppermute(to_seam, slab_axes, chip_pairs(1))  2.19 us
    pallas_call x1, Pallas kernels, shards(): call(route_kernel, struct(slabs * ROWS, LANES), [vmem()] * 5)  2 us
  transfers between devices with their start and end apart: 5, of which 1 were waited for; matrix products, arithmetic and copies ran while one was open for 1% of the time, Pallas kernels for 2%

profile of v2, /device:TPU:49, one launch (start us, length us, event | category | flops | bytes accessed | tf_op | source)
XLA Modules:
  0.0 68.6 jit_solution(7026316768564322646)
XLA Ops:
  0.0 0.0 copy-start
  0.0 2.0 %shard_map.118 = bf16[512,128]{1,0:T(8,128)(2,1)} custom-call(s32[1,128]{1,0:T(1,128)} %bitcast.21, s32[1,128]{1,0:T(1,128)} %bins_ref.1, bf16[128,256]{1,0:T(8,128)(2,1)} %bitcast.18, bf16[256,128]{1,0:T(8,128)(2,1)} %constant.56.clone.high_ref, bf16[256,128]{1,0:T(8,128)(2,1)} %constant.57.clone.low_ref), custom_call_target="tpu_custom_call" | custom-call | bytes 1048576 | tf_op jit(solution)/shard_map/pallas_call | solution.py:293
  2.0 18.7 %all-to-all-start = ((bf16[64,8,128]{2,1,0:T(8,128)(2,1)}), bf16[64,8,128]{2,1,0:T(8,128)(2,1)S(1)}, u32[]{:S(2)}, u32[]{:S(2)}) async-start(bf16[64,8,128]{2,1,0:T(8,128)(2,1)} %bitcast.17), calls=%async_computation | async-start | bytes 262144 | tf_op jit(solution)/shard_map/all_to_all | solution.py:296
  20.8 0.0 copy-start.4
  20.8 0.0 copy-done.6
  20.8 0.1 constant_dynamic-slice_fusion.1
  20.9 0.1 copy.13
  21.0 0.1 copy.16.refs_1_.foot_ref
  21.1 0.0 copy-done
  21.1 0.1 constant_dynamic-slice_fusion
  21.2 0.1 copy.17
  21.3 0.1 tile.13.refs_3_.lateral_ref
  21.4 0.1 pad_add_fusion.refs_0_.place_ref
  21.4 14.5 %all-to-all-done = bf16[64,8,128]{2,1,0:T(8,128)(2,1)S(1)} async-done(((bf16[64,8,128]{2,1,0:T(8,128)(2,1)}), bf16[64,8,128]{2,1,0:T(8,128)(2,1)S(1)}, u32[]{:S(2)}, u32[]{:S(2)}) %all-to-all-start) | async-done | bytes 131104 | tf_op jit(solution)/shard_map/all_to_all | solution.py:296
  35.9 0.0 copy-done.1
  35.9 0.0 copy-done.5
  36.0 0.0 copy-done.4
  36.0 0.0 copy-done.2
  36.0 0.0 copy-done.3
  36.0 3.2 %shard_map.119 = (bf16[3,256,128]{2,1,0:T(8,128)(2,1)S(1)}, bf16[2,256,128]{2,1,0:T(8,128)(2,1)S(1)}, bf16[256,128]{1,0:T(8,128)(2,1)S(1)}, f32[2,1024]{1,0:T(2,128)S(1)}) custom-call(s32[2]{0:T(128)S(1)} %pad_add_fusion.refs_0_.place_ref, s32[7,2]{1,0:T(8,128)S(1)} %copy.16.refs_1_.foot_ref, bf16[512,128]{1,0:T(8,128)(2,1)S(1)} %bitcast.12, ...), custom_call_target="tpu_custom_call" | custom-call | bytes 1048576 | tf_op jit(solution)/shard_map/pallas_call | solution.py:306
  39.1 2.2 %collective-permute-start = (bf16[3,256,128]{2,1,0:T(8,128)(2,1)S(1)}, bf16[3,256,128]{2,1,0:T(8,128)(2,1)S(1)}, u32[]{:S(2)}, u32[]{:S(2)}) collective-permute-start(bf16[3,256,128]{2,1,0:T(8,128)(2,1)S(1)} %get-tuple-element.10), channel_id=1, source_target_pairs={{2,4},{3,5},{4,2},{5,3},{6,8},{7,9},{8,6},{9,7},{10,12},{11,13},{1... | collective-permute-start | bytes 589832 | tf_op jit(solution)/shard_map/ppermute | solution.py:325
  41.3 3.0 %collective-permute-start.2 = (bf16[256,128]{1,0:T(8,128)(2,1)S(1)}, bf16[256,128]{1,0:T(8,128)(2,1)S(1)}, u32[]{:S(2)}, u32[]{:S(2)}) collective-permute-start(bf16[256,128]{1,0:T(8,128)(2,1)S(1)} %get-tuple-element.12), channel_id=1, source_target_pairs={{1,4},{3,6},{4,1},{5,8},{6,3},{7,10},{8,5},{9,12},{10,7},{11,14},{... | collective-permute-start | bytes 196616 | tf_op jit(solution)/shard_map/ppermute | solution.py:327
  44.3 3.8 %collective-permute-start.1 = (bf16[2,256,128]{2,1,0:T(8,128)(2,1)S(1)}, bf16[2,256,128]{2,1,0:T(8,128)(2,1)S(1)}, u32[]{:S(2)}, u32[]{:S(2)}) collective-permute-start(bf16[2,256,128]{2,1,0:T(8,128)(2,1)S(1)} %get-tuple-element.11), channel_id=1, source_target_pairs={{0,2},{1,3},{2,0},{3,1},{4,6},{5,7},{6,4},{7,5},{8,10},{9,11},{10,... | collective-permute-start | bytes 393224 | tf_op jit(solution)/shard_map/ppermute | solution.py:326
  48.1 0.0 collective-permute-done.seam_ref
  48.1 0.7 collective-permute-start.3
  48.8 1.6 %shard_map.120.near_ref = f32[2,256,128]{2,1,0:T(8,128)S(1)} custom-call(s32[2]{0:T(128)S(1)} %pad_add_fusion.refs_0_.place_ref, s32[7,2]{1,0:T(8,128)S(1)} %copy.16.refs_1_.foot_ref, f32[2,1024]{1,0:T(2,128)S(1)} %get-tuple-element.9.beam_ref, f32[7,128]{1,0:T(8,128)S(1)} %tile.13.refs_3_.lateral_ref, f32[7,16,256]{2,1,0:T(8,128)S(1)} %bitcast.14, ...), custom_call_target="tpu_custom_call" | custom-call | flops 268435456 | bytes 1048576 | tf_op jit(solution)/shard_map/pallas_call | solution.py:328
  50.4 0.0 collective-permute-done.2.outer_ref
  50.4 0.0 collective-permute-done.1.pair_ref
  50.4 0.0 collective-permute-done.3.last_ref
  50.5 0.6 shard_map.121
  51.1 16.9 %all_to_all.10.parts_ref = bf16[16,32,128]{2,1,0:T(8,128)(2,1)S(1)} all-to-all(bf16[16,32,128]{2,1,0:T(8,128)(2,1)S(1)} %shard_map.121), channel_id=1, replica_groups=mesh['offset'=8,'chip'=32,'core'=2] {'offset','core'}, dimensions={0} | all-to-all | bytes 262144 | tf_op jit(solution)/shard_map/all_to_all | solution.py:340
  68.0 0.6 shard_map.122
  (7 shorter events, 0.0 us)
Async XLA Ops:
  0.0 21.1 %copy-start = (f32[1,64,7,16]{1,3,2,0:T(8,128)S(1)}, f32[1,64,7,16]{1,3,2,0:T(8,128)}, u32[]{:S(2)}) copy-start(f32[1,64,7,16]{1,3,2,0:T(8,128)} %param.17) | copy-start | bytes 86020
  0.0 20.8 %copy-start.6 = (s32[64,7,2]{0,2,1:T(2,128)S(1)}, s32[64,7,2]{0,2,1:T(2,128)}, u32[]{:S(2)}) copy-start(s32[64,7,2]{0,2,1:T(2,128)} %param.18) | copy-start | bytes 10756
  2.0 33.9 %copy-start.1 = (bf16[128,1024]{1,0:T(8,128)(2,1)S(1)}, bf16[128,1024]{1,0:T(8,128)(2,1)}, u32[]{:S(2)}) copy-start(bf16[128,1024]{1,0:T(8,128)(2,1)} %constant.58.clone.refs_6_) | copy-start | bytes 786436
  2.0 33.9 %copy-start.5 = (f32[16,1024]{1,0:T(8,128)S(1)}, f32[16,1024]{1,0:T(8,128)}, u32[]{:S(2)}) copy-start(f32[16,1024]{1,0:T(8,128)} %constant.59.clone.refs_7_) | copy-start | bytes 196612
  2.0 33.9 %all-to-all-start = ((bf16[64,8,128]{2,1,0:T(8,128)(2,1)}), bf16[64,8,128]{2,1,0:T(8,128)(2,1)S(1)}, u32[]{:S(2)}, u32[]{:S(2)}) async-start(bf16[64,8,128]{2,1,0:T(8,128)(2,1)} %bitcast.17), calls=%async_computation | async-start | bytes 262144 | tf_op jit(solution)/shard_map/all_to_all | solution.py:296
  20.8 15.2 %copy-start.4 = (f32[16,1024]{1,0:T(8,128)S(1)}, f32[16,1024]{1,0:T(8,128)}, u32[]{:S(2)}) copy-start(f32[16,1024]{1,0:T(8,128)} %constant.60.clone.refs_8_) | copy-start | bytes 196612
  21.1 14.9 %copy-start.2 = (f32[1,1,7,16,256]{4,3,2,1,0:T(8,128)S(1)}, f32[1,1,7,16,256]{4,3,2,1,0:T(8,128)}, u32[]{:S(2)}) copy-start(f32[1,1,7,16,256]{4,3,2,1,0:T(8,128)} %param.15) | copy-start | bytes 344068
  21.1 14.9 %copy-start.3 = (f32[1,1,7,16,256]{4,3,2,1,0:T(8,128)S(1)}, f32[1,1,7,16,256]{4,3,2,1,0:T(8,128)}, u32[]{:S(2)}) copy-start(f32[1,1,7,16,256]{4,3,2,1,0:T(8,128)} %param.16) | copy-start | bytes 344068
  39.1 9.0 %collective-permute-start = (bf16[3,256,128]{2,1,0:T(8,128)(2,1)S(1)}, bf16[3,256,128]{2,1,0:T(8,128)(2,1)S(1)}, u32[]{:S(2)}, u32[]{:S(2)}) collective-permute-start(bf16[3,256,128]{2,1,0:T(8,128)(2,1)S(1)} %get-tuple-element.10), channel_id=1, source_target_pairs={{2,4},{3,5},{4,2},{5,3},{6,8},{7,9},{8,6},{9,7},{10,12},{11,13},{1... | collective-permute-start | bytes 589832 | tf_op jit(solution)/shard_map/ppermute | solution.py:325
  41.3 9.1 %collective-permute-start.2 = (bf16[256,128]{1,0:T(8,128)(2,1)S(1)}, bf16[256,128]{1,0:T(8,128)(2,1)S(1)}, u32[]{:S(2)}, u32[]{:S(2)}) collective-permute-start(bf16[256,128]{1,0:T(8,128)(2,1)S(1)} %get-tuple-element.12), channel_id=1, source_target_pairs={{1,4},{3,6},{4,1},{5,8},{6,3},{7,10},{8,5},{9,12},{10,7},{11,14},{... | collective-permute-start | bytes 196616 | tf_op jit(solution)/shard_map/ppermute | solution.py:327
  44.3 6.1 %collective-permute-start.1 = (bf16[2,256,128]{2,1,0:T(8,128)(2,1)S(1)}, bf16[2,256,128]{2,1,0:T(8,128)(2,1)S(1)}, u32[]{:S(2)}, u32[]{:S(2)}) collective-permute-start(bf16[2,256,128]{2,1,0:T(8,128)(2,1)S(1)} %get-tuple-element.11), channel_id=1, source_target_pairs={{0,2},{1,3},{2,0},{3,1},{4,6},{5,7},{6,4},{7,5},{8,10},{9,11},{10,... | collective-permute-start | bytes 393224 | tf_op jit(solution)/shard_map/ppermute | solution.py:326
  48.1 2.3 %collective-permute-start.3 = (bf16[256,128]{1,0:T(8,128)(2,1)S(1)}, bf16[256,128]{1,0:T(8,128)(2,1)S(1)}, u32[]{:S(2)}, u32[]{:S(2)}) collective-permute-start(bf16[256,128]{1,0:T(8,128)(2,1)S(1)} %slice_bitcast_fusion), channel_id=1, source_target_pairs={{30,29},{33,34},{94,93},{97,98},{158,157},{161,162},{222,221},{225... | collective-permute-start | bytes 196616 | tf_op jit(solution)/shard_map/ppermute | solution.py:336

commit v3 on v2

--- a/solution.py
+++ b/solution.py
@@ -21,6 +21,7 @@
 LANES = 128
 HALF = (WIN - 1) // 2
 GROUPS = P_SIZE * NF // LANES
+GROUP = 4
 
 two_pi = 2.0 * math.pi
 slow_step = 0.25
@@ -193,9 +194,9 @@
 
 def far_kernel(
     place_ref, foot_ref, arrived_ref, lateral_ref, times_ref, amps_ref, spread_ref, cos_ref,
-    sin_ref, seam_ref, pair_ref, outer_ref, beam_ref, u_ref, *, scale,
+    sin_ref, seam_ref, outer_ref, beam_ref, u_ref, *, scale,
 ):
-    core, odd = place_ref[0], place_ref[1]
+    place = place_ref[0]
 
     def beams_of():
         beams = slant_stack(
@@ -207,16 +208,15 @@
 
     def store(i, block):
         block = block.astype(bf16)
-        if i < 3:
-            seam_ref[i] = block
-        else:
-            pair_ref[i - 3] = block
-        if i == 2:
-            outer_ref[...] = block
-
-    left, right = 1 - core, 5 - core
-    to_seam, to_pair = jnp.where(odd == 0, left, right), jnp.where(odd == 0, right, left)
-    windows = [to_seam, to_seam + 1, core * (WIN - 1), to_pair, to_pair + 1]
+        is_outer = place == {0: 1, 1: -1, 2: 2}[i]
+        seam_ref[i] = jnp.where(is_outer, jnp.zeros_like(block), block)
+        if i != 1:
+
+            @pl.when(is_outer | (i == 0))
+            def _():
+                outer_ref[...] = block
+
+    windows = [(i - place + WIN) % WIN for i in range(HALF)]
     contributions(windows, beams_of, foot_ref, lateral_ref, times_ref, amps_ref, u_ref, store)
 
 
@@ -228,20 +228,26 @@
 
     first = HALF - place_ref[0]
     contributions(
-        [first, first + 1], lambda: (beam_ref[0:1], beam_ref[1:2]),
+        [first + i for i in range(GROUP)], lambda: (beam_ref[0:1], beam_ref[1:2]),
         foot_ref, lateral_ref, times_ref, amps_ref, u_ref, store,
     )
 
 
-def merge_kernel(place_ref, near_ref, seam_ref, pair_ref, outer_ref, last_ref, out_ref):
-    core = place_ref[0]
-    cores, rows = 2, out_ref.shape[1]
-    outer = outer_ref[...].astype(f32) + last_ref[...].astype(f32)
-    for i in range(cores):
-        total = near_ref[i] + seam_ref[i].astype(f32) + pair_ref[i].astype(f32)
-        total = (total + jnp.where(core == i, outer, 0.0)).astype(bf16)
-        for o in range(out_ref.shape[0] // cores):
-            out_ref[o * cores + i] = total[o * rows : (o + 1) * rows]
+def merge_kernel(place_ref, near_ref, seam_ref, outer_ref, out_ref):
+    first_chip = place_ref[0] < GROUP // 2
+    rows = out_ref.shape[1]
+    outer = outer_ref[...].astype(f32)
+    zero = jnp.zeros_like(outer)
+    for t in range(GROUP):
+        before = seam_ref[t].astype(f32) if t < HALF else zero
+        after = seam_ref[t - 1].astype(f32) if t >= 1 else zero
+        if t == 0:
+            before = before + outer
+        if t == GROUP - 1:
+            after = after + outer
+        total = (near_ref[t] + jnp.where(first_chip, before, after)).astype(bf16)
+        for o in range(out_ref.shape[0] // GROUP):
+            out_ref[o * GROUP + t] = total[o * rows : (o + 1) * rows]
 
 
 def total_kernel(parts_ref, out_ref):
@@ -282,7 +288,7 @@
 
 
 def shards(traces, centre_ids, midpoint_bins, ray_times, ray_amps, beam_lateral, footprint):
-    slab_axes = ("chip", "core")
+    slab_axes = ("group", "chip", "core")
     my_slab = lax.axis_index(slab_axes)
     slabs = lax.axis_size(slab_axes)
     offsets = lax.axis_size("offset")
@@ -301,52 +307,49 @@
     lateral = jnp.tile(lateral, (1, LANES // P_SIZE))
     foot = lax.dynamic_index_in_dim(footprint, my_slab, 0, keepdims=False)
     u_rows = 2 * P_SIZE * NF
-    place = jnp.stack([my_slab % 2, my_slab // 2 % 2]).astype(jnp.int32)
+    place = (my_slab % GROUP).astype(jnp.int32).reshape(1)
     cosine, sine, spread = slant_tables()
-    to_seam, to_pair, to_outer, beams = call(
+    to_seam, to_outer, beams = call(
         lambda *refs: far_kernel(*refs, scale=1.0 / math.sqrt(NT * count)),
-        (struct(3, depth, XW), struct(2, depth, XW), struct(depth, XW), struct32(2, NF * P_SIZE)),
+        (struct(HALF, depth, XW), struct(depth, XW), struct32(2, NF * P_SIZE)),
         [smem()] * 2 + [vmem()] * 7,
         24,
-        [pltpu.VMEM((WIN - 2, u_rows, depth), bf16)],
+        [pltpu.VMEM((HALF, u_rows, depth), bf16)],
     )(
         place, foot, arrived, lateral, ray_times[0, 0], ray_amps[0, 0],
         jnp.asarray(spread), jnp.asarray(cosine), jnp.asarray(sine),
     )
 
-    half = slabs // 2
-
-    def chip_pairs(parity):
-        pairs = [(i, i + 2 if i // 2 % 2 == parity else i - 2) for i in range(slabs)]
-        return [(i, j) for i, j in pairs if 0 <= j < slabs]
-
-    outward = [(i, i + 3 if i % 2 else i - 3) for i in range(slabs)]
-    outward = [(i, j) for i, j in outward if 0 <= j < slabs and i not in (half - 1, half)]
-    from_seam = lax.ppermute(to_seam, slab_axes, chip_pairs(1))
-    from_pair = lax.ppermute(to_pair, slab_axes, chip_pairs(0))
+    seam_step = (-2, -2, 2, 2)
+    outer_step = (0, 3, -3, 0)
+    over_seam = [(i, i + seam_step[i % GROUP]) for i in range(slabs)]
+    outward = [(i, i + outer_step[i % GROUP]) for i in range(slabs)]
+    over_seam = [(i, j) for i, j in over_seam if 0 <= j < slabs]
+    outward = [(i, j) for i, j in outward if 0 <= j < slabs and i != j]
+    from_seam = lax.ppermute(to_seam, slab_axes, over_seam)
     from_outer = lax.ppermute(to_outer, slab_axes, outward)
     near = call(
         near_kernel,
-        struct32(2, depth, XW),
+        struct32(GROUP, depth, XW),
         [smem()] * 2 + [vmem()] * 4,
         24,
-        [pltpu.VMEM((2, u_rows, depth), bf16)],
+        [pltpu.VMEM((GROUP, u_rows, depth), bf16)],
         flops=1 << 28,
     )(place, foot, beams, lateral, ray_times[0, 0], ray_amps[0, 0])
-    last = lax.ppermute(from_seam[2], slab_axes, [(half - 2, half - 3), (half + 1, half + 2)])
-    merged = call(merge_kernel, struct(2 * offsets, part, XW), [smem()] + [vmem()] * 5, 8)(
-        place, near, from_seam, from_pair, from_outer, last
+    merged = call(merge_kernel, struct(GROUP * offsets, part, XW), [smem()] + [vmem()] * 3, 8)(
+        place, near, from_seam, from_outer
     )
     parts = lax.all_to_all(
-        merged, ("offset", "core"), split_axis=0, concat_axis=0, tiled=True
+        merged, ("offset", "chip", "core"), split_axis=0, concat_axis=0, tiled=True
     )
     return call(total_kernel, struct32(part, XW), [vmem()], 4)(parts)
 
 
 def solution(mesh):
     offsets, slabs = mesh.devices.shape
-    chips = Mesh(mesh.devices.reshape(offsets, slabs // 2, 2), ("offset", "chip", "core"))
-    slab = ("chip", "core")
+    shape = (offsets, slabs // GROUP, GROUP // 2, 2)
+    chips = Mesh(mesh.devices.reshape(shape), ("offset", "group", "chip", "core"))
+    slab = ("group", "chip", "core")
     return jax.shard_map(
         shards,
         mesh=chips,

time: 69 us -> 67.1 us (0.972)
  the two profiles are of different devices: /device:TPU:49 before, /device:TPU:1 now
where the time goes in v3:
time: 67.1 us; the launch traced here: 66.6 us
  starting transfers between devices  26.1 us (39%)
  waiting for transfers between devices  17.4 us (26%)
  blocking collectives  14.3 us (21%)
  Pallas kernels  7.49 us (11%)
  local copies, waits for them, and re-layouts  1.26 us (2%)
    all_to_all x1, starting transfers between devices, shards(): lax.all_to_all(routed.reshape(slabs, ROWS, LANES), slab_axes, split_axis=...  19.9 us
    all_to_all x1, waiting for transfers between devices, shards(): lax.all_to_all(routed.reshape(slabs, ROWS, LANES), slab_axes, split_axis=...  17.3 us
    all_to_all x1, blocking collectives, shards(): lax.all_to_all(merged, ('offset', 'chip', 'core'), split_axis=0, concat_a...  14.3 us
    ppermute x1, starting transfers between devices, shards(): from_outer = lax.ppermute(to_outer, slab_axes, outward)  5.48 us
    pallas_call x1, Pallas kernels, shards(): call(near_kernel, struct32(GROUP, depth, XW), [smem()] * 2 + [vmem()] * 4...  2.38 us
    pallas_call x1, Pallas kernels, shards(): call(lambda *refs: far_kernel(*refs, scale=1.0 / math.sqrt(NT * count)),...  2.35 us
    pallas_call x1, Pallas kernels, shards(): call(route_kernel, struct(slabs * ROWS, LANES), [vmem()] * 5)  2.01 us
  transfers between devices with their start and end apart: 3, of which 1 were waited for; matrix products, arithmetic and copies ran while one was open for 1% of the time, Pallas kernels for 4%

profile of v3, /device:TPU:1, one launch (start us, length us, event | category | flops | bytes accessed | tf_op | source)
XLA Modules:
  0.0 66.6 jit_solution(5091012975509648312)
XLA Ops:
  0.0 0.0 copy-start
  0.0 0.0 copy-start.5
  0.0 2.0 %shard_map.118 = bf16[512,128]{1,0:T(8,128)(2,1)} custom-call(s32[1,128]{1,0:T(1,128)} %bitcast.18, s32[1,128]{1,0:T(1,128)} %bins_ref.1, bf16[128,256]{1,0:T(8,128)(2,1)} %bitcast.15, bf16[256,128]{1,0:T(8,128)(2,1)} %constant.47.clone.high_ref, bf16[256,128]{1,0:T(8,128)(2,1)} %constant.48.clone.low_ref), custom_call_target="tpu_custom_call" | custom-call | bytes 1048576 | tf_op jit(solution)/shard_map/pallas_call | solution.py:299
  2.0 0.0 copy-start.1
  2.0 19.9 %all-to-all-start = ((bf16[64,8,128]{2,1,0:T(8,128)(2,1)}), bf16[64,8,128]{2,1,0:T(8,128)(2,1)S(1)}, u32[]{:S(2)}, u32[]{:S(2)}) async-start(bf16[64,8,128]{2,1,0:T(8,128)(2,1)} %bitcast.14), calls=%async_computation | async-start | bytes 262144 | tf_op jit(solution)/shard_map/all_to_all | solution.py:302
  21.9 0.0 copy-start.6
  22.0 0.0 copy-start.4
  22.0 0.7 copy-done.6
  22.6 0.1 constant_dynamic-slice_fusion.1
  22.7 0.1 copy.13
  22.8 0.1 copy.16.refs_1_.foot_ref
  22.9 0.0 copy-done
  22.9 0.0 copy-start.2
  22.9 0.0 copy-start.3
  22.9 0.1 constant_dynamic-slice_fusion
  23.0 0.1 copy.17
  23.1 0.1 tile.13.refs_3_.lateral_ref
  23.2 17.3 %all-to-all-done = bf16[64,8,128]{2,1,0:T(8,128)(2,1)S(1)} async-done(((bf16[64,8,128]{2,1,0:T(8,128)(2,1)}), bf16[64,8,128]{2,1,0:T(8,128)(2,1)S(1)}, u32[]{:S(2)}, u32[]{:S(2)}) %all-to-all-start) | async-done | bytes 131104 | tf_op jit(solution)/shard_map/all_to_all | solution.py:302
  40.6 0.0 copy-done.5
  40.6 0.0 copy-done.1
  40.6 0.0 copy-done.4
  40.6 0.0 copy-done.2
  40.6 0.0 copy-done.3
  40.6 2.3 %shard_map.119 = (bf16[3,256,128]{2,1,0:T(8,128)(2,1)S(1)}, bf16[256,128]{1,0:T(8,128)(2,1)S(1)}, f32[2,1024]{1,0:T(2,128)S(1)}) custom-call(s32[1]{0:T(128)} %bitcast.refs_0_.place_ref, s32[7,2]{1,0:T(8,128)S(1)} %copy.16.refs_1_.foot_ref, bf16[512,128]{1,0:T(8,128)(2,1)S(1)} %bitcast.9, f32[7,128]{1,0:T(8,128)S(1)} %tile.13.refs_3_.lateral_ref, ...), custom_call_target="tpu_custom_call" | custom-call | bytes 1048576 | tf_op jit(solution)/shard_map/pallas_call | solution.py:312
  42.9 0.7 %collective-permute-start = (bf16[3,256,128]{2,1,0:T(8,128)(2,1)S(1)}, bf16[3,256,128]{2,1,0:T(8,128)(2,1)S(1)}, u32[]{:S(2)}, u32[]{:S(2)}) collective-permute-start(bf16[3,256,128]{2,1,0:T(8,128)(2,1)S(1)} %get-tuple-element.9), channel_id=1, source_target_pairs={{2,4},{3,5},{4,2},{5,3},{6,8},{7,9},{8,6},{9,7},{10,12},{11,13},{1... | collective-permute-start | bytes 589832 | tf_op jit(solution)/shard_map/ppermute | solution.py:329
  43.6 5.5 %collective-permute-start.1 = (bf16[256,128]{1,0:T(8,128)(2,1)S(1)}, bf16[256,128]{1,0:T(8,128)(2,1)S(1)}, u32[]{:S(2)}, u32[]{:S(2)}) collective-permute-start(bf16[256,128]{1,0:T(8,128)(2,1)S(1)} %get-tuple-element.10), channel_id=1, source_target_pairs={{1,4},{5,8},{6,3},{9,12},{10,7},{13,16},{14,11},{17,20},{18,15},{2... | collective-permute-start | bytes 196616 | tf_op jit(solution)/shard_map/ppermute | solution.py:330
  49.1 2.4 %shard_map.120.near_ref = f32[4,256,128]{2,1,0:T(8,128)S(1)} custom-call(s32[1]{0:T(128)} %bitcast.refs_0_.place_ref, s32[7,2]{1,0:T(8,128)S(1)} %copy.16.refs_1_.foot_ref, f32[2,1024]{1,0:T(2,128)S(1)} %get-tuple-element.8.beam_ref, f32[7,128]{1,0:T(8,128)S(1)} %tile.13.refs_3_.lateral_ref, f32[7,16,256]{2,1,0:T(8,128)S(1)} %bitcast.11, ...), custom_call_target="tpu_custom_call" | custom-call | flops 268435456 | bytes 1048576 | tf_op jit(solution)/shard_map/pallas_call | solution.py:331
  51.5 0.0 collective-permute-done.1.outer_ref
  51.5 0.0 collective-permute-done.seam_ref
  51.5 0.1 shard_map.121
  51.6 14.3 %all_to_all.10.parts_ref = bf16[32,32,128]{2,1,0:T(8,128)(2,1)S(1)} all-to-all(bf16[32,32,128]{2,1,0:T(8,128)(2,1)S(1)} %shard_map.121), channel_id=1, replica_groups=mesh['offset'=8,'group'=16,'chip'=2,'core'=2] {'offset','chip','core'}, dimensions={0} | all-to-all | bytes 524288 | tf_op jit(solution)/shard_map/all_to_all | solution.py:342
  66.0 0.7 shard_map.122
  (1 shorter events, 0.0 us)
Async XLA Ops:
  0.0 22.9 %copy-start = (f32[1,64,7,16]{1,3,2,0:T(8,128)S(1)}, f32[1,64,7,16]{1,3,2,0:T(8,128)}, u32[]{:S(2)}) copy-start(f32[1,64,7,16]{1,3,2,0:T(8,128)} %param.17) | copy-start | bytes 86020
  0.0 40.6 %copy-start.5 = (f32[16,1024]{1,0:T(8,128)S(1)}, f32[16,1024]{1,0:T(8,128)}, u32[]{:S(2)}) copy-start(f32[16,1024]{1,0:T(8,128)} %constant.50.clone.refs_7_) | copy-start | bytes 196612
  2.0 38.6 %copy-start.1 = (bf16[128,1024]{1,0:T(8,128)(2,1)S(1)}, bf16[128,1024]{1,0:T(8,128)(2,1)}, u32[]{:S(2)}) copy-start(bf16[128,1024]{1,0:T(8,128)(2,1)} %constant.49.clone.refs_6_) | copy-start | bytes 786436
  2.0 38.5 %all-to-all-start = ((bf16[64,8,128]{2,1,0:T(8,128)(2,1)}), bf16[64,8,128]{2,1,0:T(8,128)(2,1)S(1)}, u32[]{:S(2)}, u32[]{:S(2)}) async-start(bf16[64,8,128]{2,1,0:T(8,128)(2,1)} %bitcast.14), calls=%async_computation | async-start | bytes 262144 | tf_op jit(solution)/shard_map/all_to_all | solution.py:302
  21.9 0.7 %copy-start.6 = (s32[64,7,2]{0,2,1:T(2,128)S(1)}, s32[64,7,2]{0,2,1:T(2,128)}, u32[]{:S(2)}) copy-start(s32[64,7,2]{0,2,1:T(2,128)} %param.18) | copy-start | bytes 10756
  22.0 18.6 %copy-start.4 = (f32[16,1024]{1,0:T(8,128)S(1)}, f32[16,1024]{1,0:T(8,128)}, u32[]{:S(2)}) copy-start(f32[16,1024]{1,0:T(8,128)} %constant.51.clone.refs_8_) | copy-start | bytes 196612
  22.9 17.7 %copy-start.2 = (f32[1,1,7,16,256]{4,3,2,1,0:T(8,128)S(1)}, f32[1,1,7,16,256]{4,3,2,1,0:T(8,128)}, u32[]{:S(2)}) copy-start(f32[1,1,7,16,256]{4,3,2,1,0:T(8,128)} %param.15) | copy-start | bytes 344068
  22.9 17.7 %copy-start.3 = (f32[1,1,7,16,256]{4,3,2,1,0:T(8,128)S(1)}, f32[1,1,7,16,256]{4,3,2,1,0:T(8,128)}, u32[]{:S(2)}) copy-start(f32[1,1,7,16,256]{4,3,2,1,0:T(8,128)} %param.16) | copy-start | bytes 344068
  42.9 8.6 %collective-permute-start = (bf16[3,256,128]{2,1,0:T(8,128)(2,1)S(1)}, bf16[3,256,128]{2,1,0:T(8,128)(2,1)S(1)}, u32[]{:S(2)}, u32[]{:S(2)}) collective-permute-start(bf16[3,256,128]{2,1,0:T(8,128)(2,1)S(1)} %get-tuple-element.9), channel_id=1, source_target_pairs={{2,4},{3,5},{4,2},{5,3},{6,8},{7,9},{8,6},{9,7},{10,12},{11,13},{1... | collective-permute-start | bytes 589832 | tf_op jit(solution)/shard_map/ppermute | solution.py:329
  43.6 7.9 %collective-permute-start.1 = (bf16[256,128]{1,0:T(8,128)(2,1)S(1)}, bf16[256,128]{1,0:T(8,128)(2,1)S(1)}, u32[]{:S(2)}, u32[]{:S(2)}) collective-permute-start(bf16[256,128]{1,0:T(8,128)(2,1)S(1)} %get-tuple-element.10), channel_id=1, source_target_pairs={{1,4},{5,8},{6,3},{9,12},{10,7},{13,16},{14,11},{17,20},{18,15},{2... | collective-permute-start | bytes 196616 | tf_op jit(solution)/shard_map/ppermute | solution.py:330

commit v4 on v3

--- a/solution.py
+++ b/solution.py
@@ -158,12 +158,12 @@
             yield
 
 
-def v_groups(w, beam_re, beam_im, foot_ref, lateral_ref):
-    xs = iota((XW, LANES), 0)
+def v_groups(lateral, first, end, beam_re, beam_im):
+    xs = iota((XW, LANES), 0).astype(f32)
     freq = (iota((XW, LANES), 1) // P_SIZE + KLO).astype(f32) * (omega_step / width_scale)
-    away = xs.astype(f32) - lateral_ref[pl.ds(w, 1), :]
+    away = xs - lateral
     minus = -(away * away)
-    inside = (xs >= foot_ref[w, 0]) & (xs < foot_ref[w, 1])
+    inside = (xs >= first) & (xs < end)
     gauss = jnp.where(inside, jnp.exp(minus * freq), 0.0) * (1.0 / math.sqrt(P_SIZE * NF))
     ratio = jnp.exp(minus * ((LANES // P_SIZE) * omega_step / width_scale))
     for group in range(GROUPS):
@@ -175,77 +175,93 @@
         gauss = gauss * ratio
 
 
-def contributions(windows, beams_of, foot_ref, lateral_ref, times_ref, amps_ref, u_ref, store):
-    def u_of(i):
-        return u_groups(u_ref.at[i], times_ref[windows[i]], amps_ref[windows[i]])
-
-    for _ in u_of(0):
+def contributions(windows, u_ref):
+    blocks = []
+    for _ in u_groups(u_ref.at[0], *windows[0][:2]):
         pass
-    beam_re, beam_im = beams_of()
-    for i, w in enumerate(windows):
-        following = u_of(i + 1) if i + 1 < len(windows) else iter(())
+    for i, window in enumerate(windows):
+        following = iter(())
+        if i + 1 < len(windows):
+            following = u_groups(u_ref.at[i + 1], *windows[i + 1][:2])
         total = None
-        for group, v in enumerate(v_groups(w, beam_re, beam_im, foot_ref, lateral_ref)):
+        for group, v in enumerate(v_groups(*window[2:])):
             part = dot(v, u_ref[i, pl.ds(group * 2 * LANES, 2 * LANES), :])
             total = part if total is None else total + part
             next(following, None)
-        store(i, total.T)
-
-
-def far_kernel(
-    place_ref, foot_ref, arrived_ref, lateral_ref, times_ref, amps_ref, spread_ref, cos_ref,
-    sin_ref, seam_ref, outer_ref, beam_ref, u_ref, *, scale,
-):
+        blocks.append(total.T)
+    return blocks
+
+
+def pack_kernel(place_ref, foot_ref, lateral_ref, times_ref, amps_ref, seam_ref, outer_ref):
     place = place_ref[0]
 
-    def beams_of():
-        beams = slant_stack(
-            arrived_ref[...], spread_ref[...], cos_ref[...], sin_ref[...], scale
-        )
-        for i in range(2):
-            beam_ref[i : i + 1] = beams[i]
-        return beams
-
-    def store(i, block):
-        block = block.astype(bf16)
-        is_outer = place == {0: 1, 1: -1, 2: 2}[i]
-        seam_ref[i] = jnp.where(is_outer, jnp.zeros_like(block), block)
-        if i != 1:
-
-            @pl.when(is_outer | (i == 0))
-            def _():
-                outer_ref[...] = block
-
-    windows = [(i - place + WIN) % WIN for i in range(HALF)]
-    contributions(windows, beams_of, foot_ref, lateral_ref, times_ref, amps_ref, u_ref, store)
+    def pack(w, ref):
+        ref[0:P_SIZE] = times_ref[w]
+        ref[P_SIZE : 2 * P_SIZE] = amps_ref[w]
+        sub = iota((8, LANES), 0)
+        first, end = foot_ref[w, 0].astype(f32), foot_ref[w, 1].astype(f32)
+        lateral = jnp.broadcast_to(lateral_ref[pl.ds(w, 1), :], (8, LANES))
+        tail = jnp.where(sub == 0, lateral, jnp.where(sub == 1, first, end))
+        ref[2 * P_SIZE :] = jnp.concatenate([tail] * (ref.shape[1] // LANES), axis=1)
+
+    for i in range(HALF):
+        pack((i - place + WIN) % WIN, seam_ref.at[i])
+    pack(jnp.where(place == 1, WIN - 1, 0), outer_ref)
+
+
+def beams_kernel(arrived_ref, spread_ref, cos_ref, sin_ref, beam_ref, *, scale):
+    beams = slant_stack(arrived_ref[...], spread_ref[...], cos_ref[...], sin_ref[...], scale)
+    for i in range(2):
+        beam_ref[i : i + 1] = beams[i]
 
 
 def near_kernel(
     place_ref, foot_ref, beam_ref, lateral_ref, times_ref, amps_ref, near_ref, u_ref
 ):
-    def store(i, block):
+    windows = []
+    for i in range(GROUP):
+        w = HALF - place_ref[0] + i
+        first, end = foot_ref[w, 0].astype(f32), foot_ref[w, 1].astype(f32)
+        windows.append(
+            (times_ref[w], amps_ref[w], lateral_ref[pl.ds(w, 1), :], first, end,
+             beam_ref[0:1], beam_ref[1:2])
+        )
+    for i, block in enumerate(contributions(windows, u_ref)):
         near_ref[i] = block
 
-    first = HALF - place_ref[0]
-    contributions(
-        [first + i for i in range(GROUP)], lambda: (beam_ref[0:1], beam_ref[1:2]),
-        foot_ref, lateral_ref, times_ref, amps_ref, u_ref, store,
-    )
-
-
-def merge_kernel(place_ref, near_ref, seam_ref, outer_ref, out_ref):
-    first_chip = place_ref[0] < GROUP // 2
+
+def far_kernel(
+    place_ref, near_ref, seam_beam_ref, outer_beam_ref, seam_ref, outer_ref, out_ref, u_ref
+):
+    place = place_ref[0]
     rows = out_ref.shape[1]
-    outer = outer_ref[...].astype(f32)
-    zero = jnp.zeros_like(outer)
-    for t in range(GROUP):
-        before = seam_ref[t].astype(f32) if t < HALF else zero
-        after = seam_ref[t - 1].astype(f32) if t >= 1 else zero
-        if t == 0:
-            before = before + outer
-        if t == GROUP - 1:
-            after = after + outer
-        total = (near_ref[t] + jnp.where(first_chip, before, after)).astype(bf16)
+    windows = []
+    for i in range(HALF):
+        rays, beam_re, beam_im = seam_ref[i], seam_beam_ref[0:1], seam_beam_ref[1:2]
+        if i != 1:
+            from_outer = place == (0 if i else GROUP - 1)
+            rays = jnp.where(from_outer, outer_ref[...], rays)
+            beam_re = jnp.where(from_outer, outer_beam_ref[0:1], beam_re)
+            beam_im = jnp.where(from_outer, outer_beam_ref[1:2], beam_im)
+        tail = rays[2 * P_SIZE :, :LANES]
+        windows.append(
+            (rays[:P_SIZE], rays[P_SIZE : 2 * P_SIZE], tail[0:1], tail[1:2], tail[2:3],
+             beam_re, beam_im)
+        )
+    blocks = contributions(windows, u_ref)
+    first_chip = place < GROUP // 2
+    zero = jnp.zeros_like(blocks[0])
+    takes = (
+        ((first_chip, 0), (place == 0, 2)),
+        ((first_chip, 1), (place == 2, 0)),
+        ((place == 1, 2), (~first_chip, 1)),
+        ((place == 3, 0), (~first_chip, 2)),
+    )
+    for t, taken in enumerate(takes):
+        total = near_ref[t]
+        for when, i in taken:
+            total = total + jnp.where(when, blocks[i], zero)
+        total = total.astype(bf16)
         for o in range(out_ref.shape[0] // GROUP):
             out_ref[o * GROUP + t] = total[o * rows : (o + 1) * rows]
 
@@ -308,17 +324,6 @@
     foot = lax.dynamic_index_in_dim(footprint, my_slab, 0, keepdims=False)
     u_rows = 2 * P_SIZE * NF
     place = (my_slab % GROUP).astype(jnp.int32).reshape(1)
-    cosine, sine, spread = slant_tables()
-    to_seam, to_outer, beams = call(
-        lambda *refs: far_kernel(*refs, scale=1.0 / math.sqrt(NT * count)),
-        (struct(HALF, depth, XW), struct(depth, XW), struct32(2, NF * P_SIZE)),
-        [smem()] * 2 + [vmem()] * 7,
-        24,
-        [pltpu.VMEM((HALF, u_rows, depth), bf16)],
-    )(
-        place, foot, arrived, lateral, ray_times[0, 0], ray_amps[0, 0],
-        jnp.asarray(spread), jnp.asarray(cosine), jnp.asarray(sine),
-    )
 
     seam_step = (-2, -2, 2, 2)
     outer_step = (0, 3, -3, 0)
@@ -326,8 +331,26 @@
     outward = [(i, i + outer_step[i % GROUP]) for i in range(slabs)]
     over_seam = [(i, j) for i, j in over_seam if 0 <= j < slabs]
     outward = [(i, j) for i, j in outward if 0 <= j < slabs and i != j]
-    from_seam = lax.ppermute(to_seam, slab_axes, over_seam)
-    from_outer = lax.ppermute(to_outer, slab_axes, outward)
+    ray_rows = 2 * P_SIZE + 8
+    seam_rays, outer_rays = call(
+        pack_kernel,
+        (struct32(HALF, ray_rows, depth), struct32(ray_rows, depth)),
+        [smem()] * 2 + [vmem()] * 3,
+        8,
+        flops=1 << 28,
+    )(place, foot, lateral, ray_times[0, 0], ray_amps[0, 0])
+    seam_rays = lax.ppermute(seam_rays, slab_axes, over_seam)
+    outer_rays = lax.ppermute(outer_rays, slab_axes, outward)
+
+    cosine, sine, spread = slant_tables()
+    beams = call(
+        lambda *refs: beams_kernel(*refs, scale=1.0 / math.sqrt(NT * count)),
+        struct32(2, NF * P_SIZE),
+        [vmem()] * 4,
+        8,
+    )(arrived, jnp.asarray(spread), jnp.asarray(cosine), jnp.asarray(sine))
+    seam_beams = lax.ppermute(beams, slab_axes, over_seam)
+    outer_beams = lax.ppermute(beams, slab_axes, outward)
     near = call(
         near_kernel,
         struct32(GROUP, depth, XW),
@@ -336,9 +359,13 @@
         [pltpu.VMEM((GROUP, u_rows, depth), bf16)],
         flops=1 << 28,
     )(place, foot, beams, lateral, ray_times[0, 0], ray_amps[0, 0])
-    merged = call(merge_kernel, struct(GROUP * offsets, part, XW), [smem()] + [vmem()] * 3, 8)(
-        place, near, from_seam, from_outer
-    )
+    merged = call(
+        far_kernel,
+        struct(GROUP * offsets, part, XW),
+        [smem()] + [vmem()] * 5,
+        24,
+        [pltpu.VMEM((HALF, u_rows, depth), bf16)],
+    )(place, near, seam_beams, outer_beams, seam_rays, outer_rays)
     parts = lax.all_to_all(
         merged, ("offset", "chip", "core"), split_axis=0, concat_axis=0, tiled=True
     )

time: 67.1 us -> 64.3 us (0.958)
  waiting for transfers between devices: 17.4 us -> 9.13 us
  starting transfers between devices: 26.1 us -> 30.1 us
    all_to_all x1, waiting for transfers between devices: 17.3 us -> 9.12 us  [shards(): lax.all_to_all(routed.reshape(slabs, ROWS, LANES), slab_axes, split_axis=...]
    ppermute x2 -> x4, starting transfers between devices: 6.16 us -> 10.3 us  [the longest x1 6.24 us: shards(): outer_rays = lax.ppermute(outer_rays, slab_axes, outward)]
    pallas_call x2 -> x3, Pallas kernels: 2.45 us -> 2.55 us  [the longest x1 1.38 us: shards(): call(far_kernel, struct(GROUP * offsets, part, XW), [smem()] + [vmem()] *...]
  transfers between devices with their start and end apart: 3 -> 5, of which waited for: 1 -> 1; matrix products, arithmetic and copies ran while one was open for 1% -> 1% of each run, Pallas kernels for 4% -> 6%
where the time goes in v4:
time: 64.3 us; the launch traced here: 63.3 us
  starting transfers between devices  30.1 us (47%)
  blocking collectives  14.4 us (22%)
  waiting for transfers between devices  9.13 us (14%)
  Pallas kernels  7.57 us (12%)
  local copies, waits for them, and re-layouts  1.93 us (3%)
    all_to_all x1, starting transfers between devices, shards(): lax.all_to_all(routed.reshape(slabs, ROWS, LANES), slab_axes, split_axis=...  19.8 us
    all_to_all x1, blocking collectives, shards(): lax.all_to_all(merged, ('offset', 'chip', 'core'), split_axis=0, concat_a...  14.4 us
    all_to_all x1, waiting for transfers between devices, shards(): lax.all_to_all(routed.reshape(slabs, ROWS, LANES), slab_axes, split_axis=...  9.12 us
    ppermute x1, starting transfers between devices, shards(): outer_rays = lax.ppermute(outer_rays, slab_axes, outward)  6.24 us
    ppermute x1, starting transfers between devices, shards(): outer_beams = lax.ppermute(beams, slab_axes, outward)  2.76 us
    pallas_call x1, Pallas kernels, shards(): call(near_kernel, struct32(GROUP, depth, XW), [smem()] * 2 + [vmem()] * 4...  2.37 us
    pallas_call x1, Pallas kernels, shards(): call(route_kernel, struct(slabs * ROWS, LANES), [vmem()] * 5)  1.99 us
    unnamed x15, local copies, waits for them, and re-layouts  1.48 us
  transfers between devices with their start and end apart: 5, of which 1 were waited for; matrix products, arithmetic and copies ran while one was open for 1% of the time, Pallas kernels for 6%

profile of v4, /device:TPU:1, one launch (start us, length us, event | category | flops | bytes accessed | tf_op | source)
XLA Modules:
  0.0 63.3 jit_solution(8062395174098665864)
XLA Ops:
  0.0 0.0 copy-start
  0.0 2.0 %shard_map.118 = bf16[512,128]{1,0:T(8,128)(2,1)} custom-call(s32[1,128]{1,0:T(1,128)} %bitcast.18, s32[1,128]{1,0:T(1,128)} %bins_ref.1, bf16[128,256]{1,0:T(8,128)(2,1)} %bitcast.15, bf16[256,128]{1,0:T(8,128)(2,1)} %constant.47.clone.high_ref, bf16[256,128]{1,0:T(8,128)(2,1)} %constant.48.clone.low_ref), custom_call_target="tpu_custom_call" | custom-call | bytes 1048576 | tf_op jit(solution)/shard_map/pallas_call | solution.py:315
  2.0 19.8 %all-to-all-start = ((bf16[64,8,128]{2,1,0:T(8,128)(2,1)}), bf16[64,8,128]{2,1,0:T(8,128)(2,1)S(1)}, u32[]{:S(2)}, u32[]{:S(2)}) async-start(bf16[64,8,128]{2,1,0:T(8,128)(2,1)} %bitcast.14), calls=%async_computation | async-start | bytes 262144 | tf_op jit(solution)/shard_map/all_to_all | solution.py:318
  21.8 0.0 copy-start.6
  21.8 0.7 %copy-done.6 = s32[64,7,2]{0,2,1:T(2,128)S(1)} copy-done((s32[64,7,2]{0,2,1:T(2,128)S(1)}, s32[64,7,2]{0,2,1:T(2,128)}, u32[]{:S(2)}) %copy-start.6) | copy-done | bytes 3608
  22.5 0.1 constant_dynamic-slice_fusion.1
  22.6 0.1 copy.13
  22.7 0.1 copy.15.foot_ref
  22.8 0.0 copy-done
  22.8 0.1 constant_dynamic-slice_fusion
  22.9 0.1 copy.17
  23.0 0.1 tile.13.lateral_ref
  23.1 0.6 copy-done.4
  23.7 0.1 copy-done.5
  23.7 0.6 shard_map.121
  24.4 0.7 %collective-permute-start.2 = (f32[3,40,256]{2,1,0:T(8,128)S(1)}, f32[3,40,256]{2,1,0:T(8,128)S(1)}, u32[]{:S(2)}, u32[]{:S(2)}) collective-permute-start(f32[3,40,256]{2,1,0:T(8,128)S(1)} %get-tuple-element.7), channel_id=1, source_target_pairs={{2,4},{3,5},{4,2},{5,3},{6,8},{7,9},{8,6},{9,7},{10,12},{11,13},{1... | collective-permute-start | bytes 368648 | tf_op jit(solution)/shard_map/ppermute | solution.py:342
  25.0 6.2 %collective-permute-start.3 = (f32[40,256]{1,0:T(8,128)S(1)}, f32[40,256]{1,0:T(8,128)S(1)}, u32[]{:S(2)}, u32[]{:S(2)}) collective-permute-start(f32[40,256]{1,0:T(8,128)S(1)} %get-tuple-element.8), channel_id=1, source_target_pairs={{1,4},{5,8},{6,3},{9,12},{10,7},{13,16},{14,11},{17,20},{18,15},{2... | collective-permute-start | bytes 122888 | tf_op jit(solution)/shard_map/ppermute | solution.py:343
  31.3 9.1 %all-to-all-done = bf16[64,8,128]{2,1,0:T(8,128)(2,1)S(1)} async-done(((bf16[64,8,128]{2,1,0:T(8,128)(2,1)}), bf16[64,8,128]{2,1,0:T(8,128)(2,1)S(1)}, u32[]{:S(2)}, u32[]{:S(2)}) %all-to-all-start) | async-done | bytes 131104 | tf_op jit(solution)/shard_map/all_to_all | solution.py:318
  40.4 0.0 copy-done.1
  40.4 0.0 copy-done.2
  40.4 0.0 copy-done.3
  40.4 0.5 shard_map.119.beam_ref
  41.0 2.8 %collective-permute-start.1 = (f32[2,1024]{1,0:T(2,128)S(1)}, f32[2,1024]{1,0:T(2,128)S(1)}, u32[]{:S(2)}, u32[]{:S(2)}) collective-permute-start(f32[2,1024]{1,0:T(2,128)S(1)} %shard_map.119.beam_ref), channel_id=1, source_target_pairs={{1,4},{5,8},{6,3},{9,12},{10,7},{13,16},{14,11},{17,20},{18,15},{2... | collective-permute-start | bytes 24584 | tf_op jit(solution)/shard_map/ppermute | solution.py:353
  43.7 0.7 %collective-permute-start = (f32[2,1024]{1,0:T(2,128)S(1)}, f32[2,1024]{1,0:T(2,128)S(1)}, u32[]{:S(2)}, u32[]{:S(2)}) collective-permute-start(f32[2,1024]{1,0:T(2,128)S(1)} %shard_map.119.beam_ref), channel_id=1, source_target_pairs={{2,4},{3,5},{4,2},{5,3},{6,8},{7,9},{8,6},{9,7},{10,12},{11,13},{1... | collective-permute-start | bytes 24584 | tf_op jit(solution)/shard_map/ppermute | solution.py:352
  44.4 2.4 %shard_map.120.near_ref = f32[4,256,128]{2,1,0:T(8,128)S(1)} custom-call(s32[1]{0:T(128)} %bitcast.place_ref, s32[7,2]{1,0:T(8,128)S(1)} %copy.15.foot_ref, f32[2,1024]{1,0:T(2,128)S(1)} %shard_map.119.beam_ref, f32[7,128]{1,0:T(8,128)S(1)} %tile.13.lateral_ref, f32[7,16,256]{2,1,0:T(8,128)S(1)} %bitcast.11, f32[7,16,256]{2,1,0:T(8,128)S(1)} %bitcast.13), custom_call_target="tpu_custom_call" | custom-call | flops 268435456 | bytes 1048576 | tf_op jit(solution)/shard_map/pallas_call | solution.py:354
  46.8 0.0 collective-permute-done.3.outer_ref
  46.8 0.0 collective-permute-done.2.seam_ref
  46.8 0.0 collective-permute-done.1.outer_beam_ref
  46.8 0.0 collective-permute-done.seam_beam_ref
  46.8 1.4 %shard_map.122 = bf16[32,32,128]{2,1,0:T(8,128)(2,1)S(1)} custom-call(s32[1]{0:T(128)} %bitcast.place_ref, f32[4,256,128]{2,1,0:T(8,128)S(1)} %shard_map.120.near_ref, f32[2,1024]{1,0:T(2,128)S(1)} %collective-permute-done.seam_beam_ref, f32[2,1024]{1,0:T(2,128)S(1)} %collective-permute-done.1.outer_beam_ref, ...), custom_call_target="tpu_custom_call" | custom-call | bytes 1048576 | tf_op jit(solution)/shard_map/pallas_call | solution.py:362
  48.2 14.4 %all_to_all.10.parts_ref = bf16[32,32,128]{2,1,0:T(8,128)(2,1)S(1)} all-to-all(bf16[32,32,128]{2,1,0:T(8,128)(2,1)S(1)} %shard_map.122), channel_id=1, replica_groups=mesh['offset'=8,'group'=16,'chip'=2,'core'=2] {'offset','chip','core'}, dimensions={0} | all-to-all | bytes 524288 | tf_op jit(solution)/shard_map/all_to_all | solution.py:369
  62.6 0.7 %shard_map.123 = f32[32,128]{1,0:T(8,128)} custom-call(bf16[32,32,128]{2,1,0:T(8,128)(2,1)S(1)} %all_to_all.10.parts_ref), custom_call_target="tpu_custom_call" | custom-call | bytes 1048576 | tf_op jit(solution)/shard_map/pallas_call | solution.py:372
  (6 shorter events, 0.0 us)
Async XLA Ops:
  0.0 22.8 %copy-start = (f32[1,64,7,16]{1,3,2,0:T(8,128)S(1)}, f32[1,64,7,16]{1,3,2,0:T(8,128)}, u32[]{:S(2)}) copy-start(f32[1,64,7,16]{1,3,2,0:T(8,128)} %param.17) | copy-start | bytes 86020
  2.0 38.4 %all-to-all-start = ((bf16[64,8,128]{2,1,0:T(8,128)(2,1)}), bf16[64,8,128]{2,1,0:T(8,128)(2,1)S(1)}, u32[]{:S(2)}, u32[]{:S(2)}) async-start(bf16[64,8,128]{2,1,0:T(8,128)(2,1)} %bitcast.14), calls=%async_computation | async-start | bytes 262144 | tf_op jit(solution)/shard_map/all_to_all | solution.py:318
  21.8 0.7 %copy-start.6 = (s32[64,7,2]{0,2,1:T(2,128)S(1)}, s32[64,7,2]{0,2,1:T(2,128)}, u32[]{:S(2)}) copy-start(s32[64,7,2]{0,2,1:T(2,128)} %param.18) | copy-start | bytes 10756
  22.8 0.9 %copy-start.4 = (f32[1,1,7,16,256]{4,3,2,1,0:T(8,128)S(1)}, f32[1,1,7,16,256]{4,3,2,1,0:T(8,128)}, u32[]{:S(2)}) copy-start(f32[1,1,7,16,256]{4,3,2,1,0:T(8,128)} %param.15) | copy-start | bytes 344068
  22.8 1.0 %copy-start.5 = (f32[1,1,7,16,256]{4,3,2,1,0:T(8,128)S(1)}, f32[1,1,7,16,256]{4,3,2,1,0:T(8,128)}, u32[]{:S(2)}) copy-start(f32[1,1,7,16,256]{4,3,2,1,0:T(8,128)} %param.16) | copy-start | bytes 344068
  23.7 16.7 %copy-start.1 = (bf16[128,1024]{1,0:T(8,128)(2,1)S(1)}, bf16[128,1024]{1,0:T(8,128)(2,1)}, u32[]{:S(2)}) copy-start(bf16[128,1024]{1,0:T(8,128)(2,1)} %constant.49.clone.refs_1_) | copy-start | bytes 786436
  23.7 16.7 %copy-start.2 = (f32[16,1024]{1,0:T(8,128)S(1)}, f32[16,1024]{1,0:T(8,128)}, u32[]{:S(2)}) copy-start(f32[16,1024]{1,0:T(8,128)} %constant.51.clone.refs_3_) | copy-start | bytes 196612
  23.7 16.7 %copy-start.3 = (f32[16,1024]{1,0:T(8,128)S(1)}, f32[16,1024]{1,0:T(8,128)}, u32[]{:S(2)}) copy-start(f32[16,1024]{1,0:T(8,128)} %constant.50.clone.refs_2_) | copy-start | bytes 196612
  24.4 22.4 %collective-permute-start.2 = (f32[3,40,256]{2,1,0:T(8,128)S(1)}, f32[3,40,256]{2,1,0:T(8,128)S(1)}, u32[]{:S(2)}, u32[]{:S(2)}) collective-permute-start(f32[3,40,256]{2,1,0:T(8,128)S(1)} %get-tuple-element.7), channel_id=1, source_target_pairs={{2,4},{3,5},{4,2},{5,3},{6,8},{7,9},{8,6},{9,7},{10,12},{11,13},{1... | collective-permute-start | bytes 368648 | tf_op jit(solution)/shard_map/ppermute | solution.py:342
  25.0 21.8 %collective-permute-start.3 = (f32[40,256]{1,0:T(8,128)S(1)}, f32[40,256]{1,0:T(8,128)S(1)}, u32[]{:S(2)}, u32[]{:S(2)}) collective-permute-start(f32[40,256]{1,0:T(8,128)S(1)} %get-tuple-element.8), channel_id=1, source_target_pairs={{1,4},{5,8},{6,3},{9,12},{10,7},{13,16},{14,11},{17,20},{18,15},{2... | collective-permute-start | bytes 122888 | tf_op jit(solution)/shard_map/ppermute | solution.py:343
  41.0 5.8 %collective-permute-start.1 = (f32[2,1024]{1,0:T(2,128)S(1)}, f32[2,1024]{1,0:T(2,128)S(1)}, u32[]{:S(2)}, u32[]{:S(2)}) collective-permute-start(f32[2,1024]{1,0:T(2,128)S(1)} %shard_map.119.beam_ref), channel_id=1, source_target_pairs={{1,4},{5,8},{6,3},{9,12},{10,7},{13,16},{14,11},{17,20},{18,15},{2... | collective-permute-start | bytes 24584 | tf_op jit(solution)/shard_map/ppermute | solution.py:353
  43.7 3.1 %collective-permute-start = (f32[2,1024]{1,0:T(2,128)S(1)}, f32[2,1024]{1,0:T(2,128)S(1)}, u32[]{:S(2)}, u32[]{:S(2)}) collective-permute-start(f32[2,1024]{1,0:T(2,128)S(1)} %shard_map.119.beam_ref), channel_id=1, source_target_pairs={{2,4},{3,5},{4,2},{5,3},{6,8},{7,9},{8,6},{9,7},{10,12},{11,13},{1... | collective-permute-start | bytes 24584 | tf_op jit(solution)/shard_map/ppermute | solution.py:352

commit v5 on v4

--- a/solution.py
+++ b/solution.py
@@ -1,3 +1,4 @@
+import functools
 import math
 
 import jax
@@ -17,11 +18,15 @@
 CAP = 6
 WIN = 7
 XW = 128
-ROWS = 8
+ROWS = 16
 LANES = 128
 HALF = (WIN - 1) // 2
 GROUPS = P_SIZE * NF // LANES
 GROUP = 4
+FIRST_SLAB = 16
+SECOND_STEP = (-1, -3, 3, 1)
+THIRD_STEP = (-3, -4, 4, 3)
+THIRD_SLOT = (0, 3, 3, 0)
 
 two_pi = 2.0 * math.pi
 slow_step = 0.25
@@ -63,7 +68,14 @@
     return jnp.dot(a, b, preferred_element_type=f32)
 
 
-def route_kernel(ids_ref, bins_ref, traces_ref, high_ref, low_ref, out_ref):
+def by_place(place, choices):
+    value = choices[-1]
+    for i in reversed(range(len(choices) - 1)):
+        value = jnp.where(place == i, choices[i], value)
+    return value
+
+
+def route_kernel(ids_ref, bins_ref, traces_ref, high_ref, low_ref, out_ref, *, groups):
     count = traces_ref.shape[0]
     square = (count, count)
     row, col = iota(square, 0), iota(square, 1)
@@ -73,50 +85,69 @@
     )
     same = ids_down == ids_across.astype(f32)
     rank_across = jnp.sum(jnp.where(same & (row < col), 1.0, 0.0), axis=0, keepdims=True)
-    rank_down = jnp.sum(jnp.where(same & (col < row), 1.0, 0.0), axis=1, keepdims=True)
+    code_across = ids_across * 8 + rank_across.astype(jnp.int32)
     place_across = bins_ref[...].astype(f32) - (BINS - 1) / 2.0
     place_down = jnp.sum(jnp.where(row == col, place_across, 0.0), axis=1, keepdims=True)
     traces = traces_ref[...]
     spectrum = dot(traces, high_ref[...]) + dot(traces, low_ref[...])
-    places = jnp.where(col == rank_down.astype(jnp.int32), place_down, 0.0)
-    values = jnp.concatenate([spectrum, places], axis=1).astype(bf16)
-    out_rows = out_ref.shape[0]
-    slot = iota((out_rows, count), 0)
-    place_row = slot % ROWS == CAP
-    target = ids_across * ROWS + rank_across.astype(jnp.int32)
-    pick = (slot == target) | (place_row & (slot // ROWS == ids_across))
-    picked = dot(jnp.where(pick, 1.0, 0.0).astype(bf16), values)
-    out_ref[...] = jnp.where(place_row, picked[:, LANES:], picked[:, :LANES]).astype(bf16)
+    values = jnp.concatenate([spectrum, jnp.broadcast_to(place_down, square)], axis=1).astype(bf16)
+
+    group_rows = GROUP * ROWS
+    slot = iota((group_rows, count), 0) % ROWS
+    slab = iota((group_rows, count), 0) // ROWS
+    second = (slab + by_place(slab, SECOND_STEP)) * 8 + slot - CAP
+    third = (slab + by_place(slab, THIRD_STEP)) * 8 + slot - 2 * CAP
+    third = third + by_place(slab, THIRD_SLOT)
+    wanted = jnp.where(slot < CAP, slab * 8 + slot, jnp.where(slot < 2 * CAP, second, third))
+    wanted = jnp.where(slot == ROWS - 1, -(1 << 20), wanted)
+    pick = [
+        jnp.where(wanted + group * GROUP * 8 == code_across, 1.0, 0.0).astype(bf16)
+        for group in groups
+    ]
+    picked = dot(jnp.concatenate(pick, axis=0), values).reshape(-1, ROWS, 2 * LANES)
+    shape = picked.shape[:2] + (LANES,)
+    places = jnp.where(iota(shape, 1) == iota(shape, 2), picked[:, :, LANES:], 0.0)
+    places = jnp.broadcast_to(jnp.sum(places, axis=1, keepdims=True), shape)
+    block = jnp.where(iota(shape, 1) == ROWS - 1, places, picked[:, :, :LANES])
+    out_ref[...] = block.reshape(out_ref.shape).astype(bf16)
 
 
 def slant_stack(arrived, spread, cosine, sine, scale):
     rows = arrived.shape[0]
-    full = arrived.astype(f32).reshape(rows // ROWS, ROWS, LANES)
-    sub, lane = iota((rows // ROWS, ROWS, LANES), 1), iota((rows // ROWS, ROWS, LANES), 2)
-    own = jnp.where(sub == lane, jnp.broadcast_to(full[:, CAP : CAP + 1, :], full.shape), 0.0)
-    own = own.reshape(rows, LANES).astype(bf16)
+    shape = (rows // ROWS, ROWS, LANES)
+    full = arrived.astype(f32).reshape(shape)
+    last = jnp.broadcast_to(full[:, ROWS - 1 :, :], shape)
+    own = jnp.where(iota(shape, 1) == iota(shape, 2), last, 0.0).reshape(rows, LANES).astype(bf16)
     place = dot(own, jnp.ones((LANES, LANES), bf16))
-    bin_place = iota((rows, LANES), 1).astype(f32) - (BINS - 1) / 2.0
-    in_bin = jnp.where((place == bin_place) & (place != 0.0), 1.0, 0.0).astype(bf16)
+    lane, slot = iota((rows, LANES), 1), iota((rows, LANES), 0) % ROWS
+    centre = jnp.where(slot < CAP, 0, jnp.where(slot < 2 * CAP, 1, 2))
+    bin_place = (lane % BINS).astype(f32) - (BINS - 1) / 2.0
+    hit = (place == bin_place) & (lane // BINS == centre) & (slot < ROWS - 1)
+    in_bin = jnp.where(hit, 1.0, 0.0).astype(bf16)
+    number = 3 * BINS
     binned = lax.dot_general(
         in_bin, arrived, (((0,), (0,)), ((), ())), preferred_element_type=f32
-    )[:BINS]
-    real = iota((BINS, LANES), 1) < NF
-    binned_re = jnp.where(real, binned, 0.0)
-    binned_im = jnp.where(real, 0.0, binned)
+    )[:number]
+    real = iota((number, LANES), 1) < NF
     parts = []
-    for part in (binned_re, binned_im):
+    for part in (jnp.where(real, binned, 0.0), jnp.where(real, 0.0, binned)):
         high = part.astype(bf16)
         parts += [high, (part - high.astype(f32)).astype(bf16)]
     wide = dot(jnp.concatenate(parts, axis=0), spread)
-    wide_re = wide[:BINS] + wide[BINS : 2 * BINS]
-    wide_im = wide[2 * BINS : 3 * BINS] + wide[3 * BINS :]
-    beam_re = jnp.sum(wide_re * cosine + wide_im * sine, axis=0, keepdims=True)
-    beam_im = jnp.sum(wide_im * cosine - wide_re * sine, axis=0, keepdims=True)
-    return (
-        (beam_re * scale).astype(bf16).astype(f32),
-        (beam_im * scale).astype(bf16).astype(f32),
-    )
+    wide_re = wide[:number] + wide[number : 2 * number]
+    wide_im = wide[2 * number : 3 * number] + wide[3 * number :]
+    beams = []
+    for first in range(0, number, BINS):
+        re, im = wide_re[first : first + BINS], wide_im[first : first + BINS]
+        beam_re = jnp.sum(re * cosine + im * sine, axis=0, keepdims=True)
+        beam_im = jnp.sum(im * cosine - re * sine, axis=0, keepdims=True)
+        beams.append(
+            (
+                (beam_re * scale).astype(bf16).astype(f32),
+                (beam_im * scale).astype(bf16).astype(f32),
+            )
+        )
+    return beams
 
 
 def cos_sin_turns(turns):
@@ -188,11 +219,13 @@
             part = dot(v, u_ref[i, pl.ds(group * 2 * LANES, 2 * LANES), :])
             total = part if total is None else total + part
             next(following, None)
-        blocks.append(total.T)
+        blocks.append(total)
     return blocks
 
 
-def pack_kernel(place_ref, foot_ref, lateral_ref, times_ref, amps_ref, seam_ref, outer_ref):
+def pack_kernel(
+    place_ref, foot_ref, lateral_ref, times_ref, amps_ref, seam_ref, outer_ref, near_ref, flag_ref
+):
     place = place_ref[0]
 
     def pack(w, ref):
@@ -204,64 +237,48 @@
         tail = jnp.where(sub == 0, lateral, jnp.where(sub == 1, first, end))
         ref[2 * P_SIZE :] = jnp.concatenate([tail] * (ref.shape[1] // LANES), axis=1)
 
+    base = jnp.where(place < GROUP // 2, 0, WIN - place)
     for i in range(HALF):
-        pack((i - place + WIN) % WIN, seam_ref.at[i])
+        pack(jnp.minimum(base + i, WIN - 1), seam_ref.at[i])
     pack(jnp.where(place == 1, WIN - 1, 0), outer_ref)
-
-
-def beams_kernel(arrived_ref, spread_ref, cos_ref, sin_ref, beam_ref, *, scale):
-    beams = slant_stack(arrived_ref[...], spread_ref[...], cos_ref[...], sin_ref[...], scale)
-    for i in range(2):
-        beam_ref[i : i + 1] = beams[i]
-
-
-def near_kernel(
-    place_ref, foot_ref, beam_ref, lateral_ref, times_ref, amps_ref, near_ref, u_ref
+    for i in range(GROUP):
+        pack(HALF - place + i, near_ref.at[i])
+    flag_ref[...] = jnp.full(flag_ref.shape, place.astype(f32))
+
+
+def unpack(rays):
+    tail = rays[2 * P_SIZE :, :LANES]
+    return rays[:P_SIZE], rays[P_SIZE : 2 * P_SIZE], tail[0:1], tail[1:2], tail[2:3]
+
+
+def migrate_kernel(
+    flag_ref, arrived_ref, spread_ref, cos_ref, sin_ref, near_ref, second_ref, third_0_ref,
+    third_1_ref, out_ref, u_ref, *, scale,
 ):
-    windows = []
-    for i in range(GROUP):
-        w = HALF - place_ref[0] + i
-        first, end = foot_ref[w, 0].astype(f32), foot_ref[w, 1].astype(f32)
-        windows.append(
-            (times_ref[w], amps_ref[w], lateral_ref[pl.ds(w, 1), :], first, end,
-             beam_ref[0:1], beam_ref[1:2])
-        )
-    for i, block in enumerate(contributions(windows, u_ref)):
-        near_ref[i] = block
-
-
-def far_kernel(
-    place_ref, near_ref, seam_beam_ref, outer_beam_ref, seam_ref, outer_ref, out_ref, u_ref
-):
-    place = place_ref[0]
+    own, second, third = slant_stack(
+        arrived_ref[...], spread_ref[...], cos_ref[...], sin_ref[...], scale
+    )
+    windows = [unpack(near_ref[i]) + own for i in range(GROUP)]
+    windows += [unpack(second_ref[i]) + second for i in range(HALF)]
+    windows += [unpack(third_0_ref[...] + third_1_ref[...]) + third]
+    blocks = contributions(windows, u_ref)
+    near, (a, b, c, d) = blocks[:GROUP], blocks[GROUP:]
     rows = out_ref.shape[1]
-    windows = []
-    for i in range(HALF):
-        rays, beam_re, beam_im = seam_ref[i], seam_beam_ref[0:1], seam_beam_ref[1:2]
-        if i != 1:
-            from_outer = place == (0 if i else GROUP - 1)
-            rays = jnp.where(from_outer, outer_ref[...], rays)
-            beam_re = jnp.where(from_outer, outer_beam_ref[0:1], beam_re)
-            beam_im = jnp.where(from_outer, outer_beam_ref[1:2], beam_im)
-        tail = rays[2 * P_SIZE :, :LANES]
-        windows.append(
-            (rays[:P_SIZE], rays[P_SIZE : 2 * P_SIZE], tail[0:1], tail[1:2], tail[2:3],
-             beam_re, beam_im)
-        )
-    blocks = contributions(windows, u_ref)
-    first_chip = place < GROUP // 2
-    zero = jnp.zeros_like(blocks[0])
-    takes = (
-        ((first_chip, 0), (place == 0, 2)),
-        ((first_chip, 1), (place == 2, 0)),
-        ((place == 1, 2), (~first_chip, 1)),
-        ((place == 3, 0), (~first_chip, 2)),
-    )
-    for t, taken in enumerate(takes):
-        total = near_ref[t]
-        for when, i in taken:
-            total = total + jnp.where(when, blocks[i], zero)
-        total = total.astype(bf16)
+    place = flag_ref[0:1, :]
+    is_0, is_2, is_3 = place == 0.0, place == 2.0, place == 3.0
+    first = place < GROUP / 2
+
+    def when(condition, block):
+        return jnp.where(condition, block, 0.0)
+
+    totals = (
+        near[0] + when(first, a + d),
+        near[1] + when(first, b) + when(is_3, a),
+        near[2] + when(is_0, c) + when(is_3, b) + when(is_2, a),
+        near[3] + when(is_3, c) + when(is_2, b) + when(~first, d),
+    )
+    for t, total in enumerate(totals):
+        total = total.T.astype(bf16)
         for o in range(out_ref.shape[0] // GROUP):
             out_ref[o * GROUP + t] = total[o * rows : (o + 1) * rows]
 
@@ -312,11 +329,14 @@
     depth = ray_times.shape[4]
     part = depth // offsets
     high, low = dft_tables()
-    routed = call(route_kernel, struct(slabs * ROWS, LANES), [vmem()] * 5)(
+    groups = [(FIRST_SLAB // GROUP + i) % (slabs // GROUP) for i in range(slabs // GROUP)]
+    order = [group * GROUP + i for group in groups for i in range(GROUP)]
+    routed = call(functools.partial(route_kernel, groups=groups), struct(slabs * ROWS, LANES), [vmem()] * 5)(
         centre_ids.reshape(1, count), midpoint_bins, traces[0], jnp.asarray(high), jnp.asarray(low)
     )
     arrived = lax.all_to_all(
-        routed.reshape(slabs, ROWS, LANES), slab_axes, split_axis=0, concat_axis=0, tiled=True
+        routed.reshape(slabs, ROWS, LANES), slab_axes, split_axis=0, concat_axis=0,
+        axis_index_groups=[order], tiled=True,
     ).reshape(slabs * ROWS, LANES)
 
     lateral = lax.dynamic_index_in_dim(beam_lateral[0], my_slab, 0, keepdims=False)
@@ -325,47 +345,36 @@
     u_rows = 2 * P_SIZE * NF
     place = (my_slab % GROUP).astype(jnp.int32).reshape(1)
 
-    seam_step = (-2, -2, 2, 2)
-    outer_step = (0, 3, -3, 0)
-    over_seam = [(i, i + seam_step[i % GROUP]) for i in range(slabs)]
-    outward = [(i, i + outer_step[i % GROUP]) for i in range(slabs)]
-    over_seam = [(i, j) for i, j in over_seam if 0 <= j < slabs]
-    outward = [(i, j) for i, j in outward if 0 <= j < slabs and i != j]
+    def to_those(steps):
+        pairs = [(i + steps[i % GROUP], i) for i in range(slabs) if steps[i % GROUP]]
+        return [(i, j) for i, j in pairs if 0 <= i < slabs]
+
     ray_rows = 2 * P_SIZE + 8
-    seam_rays, outer_rays = call(
+    seam_rays, outer_rays, near_rays, flags = call(
         pack_kernel,
-        (struct32(HALF, ray_rows, depth), struct32(ray_rows, depth)),
+        (
+            struct32(HALF, ray_rows, depth), struct32(ray_rows, depth),
+            struct32(GROUP, ray_rows, depth), struct32(8, depth),
+        ),
         [smem()] * 2 + [vmem()] * 3,
         8,
         flops=1 << 28,
     )(place, foot, lateral, ray_times[0, 0], ray_amps[0, 0])
-    seam_rays = lax.ppermute(seam_rays, slab_axes, over_seam)
-    outer_rays = lax.ppermute(outer_rays, slab_axes, outward)
+    second_rays = lax.ppermute(seam_rays, slab_axes, to_those(SECOND_STEP))
+    third_0 = lax.ppermute(outer_rays, slab_axes, to_those((THIRD_STEP[0], 0, 0, THIRD_STEP[3])))
+    third_1 = lax.ppermute(outer_rays, slab_axes, to_those((0, THIRD_STEP[1], THIRD_STEP[2], 0)))
 
     cosine, sine, spread = slant_tables()
-    beams = call(
-        lambda *refs: beams_kernel(*refs, scale=1.0 / math.sqrt(NT * count)),
-        struct32(2, NF * P_SIZE),
-        [vmem()] * 4,
-        8,
-    )(arrived, jnp.asarray(spread), jnp.asarray(cosine), jnp.asarray(sine))
-    seam_beams = lax.ppermute(beams, slab_axes, over_seam)
-    outer_beams = lax.ppermute(beams, slab_axes, outward)
-    near = call(
-        near_kernel,
-        struct32(GROUP, depth, XW),
-        [smem()] * 2 + [vmem()] * 4,
-        24,
-        [pltpu.VMEM((GROUP, u_rows, depth), bf16)],
-        flops=1 << 28,
-    )(place, foot, beams, lateral, ray_times[0, 0], ray_amps[0, 0])
     merged = call(
-        far_kernel,
+        lambda *refs: migrate_kernel(*refs, scale=1.0 / math.sqrt(NT * count)),
         struct(GROUP * offsets, part, XW),
-        [smem()] + [vmem()] * 5,
-        24,
-        [pltpu.VMEM((HALF, u_rows, depth), bf16)],
-    )(place, near, seam_beams, outer_beams, seam_rays, outer_rays)
+        [vmem()] * 9,
+        32,
+        [pltpu.VMEM((GROUP + HALF + 1, u_rows, depth), bf16)],
+    )(
+        flags, arrived, jnp.asarray(spread), jnp.asarray(cosine), jnp.asarray(sine),
+        near_rays, second_rays, third_0, third_1,
+    )
     parts = lax.all_to_all(
         merged, ("offset", "chip", "core"), split_axis=0, concat_axis=0, tiled=True
     )

time: 64.3 us -> 59.5 us (0.925); the launches traced: 63.3 us -> 59.2 us
  waiting for transfers between devices: 9.13 us -> 4.89 us
    all_to_all x1, waiting for transfers between devices: 9.12 us -> 2.08 us  [shards(): lax.all_to_all(routed.reshape(slabs, ROWS, LANES), slab_axes, split_axis=...]
    all_to_all x1, starting transfers between devices: 19.8 us -> 23.4 us  [shards(): lax.all_to_all(routed.reshape(slabs, ROWS, LANES), slab_axes, split_axis=...]
    ppermute x4 -> x3, starting transfers between devices: 10.3 us -> 6.83 us  [the longest x1 4.87 us: shards(): lax.ppermute(outer_rays, slab_axes, to_those((0, THIRD_STEP[1], THIRD_STE...]
    ppermute x4 -> x3, waiting for transfers between devices: 0.01 us -> 2.8 us  [the longest x1 2.34 us: shards(): lax.ppermute(outer_rays, slab_axes, to_those((0, THIRD_STEP[1], THIRD_STE...]
    pallas_call x4 -> x2, Pallas kernels: 6.29 us -> 6.06 us  [the longest x1 3.95 us: shards(): call(lambda *refs: migrate_kernel(*refs, scale=1.0 / math.sqrt(NT * count...]
  transfers between devices with their start and end apart: 5 -> 4, of which waited for: 1 -> 3; matrix products, arithmetic and copies ran while one was open for 1% -> 1% of each run, Pallas kernels for 6% -> 1%
where the time goes in v5:
time: 59.5 us; the launch traced here: 59.2 us
  starting transfers between devices  30.2 us (51%)
  blocking collectives  14.7 us (25%)
  Pallas kernels  7.34 us (12%)
  waiting for transfers between devices  4.89 us (8%)
  local copies, waits for them, and re-layouts  1.93 us (3%)
    all_to_all x1, starting transfers between devices, shards(): lax.all_to_all(routed.reshape(slabs, ROWS, LANES), slab_axes, split_axis=...  23.4 us
    all_to_all x1, blocking collectives, shards(): lax.all_to_all(merged, ('offset', 'chip', 'core'), split_axis=0, concat_a...  14.7 us
    ppermute x1, starting transfers between devices, shards(): lax.ppermute(outer_rays, slab_axes, to_those((0, THIRD_STEP[1], THIRD_STE...  4.87 us
    pallas_call x1, Pallas kernels, shards(): call(lambda *refs: migrate_kernel(*refs, scale=1.0 / math.sqrt(NT * count...  3.95 us
    ppermute x1, waiting for transfers between devices, shards(): lax.ppermute(outer_rays, slab_axes, to_those((0, THIRD_STEP[1], THIRD_STE...  2.34 us
    pallas_call x1, Pallas kernels, shards(): call(functools.partial(route_kernel, groups=groups), struct(slabs * ROWS,...  2.1 us
    all_to_all x1, waiting for transfers between devices, shards(): lax.all_to_all(routed.reshape(slabs, ROWS, LANES), slab_axes, split_axis=...  2.08 us
    unnamed x15, local copies, waits for them, and re-layouts  1.48 us
  transfers between devices with their start and end apart: 4, of which 3 were waited for; matrix products, arithmetic and copies ran while one was open for 1% of the time, Pallas kernels for 1%

profile of v5, /device:TPU:1, one launch (start us, length us, event | category | flops | bytes accessed | tf_op | source)
XLA Modules:
  0.0 59.2 jit_solution(2825406921218329278)
XLA Ops:
  0.0 0.0 copy-start
  0.0 2.1 %shard_map.119 = bf16[1024,128]{1,0:T(8,128)(2,1)} custom-call(s32[1,128]{1,0:T(1,128)} %bitcast.16, s32[1,128]{1,0:T(1,128)} %bins_ref.1, bf16[128,256]{1,0:T(8,128)(2,1)} %bitcast.13, bf16[256,128]{1,0:T(8,128)(2,1)} %constant.47.clone.high_ref, bf16[256,128]{1,0:T(8,128)(2,1)} %constant.48.clone.low_ref), custom_call_target="tpu_custom_call" | custom-call | bytes 1048576 | tf_op jit(solution)/shard_map/pallas_call | solution.py:334
  2.1 23.4 %all-to-all-start = ((bf16[64,16,128]{2,1,0:T(8,128)(2,1)}), bf16[64,16,128]{2,1,0:T(8,128)(2,1)S(1)}, u32[]{:S(2)}, u32[]{:S(2)}) async-start(bf16[64,16,128]{2,1,0:T(8,128)(2,1)} %bitcast.12), calls=%async_computation | async-start | bytes 524288 | tf_op jit(solution)/shard_map/all_to_all | solution.py:337
  25.5 0.0 copy-start.6
  25.5 0.7 %copy-done.6 = s32[64,7,2]{0,2,1:T(2,128)S(1)} copy-done((s32[64,7,2]{0,2,1:T(2,128)S(1)}, s32[64,7,2]{0,2,1:T(2,128)}, u32[]{:S(2)}) %copy-start.6) | copy-done | bytes 3608
  26.2 0.1 constant_dynamic-slice_fusion.1
  26.3 0.1 copy.13
  26.4 0.1 copy.15.foot_ref
  26.5 0.0 copy-done
  26.5 0.0 copy-start.4
  26.5 0.0 copy-start.5
  26.5 0.1 constant_dynamic-slice_fusion
  26.5 0.1 copy.16
  26.7 0.1 tile.13.lateral_ref
  26.8 0.6 %copy-done.4 = f32[1,1,7,16,256]{4,3,2,1,0:T(8,128)S(1)} copy-done((f32[1,1,7,16,256]{4,3,2,1,0:T(8,128)S(1)}, f32[1,1,7,16,256]{4,3,2,1,0:T(8,128)}, u32[]{:S(2)}) %copy-start.4) | copy-done | bytes 114712
  27.4 0.1 copy-done.5
  27.4 0.0 copy-start.1
  27.4 0.0 copy-start.2
  27.4 0.6 %shard_map.118 = (f32[3,40,256]{2,1,0:T(8,128)S(1)}, f32[40,256]{1,0:T(8,128)S(1)}, f32[4,40,256]{2,1,0:T(8,128)S(1)}, f32[8,256]{1,0:T(8,128)S(1)}) custom-call(s32[1]{0:T(128)} %bitcast.place_ref, s32[7,2]{1,0:T(8,128)S(1)} %copy.15.foot_ref, f32[7,128]{1,0:T(8,128)S(1)} %tile.13.lateral_ref, f32[7,16,256]{2,1,0:T(8,128)S(1)} %bitcast.10, ...), custom_call_target="tpu_custom_call" | custom-call | flops 268435456 | bytes 1048576 | tf_op jit(solution)/shard_map/pallas_call | solution.py:353
  28.1 0.7 %collective-permute-start = (f32[3,40,256]{2,1,0:T(8,128)S(1)}, f32[3,40,256]{2,1,0:T(8,128)S(1)}, u32[]{:S(2)}, u32[]{:S(2)}) collective-permute-start(f32[3,40,256]{2,1,0:T(8,128)S(1)} %get-tuple-element.11), channel_id=1, source_target_pairs={{5,2},{4,3},{3,4},{2,5},{9,6},{8,7},{7,8},{6,9},{13,10},{12,11},{1... | collective-permute-start | bytes 368648 | tf_op jit(solution)/shard_map/ppermute | solution.py:363
  28.7 4.9 %collective-permute-start.2 = (f32[40,256]{1,0:T(8,128)S(1)}, f32[40,256]{1,0:T(8,128)S(1)}, u32[]{:S(2)}, u32[]{:S(2)}) collective-permute-start(f32[40,256]{1,0:T(8,128)S(1)} %get-tuple-element.12), channel_id=1, source_target_pairs={{6,2},{1,5},{10,6},{5,9},{14,10},{9,13},{18,14},{13,17},{22,18},{1... | collective-permute-start | bytes 122888 | tf_op jit(solution)/shard_map/ppermute | solution.py:365
  33.6 1.3 %collective-permute-start.1 = (f32[40,256]{1,0:T(8,128)S(1)}, f32[40,256]{1,0:T(8,128)S(1)}, u32[]{:S(2)}, u32[]{:S(2)}) collective-permute-start(f32[40,256]{1,0:T(8,128)S(1)} %get-tuple-element.12), channel_id=1, source_target_pairs={{6,3},{1,4},{10,7},{5,8},{14,11},{9,12},{18,15},{13,16},{22,19},{1... | collective-permute-start | bytes 122888 | tf_op jit(solution)/shard_map/ppermute | solution.py:364
  34.9 2.3 %collective-permute-done.2.refs_8_ = f32[40,256]{1,0:T(8,128)S(1)} collective-permute-done((f32[40,256]{1,0:T(8,128)S(1)}, f32[40,256]{1,0:T(8,128)S(1)}, u32[]{:S(2)}, u32[]{:S(2)}) %collective-permute-start.2) | collective-permute-done | bytes 40992 | tf_op jit(solution)/shard_map/ppermute | solution.py:365
  37.3 0.5 collective-permute-done.1.refs_7_
  37.7 0.0 collective-permute-done.refs_6_
  37.7 2.1 %all-to-all-done = bf16[64,16,128]{2,1,0:T(8,128)(2,1)S(1)} async-done(((bf16[64,16,128]{2,1,0:T(8,128)(2,1)}), bf16[64,16,128]{2,1,0:T(8,128)(2,1)S(1)}, u32[]{:S(2)}, u32[]{:S(2)}) %all-to-all-start) | async-done | bytes 262176 | tf_op jit(solution)/shard_map/all_to_all | solution.py:337
  39.8 0.0 copy-done.1
  39.8 0.0 copy-done.2
  39.8 0.0 copy-done.3
  39.8 4.0 %shard_map.120 = bf16[32,32,128]{2,1,0:T(8,128)(2,1)S(1)} custom-call(f32[8,256]{1,0:T(8,128)S(1)} %get-tuple-element.9.refs_0_, bf16[1024,128]{1,0:T(8,128)(2,1)S(1)} %bitcast.9, bf16[128,1024]{1,0:T(8,128)(2,1)S(1)} %copy-done.1, f32[16,1024]{1,0:T(8,128)S(1)} %copy-done.3, f32[16,1024]{1,0:T(8,128)S(1)} %copy-done.2, ...), custom_call_target="tpu_custom_call" | custom-call | bytes 1048576 | tf_op jit(solution)/shard_map/pallas_call | solution.py:368
  43.8 14.7 %all_to_all.10.parts_ref = bf16[32,32,128]{2,1,0:T(8,128)(2,1)S(1)} all-to-all(bf16[32,32,128]{2,1,0:T(8,128)(2,1)S(1)} %shard_map.120), channel_id=1, replica_groups=mesh['offset'=8,'group'=16,'chip'=2,'core'=2] {'offset','chip','core'}, dimensions={0} | all-to-all | bytes 524288 | tf_op jit(solution)/shard_map/all_to_all | solution.py:378
  58.5 0.7 %shard_map.121 = f32[32,128]{1,0:T(8,128)} custom-call(bf16[32,32,128]{2,1,0:T(8,128)(2,1)S(1)} %all_to_all.10.parts_ref), custom_call_target="tpu_custom_call" | custom-call | bytes 1048576 | tf_op jit(solution)/shard_map/pallas_call | solution.py:381
  (2 shorter events, 0.0 us)
Async XLA Ops:
  0.0 26.5 %copy-start = (f32[1,64,7,16]{1,3,2,0:T(8,128)S(1)}, f32[1,64,7,16]{1,3,2,0:T(8,128)}, u32[]{:S(2)}) copy-start(f32[1,64,7,16]{1,3,2,0:T(8,128)} %param.17) | copy-start | bytes 86020
  2.1 37.7 %all-to-all-start = ((bf16[64,16,128]{2,1,0:T(8,128)(2,1)}), bf16[64,16,128]{2,1,0:T(8,128)(2,1)S(1)}, u32[]{:S(2)}, u32[]{:S(2)}) async-start(bf16[64,16,128]{2,1,0:T(8,128)(2,1)} %bitcast.12), calls=%async_computation | async-start | bytes 524288 | tf_op jit(solution)/shard_map/all_to_all | solution.py:337
  25.5 0.7 %copy-start.6 = (s32[64,7,2]{0,2,1:T(2,128)S(1)}, s32[64,7,2]{0,2,1:T(2,128)}, u32[]{:S(2)}) copy-start(s32[64,7,2]{0,2,1:T(2,128)} %param.18) | copy-start | bytes 10756
  26.5 0.9 %copy-start.4 = (f32[1,1,7,16,256]{4,3,2,1,0:T(8,128)S(1)}, f32[1,1,7,16,256]{4,3,2,1,0:T(8,128)}, u32[]{:S(2)}) copy-start(f32[1,1,7,16,256]{4,3,2,1,0:T(8,128)} %param.15) | copy-start | bytes 344068
  26.5 1.0 %copy-start.5 = (f32[1,1,7,16,256]{4,3,2,1,0:T(8,128)S(1)}, f32[1,1,7,16,256]{4,3,2,1,0:T(8,128)}, u32[]{:S(2)}) copy-start(f32[1,1,7,16,256]{4,3,2,1,0:T(8,128)} %param.16) | copy-start | bytes 344068
  27.4 12.4 %copy-start.1 = (bf16[128,1024]{1,0:T(8,128)(2,1)S(1)}, bf16[128,1024]{1,0:T(8,128)(2,1)}, u32[]{:S(2)}) copy-start(bf16[128,1024]{1,0:T(8,128)(2,1)} %constant.49.clone.refs_2_) | copy-start | bytes 786436
  27.4 12.4 %copy-start.2 = (f32[16,1024]{1,0:T(8,128)S(1)}, f32[16,1024]{1,0:T(8,128)}, u32[]{:S(2)}) copy-start(f32[16,1024]{1,0:T(8,128)} %constant.51.clone.refs_4_) | copy-start | bytes 196612
  27.4 12.4 %copy-start.3 = (f32[16,1024]{1,0:T(8,128)S(1)}, f32[16,1024]{1,0:T(8,128)}, u32[]{:S(2)}) copy-start(f32[16,1024]{1,0:T(8,128)} %constant.50.clone.refs_3_) | copy-start | bytes 196612
  28.1 9.7 %collective-permute-start = (f32[3,40,256]{2,1,0:T(8,128)S(1)}, f32[3,40,256]{2,1,0:T(8,128)S(1)}, u32[]{:S(2)}, u32[]{:S(2)}) collective-permute-start(f32[3,40,256]{2,1,0:T(8,128)S(1)} %get-tuple-element.11), channel_id=1, source_target_pairs={{5,2},{4,3},{3,4},{2,5},{9,6},{8,7},{7,8},{6,9},{13,10},{12,11},{1... | collective-permute-start | bytes 368648 | tf_op jit(solution)/shard_map/ppermute | solution.py:363
  28.7 8.5 %collective-permute-start.2 = (f32[40,256]{1,0:T(8,128)S(1)}, f32[40,256]{1,0:T(8,128)S(1)}, u32[]{:S(2)}, u32[]{:S(2)}) collective-permute-start(f32[40,256]{1,0:T(8,128)S(1)} %get-tuple-element.12), channel_id=1, source_target_pairs={{6,2},{1,5},{10,6},{5,9},{14,10},{9,13},{18,14},{13,17},{22,18},{1... | collective-permute-start | bytes 122888 | tf_op jit(solution)/shard_map/ppermute | solution.py:365
  33.6 4.1 %collective-permute-start.1 = (f32[40,256]{1,0:T(8,128)S(1)}, f32[40,256]{1,0:T(8,128)S(1)}, u32[]{:S(2)}, u32[]{:S(2)}) collective-permute-start(f32[40,256]{1,0:T(8,128)S(1)} %get-tuple-element.12), channel_id=1, source_target_pairs={{6,3},{1,4},{10,7},{5,8},{14,11},{9,12},{18,15},{13,16},{22,19},{1... | collective-permute-start | bytes 122888 | tf_op jit(solution)/shard_map/ppermute | solution.py:364

commit v6 on v5

--- a/solution.py
+++ b/solution.py
@@ -23,7 +23,8 @@
 HALF = (WIN - 1) // 2
 GROUPS = P_SIZE * NF // LANES
 GROUP = 4
-FIRST_SLAB = 16
+FIRST_SLAB = 52
+FIRST_OFFSET = 6
 SECOND_STEP = (-1, -3, 3, 1)
 THIRD_STEP = (-3, -4, 4, 3)
 THIRD_SLOT = (0, 3, 3, 0)
@@ -223,46 +224,62 @@
     return blocks
 
 
-def pack_kernel(
-    place_ref, foot_ref, lateral_ref, times_ref, amps_ref, seam_ref, outer_ref, near_ref, flag_ref
-):
+def pack_kernel(place_ref, times_ref, amps_ref, second_ref, third_ref, near_ref):
     place = place_ref[0]
 
     def pack(w, ref):
         ref[0:P_SIZE] = times_ref[w]
-        ref[P_SIZE : 2 * P_SIZE] = amps_ref[w]
-        sub = iota((8, LANES), 0)
+        ref[P_SIZE:] = amps_ref[w]
+
+    base = jnp.where(place < GROUP // 2, 0, WIN - place)
+    for i in range(HALF):
+        pack(jnp.minimum(base + i, WIN - 1), second_ref.at[i])
+    pack(jnp.where(place == 1, WIN - 1, 0), third_ref)
+    for i in range(GROUP):
+        pack(HALF - place + i, near_ref.at[i])
+
+
+def tails_kernel(place_ref, foot_ref, lateral_ref, tail_ref, flag_ref):
+    place = place_ref[0]
+    first_chip = place < GROUP // 2
+    base = jnp.where(first_chip, HALF + 1 + place, 0)
+    windows = [HALF - place + i for i in range(GROUP)]
+    windows += [WIN + jnp.minimum(base + i, WIN - 1) for i in range(HALF)]
+    windows += [2 * WIN + jnp.where(first_chip, WIN - 1, 0)]
+    sub = iota((8, LANES), 0)
+    for i, w in enumerate(windows):
         first, end = foot_ref[w, 0].astype(f32), foot_ref[w, 1].astype(f32)
         lateral = jnp.broadcast_to(lateral_ref[pl.ds(w, 1), :], (8, LANES))
-        tail = jnp.where(sub == 0, lateral, jnp.where(sub == 1, first, end))
-        ref[2 * P_SIZE :] = jnp.concatenate([tail] * (ref.shape[1] // LANES), axis=1)
-
-    base = jnp.where(place < GROUP // 2, 0, WIN - place)
-    for i in range(HALF):
-        pack(jnp.minimum(base + i, WIN - 1), seam_ref.at[i])
-    pack(jnp.where(place == 1, WIN - 1, 0), outer_ref)
-    for i in range(GROUP):
-        pack(HALF - place + i, near_ref.at[i])
+        tail_ref[i] = jnp.where(sub == 0, lateral, jnp.where(sub == 1, first, end))
     flag_ref[...] = jnp.full(flag_ref.shape, place.astype(f32))
 
 
-def unpack(rays):
-    tail = rays[2 * P_SIZE :, :LANES]
-    return rays[:P_SIZE], rays[P_SIZE : 2 * P_SIZE], tail[0:1], tail[1:2], tail[2:3]
-
-
-def migrate_kernel(
-    flag_ref, arrived_ref, spread_ref, cos_ref, sin_ref, near_ref, second_ref, third_0_ref,
-    third_1_ref, out_ref, u_ref, *, scale,
+def unpack(rays, tail):
+    return rays[:P_SIZE], rays[P_SIZE:], tail[0:1], tail[1:2], tail[2:3]
+
+
+def near_kernel(
+    arrived_ref, spread_ref, cos_ref, sin_ref, rays_ref, tail_ref, near_ref, beam_ref, u_ref,
+    *, scale,
 ):
     own, second, third = slant_stack(
         arrived_ref[...], spread_ref[...], cos_ref[...], sin_ref[...], scale
     )
-    windows = [unpack(near_ref[i]) + own for i in range(GROUP)]
-    windows += [unpack(second_ref[i]) + second for i in range(HALF)]
-    windows += [unpack(third_0_ref[...] + third_1_ref[...]) + third]
-    blocks = contributions(windows, u_ref)
-    near, (a, b, c, d) = blocks[:GROUP], blocks[GROUP:]
+    for i, beam in enumerate(second + third):
+        beam_ref[i : i + 1] = beam
+    windows = [unpack(rays_ref[i], tail_ref[i]) + own for i in range(GROUP)]
+    for i, block in enumerate(contributions(windows, u_ref)):
+        near_ref[i] = block
+
+
+def far_kernel(
+    flag_ref, tail_ref, near_ref, beam_ref, second_ref, third_0_ref, third_1_ref, out_ref, u_ref,
+    *, parts,
+):
+    second, third = (beam_ref[0:1], beam_ref[1:2]), (beam_ref[2:3], beam_ref[3:4])
+    windows = [unpack(second_ref[i], tail_ref[GROUP + i]) + second for i in range(HALF)]
+    windows += [unpack(third_0_ref[...] + third_1_ref[...], tail_ref[GROUP + HALF]) + third]
+    a, b, c, d = contributions(windows, u_ref)
     rows = out_ref.shape[1]
     place = flag_ref[0:1, :]
     is_0, is_2, is_3 = place == 0.0, place == 2.0, place == 3.0
@@ -272,15 +289,15 @@
         return jnp.where(condition, block, 0.0)
 
     totals = (
-        near[0] + when(first, a + d),
-        near[1] + when(first, b) + when(is_3, a),
-        near[2] + when(is_0, c) + when(is_3, b) + when(is_2, a),
-        near[3] + when(is_3, c) + when(is_2, b) + when(~first, d),
+        near_ref[0] + when(first, a + d),
+        near_ref[1] + when(first, b) + when(is_3, a),
+        near_ref[2] + when(is_0, c) + when(is_3, b) + when(is_2, a),
+        near_ref[3] + when(is_3, c) + when(is_2, b) + when(~first, d),
     )
     for t, total in enumerate(totals):
         total = total.T.astype(bf16)
-        for o in range(out_ref.shape[0] // GROUP):
-            out_ref[o * GROUP + t] = total[o * rows : (o + 1) * rows]
+        for i, o in enumerate(parts):
+            out_ref[i * GROUP + t] = total[o * rows : (o + 1) * rows]
 
 
 def total_kernel(parts_ref, out_ref):
@@ -339,44 +356,67 @@
         axis_index_groups=[order], tiled=True,
     ).reshape(slabs * ROWS, LANES)
 
-    lateral = lax.dynamic_index_in_dim(beam_lateral[0], my_slab, 0, keepdims=False)
-    lateral = jnp.tile(lateral, (1, LANES // P_SIZE))
-    foot = lax.dynamic_index_in_dim(footprint, my_slab, 0, keepdims=False)
-    u_rows = 2 * P_SIZE * NF
     place = (my_slab % GROUP).astype(jnp.int32).reshape(1)
 
     def to_those(steps):
         pairs = [(i + steps[i % GROUP], i) for i in range(slabs) if steps[i % GROUP]]
         return [(i, j) for i, j in pairs if 0 <= i < slabs]
 
-    ray_rows = 2 * P_SIZE + 8
-    seam_rays, outer_rays, near_rays, flags = call(
+    ray_rows = 2 * P_SIZE
+    u_rows = 2 * P_SIZE * NF
+    second_rays, third_rays, near_rays = call(
         pack_kernel,
         (
             struct32(HALF, ray_rows, depth), struct32(ray_rows, depth),
-            struct32(GROUP, ray_rows, depth), struct32(8, depth),
+            struct32(GROUP, ray_rows, depth),
         ),
-        [smem()] * 2 + [vmem()] * 3,
+        [smem()] + [vmem()] * 2,
         8,
         flops=1 << 28,
-    )(place, foot, lateral, ray_times[0, 0], ray_amps[0, 0])
-    second_rays = lax.ppermute(seam_rays, slab_axes, to_those(SECOND_STEP))
-    third_0 = lax.ppermute(outer_rays, slab_axes, to_those((THIRD_STEP[0], 0, 0, THIRD_STEP[3])))
-    third_1 = lax.ppermute(outer_rays, slab_axes, to_those((0, THIRD_STEP[1], THIRD_STEP[2], 0)))
+    )(place, ray_times[0, 0], ray_amps[0, 0])
+    second_rays = lax.ppermute(second_rays, slab_axes, to_those(SECOND_STEP))
+    third_0 = lax.ppermute(third_rays, slab_axes, to_those((THIRD_STEP[0], 0, 0, THIRD_STEP[3])))
+    third_1 = lax.ppermute(third_rays, slab_axes, to_those((0, THIRD_STEP[1], THIRD_STEP[2], 0)))
+
+    steps = [jnp.int32(0)] + [
+        jnp.asarray(step, jnp.int32)[my_slab % GROUP] for step in (SECOND_STEP, THIRD_STEP)
+    ]
+    centres = [jnp.clip(my_slab + step, 0, slabs - 1) for step in steps]
+    lateral = jnp.concatenate(
+        [lax.dynamic_index_in_dim(beam_lateral[0], c, 0, keepdims=False) for c in centres]
+    )
+    foot = jnp.concatenate(
+        [lax.dynamic_index_in_dim(footprint, c, 0, keepdims=False) for c in centres]
+    )
+    tails, flags = call(
+        tails_kernel,
+        (struct32(GROUP + HALF + 1, 8, LANES), struct32(8, depth)),
+        [smem()] * 2 + [vmem()],
+        8,
+        flops=1 << 28,
+    )(place, foot, jnp.tile(lateral, (1, LANES // P_SIZE)))
 
     cosine, sine, spread = slant_tables()
+    near, beams = call(
+        functools.partial(near_kernel, scale=1.0 / math.sqrt(NT * count)),
+        (struct32(GROUP, XW, depth), struct32(4, NF * P_SIZE)),
+        [vmem()] * 6,
+        24,
+        [pltpu.VMEM((GROUP, u_rows, depth), bf16)],
+    )(
+        arrived, jnp.asarray(spread), jnp.asarray(cosine), jnp.asarray(sine), near_rays, tails
+    )
+    parts = [(FIRST_OFFSET + i) % offsets for i in range(offsets)]
     merged = call(
-        lambda *refs: migrate_kernel(*refs, scale=1.0 / math.sqrt(NT * count)),
+        functools.partial(far_kernel, parts=parts),
         struct(GROUP * offsets, part, XW),
-        [vmem()] * 9,
-        32,
-        [pltpu.VMEM((GROUP + HALF + 1, u_rows, depth), bf16)],
-    )(
-        flags, arrived, jnp.asarray(spread), jnp.asarray(cosine), jnp.asarray(sine),
-        near_rays, second_rays, third_0, third_1,
-    )
+        [vmem()] * 7,
+        24,
+        [pltpu.VMEM((HALF + 1, u_rows, depth), bf16)],
+    )(flags, tails, near, beams, second_rays, third_0, third_1)
     parts = lax.all_to_all(
-        merged, ("offset", "chip", "core"), split_axis=0, concat_axis=0, tiled=True
+        merged, ("offset", "chip", "core"), split_axis=0, concat_axis=0,
+        axis_index_groups=[[o * GROUP + t for o in parts for t in range(GROUP)]], tiled=True,
     )
     return call(total_kernel, struct32(part, XW), [vmem()], 4)(parts)
 

time: 59.5 us -> 55 us (0.924)
  blocking collectives: 14.7 us -> 11.3 us
  waiting for transfers between devices: 4.89 us -> 3.08 us
  starting transfers between devices: 30.2 us -> 28.7 us
  between operations: 0.08 us -> 1.48 us
    all_to_all x1, blocking collectives: 14.7 us -> 11.3 us  [shards(): lax.all_to_all(merged, ('offset', 'chip', 'core'), split_axis=0, concat_a...]
    ppermute x3, waiting for transfers between devices: 2.8 us -> 0.01 us  [the longest x1 0.01 us: shards(): lax.ppermute(third_rays, slab_axes, to_those((THIRD_STEP[0], 0, 0, THIRD_...]
    all_to_all x1, starting transfers between devices: 23.4 us -> 21.5 us  [shards(): lax.all_to_all(routed.reshape(slabs, ROWS, LANES), slab_axes, split_axis=...]
    dynamic_slice x3 -> x7, local copies, waits for them, and re-layouts: 0.25 us -> 1.74 us  [the longest x2 1.24 us: shards(): jnp.asarray(step, jnp.int32)[my_slab % GROUP]]
    unnamed x15 -> x21, local copies, waits for them, and re-layouts: 1.48 us -> 0.4 us
    all_to_all x1, waiting for transfers between devices: 2.08 us -> 3.07 us  [shards(): lax.all_to_all(routed.reshape(slabs, ROWS, LANES), slab_axes, split_axis=...]
    pallas_call x1 -> x3, Pallas kernels: 3.95 us -> 4.85 us  [the longest x1 2.28 us: shards(): call(functools.partial(near_kernel, scale=1.0 / math.sqrt(NT * count)), (...]
    pallas_call x1, Pallas kernels: 0.63 us -> 0.03 us  [shards(): call(pack_kernel, (struct32(HALF, ray_rows, depth), struct32(ray_rows, de...]
  transfers between devices with their start and end apart: 4 -> 4, of which waited for: 3 -> 1; matrix products, arithmetic and copies ran while one was open for 1% -> 4% of each run, Pallas kernels for 1% -> 6%
where the time goes in v6:
time: 55 us; the launch traced here: 54.6 us
  starting transfers between devices  28.7 us (52%)
  blocking collectives  11.3 us (21%)
  Pallas kernels  7.63 us (14%)
  waiting for transfers between devices  3.08 us (6%)
  local copies, waits for them, and re-layouts  2.33 us (4%)
  between operations  1.48 us (3%)
    all_to_all x1, starting transfers between devices, shards(): lax.all_to_all(routed.reshape(slabs, ROWS, LANES), slab_axes, split_axis=...  21.5 us
    all_to_all x1, blocking collectives, shards(): lax.all_to_all(merged, ('offset', 'chip', 'core'), split_axis=0, concat_a...  11.3 us
    ppermute x1, starting transfers between devices, shards(): lax.ppermute(third_rays, slab_axes, to_those((THIRD_STEP[0], 0, 0, THIRD_...  4.37 us
    all_to_all x1, waiting for transfers between devices, shards(): lax.all_to_all(routed.reshape(slabs, ROWS, LANES), slab_axes, split_axis=...  3.07 us
    pallas_call x1, Pallas kernels, shards(): call(functools.partial(near_kernel, scale=1.0 / math.sqrt(NT * count)), (...  2.28 us
    ppermute x1, starting transfers between devices, shards(): lax.ppermute(third_rays, slab_axes, to_those((0, THIRD_STEP[1], THIRD_STE...  2.2 us
    pallas_call x1, Pallas kernels, shards(): call(functools.partial(route_kernel, groups=groups), struct(slabs * ROWS,...  2.1 us
    pallas_call x1, Pallas kernels, shards(): call(functools.partial(far_kernel, parts=parts), struct(GROUP * offsets,...  1.81 us
  transfers between devices with their start and end apart: 4, of which 1 were waited for; matrix products, arithmetic and copies ran while one was open for 4% of the time, Pallas kernels for 6%

profile of v6, /device:TPU:1, one launch (start us, length us, event | category | flops | bytes accessed | tf_op | source)
XLA Modules:
  0.0 54.6 jit_solution(13672137508926089455)
XLA Ops:
  0.0 2.1 %shard_map.137 = bf16[1024,128]{1,0:T(8,128)(2,1)} custom-call(s32[1,128]{1,0:T(1,128)} %bitcast.26, s32[1,128]{1,0:T(1,128)} %bins_ref.1, bf16[128,256]{1,0:T(8,128)(2,1)} %bitcast.19, bf16[256,128]{1,0:T(8,128)(2,1)} %constant.70.clone.high_ref, bf16[256,128]{1,0:T(8,128)(2,1)} %constant.71.clone.low_ref), custom_call_target="tpu_custom_call" | custom-call | bytes 1048576 | tf_op jit(solution)/shard_map/pallas_call | solution.py:351
  2.1 21.5 %all-to-all-start = ((bf16[64,16,128]{2,1,0:T(8,128)(2,1)}), bf16[64,16,128]{2,1,0:T(8,128)(2,1)S(1)}, u32[]{:S(2)}, u32[]{:S(2)}) async-start(bf16[64,16,128]{2,1,0:T(8,128)(2,1)} %bitcast.18), calls=%async_computation | async-start | bytes 524288 | tf_op jit(solution)/shard_map/all_to_all | solution.py:354
  23.6 0.0 copy-start.8
  23.7 0.0 copy-start.7
  23.7 0.0 copy-start.6
  23.7 0.0 copy-start.5
  23.7 4.4 %collective-permute-start.1 = (f32[32,256]{1,0:T(8,128)S(1)}, f32[32,256]{1,0:T(8,128)S(1)}, u32[]{:S(2)}, u32[]{:S(2)}) collective-permute-start(f32[32,256]{1,0:T(8,128)S(1)} %get-tuple-element.18), channel_id=1, source_target_pairs={{6,3},{1,4},{10,7},{5,8},{14,11},{9,12},{18,15},{13,16},{22,19},{1... | collective-permute-start | bytes 98312 | tf_op jit(solution)/shard_map/ppermute | solution.py:378
  28.1 2.2 %collective-permute-start.2 = (f32[32,256]{1,0:T(8,128)S(1)}, f32[32,256]{1,0:T(8,128)S(1)}, u32[]{:S(2)}, u32[]{:S(2)}) collective-permute-start(f32[32,256]{1,0:T(8,128)S(1)} %get-tuple-element.18), channel_id=1, source_target_pairs={{6,2},{1,5},{10,6},{5,9},{14,10},{9,13},{18,14},{13,17},{22,18},{1... | collective-permute-start | bytes 98312 | tf_op jit(solution)/shard_map/ppermute | solution.py:379
  30.3 0.7 %collective-permute-start = (f32[3,32,256]{2,1,0:T(8,128)S(1)}, f32[3,32,256]{2,1,0:T(8,128)S(1)}, u32[]{:S(2)}, u32[]{:S(2)}) collective-permute-start(f32[3,32,256]{2,1,0:T(8,128)S(1)} %get-tuple-element.17), channel_id=1, source_target_pairs={{5,2},{4,3},{3,4},{2,5},{9,6},{8,7},{7,8},{6,9},{13,10},{12,11},{1... | collective-permute-start | bytes 294920 | tf_op jit(solution)/shard_map/ppermute | solution.py:377
  31.0 0.6 %dynamic_slice.29 = s32[1]{0:T(128)} dynamic-slice(s32[4]{0:T(128)S(1)} %copy-done.8, s32[]{:T(128)S(6)} %select_n.24), dynamic_slice_sizes={1} | dynamic-slice | bytes 12 | tf_op jit(solution)/shard_map/dynamic_slice | solution.py:382
  32.2 0.6 %dynamic_slice.27 = s32[1]{0:T(128)} dynamic-slice(s32[4]{0:T(128)S(1)} %copy-done.7, s32[]{:T(128)S(6)} %select_n.24), dynamic_slice_sizes={1} | dynamic-slice | bytes 12 | tf_op jit(solution)/shard_map/dynamic_slice | solution.py:382
  33.5 0.1 constant_dynamic-slice_fusion.5
  33.6 0.1 copy.35
  33.7 0.1 copy.34
  33.8 0.1 copy.33
  33.9 0.1 constant_dynamic-slice_fusion.2
  34.0 0.1 copy.42
  34.1 0.1 copy.41
  34.2 0.1 copy.40
  34.4 0.1 pad_add_fusion
  34.5 0.1 copy.39.foot_ref
  34.6 0.1 tile.10.lateral_ref
  34.7 0.0 copy-start
  34.7 0.0 copy-start.1
  34.7 0.0 copy-start.2
  34.7 0.8 %shard_map.136 = (f32[8,8,128]{2,1,0:T(8,128)S(1)}, f32[8,256]{1,0:T(8,128)S(1)}) custom-call(s32[1]{0:T(128)} %bitcast.place_ref, s32[21,2]{1,0:T(8,128)S(1)} %copy.39.foot_ref, f32[21,128]{1,0:T(8,128)S(1)} %tile.10.lateral_ref), custom_call_target="tpu_custom_call" | custom-call | flops 268435456 | bytes 1048576 | tf_op jit(solution)/shard_map/pallas_call | solution.py:391
  35.5 3.1 %all-to-all-done = bf16[64,16,128]{2,1,0:T(8,128)(2,1)S(1)} async-done(((bf16[64,16,128]{2,1,0:T(8,128)(2,1)}), bf16[64,16,128]{2,1,0:T(8,128)(2,1)S(1)}, u32[]{:S(2)}, u32[]{:S(2)}) %all-to-all-start) | async-done | bytes 262176 | tf_op jit(solution)/shard_map/all_to_all | solution.py:354
  38.6 2.3 %shard_map.139 = (f32[4,128,256]{2,1,0:T(8,128)S(1)}, f32[4,1024]{1,0:T(4,128)S(1)}) custom-call(bf16[1024,128]{1,0:T(8,128)(2,1)S(1)} %bitcast.15, bf16[128,1024]{1,0:T(8,128)(2,1)S(1)} %copy-done, f32[16,1024]{1,0:T(8,128)S(1)} %copy-done.1, f32[16,1024]{1,0:T(8,128)S(1)} %copy-done.2, f32[4,32,256]{2,1,0:T(8,128)S(1)} %get-tuple-element.14.rays_ref, ...), custom_call_target="tpu_custom_call" | custom-call | bytes 1048576 | tf_op jit(solution)/shard_map/pallas_call | solution.py:400
  40.8 0.0 collective-permute-done.1.third_0_ref
  40.9 1.8 %shard_map.140 = bf16[32,32,128]{2,1,0:T(8,128)(2,1)S(1)} custom-call(f32[8,256]{1,0:T(8,128)S(1)} %get-tuple-element.12.flag_ref, f32[8,8,128]{2,1,0:T(8,128)S(1)} %get-tuple-element.13.tail_ref, f32[4,128,256]{2,1,0:T(8,128)S(1)} %get-tuple-element.15.near_ref, f32[4,1024]{1,0:T(4,128)S(1)} %get-tuple-element.16.beam_ref, ...), custom_call_target="tpu_custom_call" | custom-call | bytes 1048576 | tf_op jit(solution)/shard_map/pallas_call | solution.py:410
  42.7 11.3 %all_to_all.10.parts_ref = bf16[32,32,128]{2,1,0:T(8,128)(2,1)S(1)} all-to-all(bf16[32,32,128]{2,1,0:T(8,128)(2,1)S(1)} %shard_map.140), channel_id=1, replica_groups={{384,385,386,387,448,449,450,451,0,1,2,3,64,65,66,67,128,129,130,131,19..., dimensions={0} | all-to-all | bytes 524288 | tf_op jit(solution)/shard_map/all_to_all | solution.py:417
  54.0 0.7 %shard_map.141 = f32[32,128]{1,0:T(8,128)} custom-call(bf16[32,32,128]{2,1,0:T(8,128)(2,1)S(1)} %all_to_all.10.parts_ref), custom_call_target="tpu_custom_call" | custom-call | bytes 1048576 | tf_op jit(solution)/shard_map/pallas_call | solution.py:421
  (16 shorter events, 0.1 us)
Async XLA Ops:
  2.1 21.5 %copy-start.3 = (f32[1,1,7,16,256]{4,3,2,1,0:T(8,128)S(1)}, f32[1,1,7,16,256]{4,3,2,1,0:T(8,128)}, u32[]{:S(2)}) copy-start(f32[1,1,7,16,256]{4,3,2,1,0:T(8,128)} %param.17) | copy-start | bytes 344068
  2.1 21.5 %copy-start.4 = (f32[1,1,7,16,256]{4,3,2,1,0:T(8,128)S(1)}, f32[1,1,7,16,256]{4,3,2,1,0:T(8,128)}, u32[]{:S(2)}) copy-start(f32[1,1,7,16,256]{4,3,2,1,0:T(8,128)} %param.18) | copy-start | bytes 344068
  2.1 36.4 %all-to-all-start = ((bf16[64,16,128]{2,1,0:T(8,128)(2,1)}), bf16[64,16,128]{2,1,0:T(8,128)(2,1)S(1)}, u32[]{:S(2)}, u32[]{:S(2)}) async-start(bf16[64,16,128]{2,1,0:T(8,128)(2,1)} %bitcast.18), calls=%async_computation | async-start | bytes 524288 | tf_op jit(solution)/shard_map/all_to_all | solution.py:354
  23.6 7.4 %copy-start.8 = (s32[4]{0:T(128)S(1)}, s32[4]{0:T(128)}, u32[]{:S(2)}) copy-start(s32[4]{0:T(128)} %constant.73.clone) | copy-start | bytes 52
  23.7 8.6 %copy-start.7 = (s32[4]{0:T(128)S(1)}, s32[4]{0:T(128)}, u32[]{:S(2)}) copy-start(s32[4]{0:T(128)} %constant.72.clone) | copy-start | bytes 52
  23.7 9.8 %copy-start.6 = (s32[64,7,2]{0,2,1:T(2,128)S(1)}, s32[64,7,2]{0,2,1:T(2,128)}, u32[]{:S(2)}) copy-start(s32[64,7,2]{0,2,1:T(2,128)} %param.20) | copy-start | bytes 10756
  23.7 10.2 %copy-start.5 = (f32[1,64,7,16]{1,3,2,0:T(8,128)S(1)}, f32[1,64,7,16]{1,3,2,0:T(8,128)}, u32[]{:S(2)}) copy-start(f32[1,64,7,16]{1,3,2,0:T(8,128)} %param.19) | copy-start | bytes 86020
  23.7 17.1 %collective-permute-start.1 = (f32[32,256]{1,0:T(8,128)S(1)}, f32[32,256]{1,0:T(8,128)S(1)}, u32[]{:S(2)}, u32[]{:S(2)}) collective-permute-start(f32[32,256]{1,0:T(8,128)S(1)} %get-tuple-element.18), channel_id=1, source_target_pairs={{6,3},{1,4},{10,7},{5,8},{14,11},{9,12},{18,15},{13,16},{22,19},{1... | collective-permute-start | bytes 98312 | tf_op jit(solution)/shard_map/ppermute | solution.py:378
  28.1 12.8 %collective-permute-start.2 = (f32[32,256]{1,0:T(8,128)S(1)}, f32[32,256]{1,0:T(8,128)S(1)}, u32[]{:S(2)}, u32[]{:S(2)}) collective-permute-start(f32[32,256]{1,0:T(8,128)S(1)} %get-tuple-element.18), channel_id=1, source_target_pairs={{6,2},{1,5},{10,6},{5,9},{14,10},{9,13},{18,14},{13,17},{22,18},{1... | collective-permute-start | bytes 98312 | tf_op jit(solution)/shard_map/ppermute | solution.py:379
  30.3 10.6 %collective-permute-start = (f32[3,32,256]{2,1,0:T(8,128)S(1)}, f32[3,32,256]{2,1,0:T(8,128)S(1)}, u32[]{:S(2)}, u32[]{:S(2)}) collective-permute-start(f32[3,32,256]{2,1,0:T(8,128)S(1)} %get-tuple-element.17), channel_id=1, source_target_pairs={{5,2},{4,3},{3,4},{2,5},{9,6},{8,7},{7,8},{6,9},{13,10},{12,11},{1... | collective-permute-start | bytes 294920 | tf_op jit(solution)/shard_map/ppermute | solution.py:377
  34.7 3.9 %copy-start = (bf16[128,1024]{1,0:T(8,128)(2,1)S(1)}, bf16[128,1024]{1,0:T(8,128)(2,1)}, u32[]{:S(2)}) copy-start(bf16[128,1024]{1,0:T(8,128)(2,1)} %constant.74.clone.spread_ref) | copy-start | bytes 786436
  34.7 3.9 %copy-start.1 = (f32[16,1024]{1,0:T(8,128)S(1)}, f32[16,1024]{1,0:T(8,128)}, u32[]{:S(2)}) copy-start(f32[16,1024]{1,0:T(8,128)} %constant.75.clone.cos_ref) | copy-start | bytes 196612
  34.7 3.9 %copy-start.2 = (f32[16,1024]{1,0:T(8,128)S(1)}, f32[16,1024]{1,0:T(8,128)}, u32[]{:S(2)}) copy-start(f32[16,1024]{1,0:T(8,128)} %constant.76.clone.sin_ref) | copy-start | bytes 196612

commit v7 on v6

--- a/solution.py
+++ b/solution.py
@@ -24,6 +24,7 @@
 GROUPS = P_SIZE * NF // LANES
 GROUP = 4
 FIRST_SLAB = 52
+READY = 2
 FIRST_OFFSET = 6
 SECOND_STEP = (-1, -3, 3, 1)
 THIRD_STEP = (-3, -4, 4, 3)
@@ -207,21 +208,31 @@
         gauss = gauss * ratio
 
 
-def contributions(windows, u_ref):
+def contributions(windows, u_ref, ready_ref=None):
     blocks = []
-    for _ in u_groups(u_ref.at[0], *windows[0][:2]):
-        pass
+    ready = 0 if ready_ref is None else ready_ref.shape[0]
+    later = [
+        u_groups(u_ref.at[i - ready], *windows[i][:2]) for i in range(ready, len(windows))
+    ]
+    if not ready:
+        for _ in later.pop(0):
+            pass
     for i, window in enumerate(windows):
-        following = iter(())
-        if i + 1 < len(windows):
-            following = u_groups(u_ref.at[i + 1], *windows[i + 1][:2])
+        following = later.pop(0) if later else iter(())
+        held = ready_ref.at[i] if i < ready else u_ref.at[i - ready]
         total = None
         for group, v in enumerate(v_groups(*window[2:])):
-            part = dot(v, u_ref[i, pl.ds(group * 2 * LANES, 2 * LANES), :])
+            part = dot(v, held[pl.ds(group * 2 * LANES, 2 * LANES), :])
             total = part if total is None else total + part
             next(following, None)
         blocks.append(total)
     return blocks
+
+
+def u_kernel(rays_ref, out_ref):
+    for i in range(out_ref.shape[0]):
+        for _ in u_groups(out_ref.at[i], rays_ref[i, :P_SIZE], rays_ref[i, P_SIZE:]):
+            pass
 
 
 def pack_kernel(place_ref, times_ref, amps_ref, second_ref, third_ref, near_ref):
@@ -239,18 +250,26 @@
         pack(HALF - place + i, near_ref.at[i])
 
 
-def tails_kernel(place_ref, foot_ref, lateral_ref, tail_ref, flag_ref):
-    place = place_ref[0]
+def tails_kernel(slab_ref, foot_ref, lateral_ref, tail_ref, flag_ref):
+    slab = slab_ref[0]
+    place = slab % GROUP
     first_chip = place < GROUP // 2
     base = jnp.where(first_chip, HALF + 1 + place, 0)
-    windows = [HALF - place + i for i in range(GROUP)]
-    windows += [WIN + jnp.minimum(base + i, WIN - 1) for i in range(HALF)]
-    windows += [2 * WIN + jnp.where(first_chip, WIN - 1, 0)]
+    second = slab + by_place(place, SECOND_STEP)
+    third = slab + by_place(place, THIRD_STEP)
+    windows = [(slab, HALF - place + i) for i in range(GROUP)]
+    windows += [(second, jnp.minimum(base + i, WIN - 1)) for i in range(HALF)]
+    windows += [(third, jnp.where(first_chip, WIN - 1, 0))]
+    slabs = lateral_ref.shape[2]
+    spread = iota((P_SIZE, LANES), 1) % P_SIZE == iota((P_SIZE, LANES), 0)
     sub = iota((8, LANES), 0)
-    for i, w in enumerate(windows):
-        first, end = foot_ref[w, 0].astype(f32), foot_ref[w, 1].astype(f32)
-        lateral = jnp.broadcast_to(lateral_ref[pl.ds(w, 1), :], (8, LANES))
-        tail_ref[i] = jnp.where(sub == 0, lateral, jnp.where(sub == 1, first, end))
+    for i, (centre, w) in enumerate(windows):
+        lateral = jnp.where(iota((P_SIZE, slabs), 1) == centre, lateral_ref[w], 0.0)
+        lateral = jnp.sum(lateral, axis=1, keepdims=True)
+        lateral = jnp.sum(jnp.where(spread, lateral, 0.0), axis=0, keepdims=True)
+        foot = jnp.where(iota((2, slabs), 1) == centre, foot_ref[w].astype(f32), 0.0)
+        foot = jnp.sum(foot, axis=1, keepdims=True)
+        tail_ref[i] = jnp.where(sub == 0, lateral, jnp.where(sub == 1, foot[0:1], foot[1:2]))
     flag_ref[...] = jnp.full(flag_ref.shape, place.astype(f32))
 
 
@@ -259,7 +278,7 @@
 
 
 def near_kernel(
-    arrived_ref, spread_ref, cos_ref, sin_ref, rays_ref, tail_ref, near_ref, beam_ref, u_ref,
+    arrived_ref, spread_ref, cos_ref, sin_ref, rays_ref, tail_ref, ready_ref, near_ref, beam_ref, u_ref,
     *, scale,
 ):
     own, second, third = slant_stack(
@@ -268,7 +287,7 @@
     for i, beam in enumerate(second + third):
         beam_ref[i : i + 1] = beam
     windows = [unpack(rays_ref[i], tail_ref[i]) + own for i in range(GROUP)]
-    for i, block in enumerate(contributions(windows, u_ref)):
+    for i, block in enumerate(contributions(windows, u_ref, ready_ref)):
         near_ref[i] = block
 
 
@@ -378,33 +397,29 @@
     third_0 = lax.ppermute(third_rays, slab_axes, to_those((THIRD_STEP[0], 0, 0, THIRD_STEP[3])))
     third_1 = lax.ppermute(third_rays, slab_axes, to_those((0, THIRD_STEP[1], THIRD_STEP[2], 0)))
 
-    steps = [jnp.int32(0)] + [
-        jnp.asarray(step, jnp.int32)[my_slab % GROUP] for step in (SECOND_STEP, THIRD_STEP)
-    ]
-    centres = [jnp.clip(my_slab + step, 0, slabs - 1) for step in steps]
-    lateral = jnp.concatenate(
-        [lax.dynamic_index_in_dim(beam_lateral[0], c, 0, keepdims=False) for c in centres]
-    )
-    foot = jnp.concatenate(
-        [lax.dynamic_index_in_dim(footprint, c, 0, keepdims=False) for c in centres]
-    )
     tails, flags = call(
         tails_kernel,
         (struct32(GROUP + HALF + 1, 8, LANES), struct32(8, depth)),
-        [smem()] * 2 + [vmem()],
+        [smem()] + [vmem()] * 2,
         8,
         flops=1 << 28,
-    )(place, foot, jnp.tile(lateral, (1, LANES // P_SIZE)))
+    )(
+        my_slab.astype(jnp.int32).reshape(1),
+        footprint.transpose(1, 2, 0),
+        beam_lateral[0].transpose(1, 2, 0),
+    )
 
     cosine, sine, spread = slant_tables()
+    ready = call(u_kernel, struct(READY, u_rows, depth), [vmem()], 8, flops=1 << 28)(near_rays)
     near, beams = call(
         functools.partial(near_kernel, scale=1.0 / math.sqrt(NT * count)),
         (struct32(GROUP, XW, depth), struct32(4, NF * P_SIZE)),
-        [vmem()] * 6,
+        [vmem()] * 7,
         24,
-        [pltpu.VMEM((GROUP, u_rows, depth), bf16)],
+        [pltpu.VMEM((GROUP - READY, u_rows, depth), bf16)],
     )(
-        arrived, jnp.asarray(spread), jnp.asarray(cosine), jnp.asarray(sine), near_rays, tails
+        arrived, jnp.asarray(spread), jnp.asarray(cosine), jnp.asarray(sine), near_rays, tails,
+        ready,
     )
     parts = [(FIRST_OFFSET + i) % offsets for i in range(offsets)]
     merged = call(

time: 55 us -> 54.9 us (level)
  starting transfers between devices: 28.7 us -> 32.3 us
  waiting for transfers between devices: 3.08 us -> 1.29 us
  between operations: 1.48 us -> 0.14 us
  blocking collectives: 11.3 us -> 12 us
  Pallas kernels: 7.63 us -> 7.04 us
    ppermute x1, starting transfers between devices: 2.2 us -> 4.3 us  [shards(): lax.ppermute(third_rays, slab_axes, to_those((0, THIRD_STEP[1], THIRD_STE...]
    all_to_all x1, waiting for transfers between devices: 3.07 us -> 1.28 us  [shards(): lax.all_to_all(routed.reshape(slabs, ROWS, LANES), slab_axes, split_axis=...]
    dynamic_slice x7 -> x0, local copies, waits for them, and re-layouts: 1.74 us -> none  [the longest x2 1.24 us: shards(): jnp.asarray(step, jnp.int32)[my_slab % GROUP]]
    ppermute x1, starting transfers between devices: 4.37 us -> 5.79 us  [shards(): lax.ppermute(third_rays, slab_axes, to_those((THIRD_STEP[0], 0, 0, THIRD_...]
    unnamed x21 -> x14, local copies, waits for them, and re-layouts: 0.4 us -> 1.81 us
    all_to_all x1, blocking collectives: 11.3 us -> 12 us  [shards(): lax.all_to_all(merged, ('offset', 'chip', 'core'), split_axis=0, concat_a...]
    pallas_call x1, Pallas kernels: 0.76 us -> 0.11 us  [shards(): call(tails_kernel, (struct32(GROUP + HALF + 1, 8, LANES), struct32(8, dep...]
  transfers between devices with their start and end apart: 4 -> 4, of which waited for: 1 -> 1; matrix products, arithmetic and copies ran while one was open for 4% -> 0% of each run, Pallas kernels for 6% -> 5%
where the time goes in v7:
time: 54.9 us; the launch traced here: 54.5 us
  starting transfers between devices  32.3 us (59%)
  blocking collectives  12 us (22%)
  Pallas kernels  7.04 us (13%)
  local copies, waits for them, and re-layouts  1.81 us (3%)
  waiting for transfers between devices  1.29 us (2%)
    all_to_all x1, starting transfers between devices, shards(): lax.all_to_all(routed.reshape(slabs, ROWS, LANES), slab_axes, split_axis=...  21.4 us
    all_to_all x1, blocking collectives, shards(): lax.all_to_all(merged, ('offset', 'chip', 'core'), split_axis=0, concat_a...  12 us
    ppermute x1, starting transfers between devices, shards(): lax.ppermute(third_rays, slab_axes, to_those((THIRD_STEP[0], 0, 0, THIRD_...  5.79 us
    ppermute x1, starting transfers between devices, shards(): lax.ppermute(third_rays, slab_axes, to_those((0, THIRD_STEP[1], THIRD_STE...  4.3 us
    pallas_call x1, Pallas kernels, shards(): call(functools.partial(route_kernel, groups=groups), struct(slabs * ROWS,...  2.09 us
    pallas_call x1, Pallas kernels, shards(): call(functools.partial(near_kernel, scale=1.0 / math.sqrt(NT * count)), (...  1.95 us
    unnamed x14, local copies, waits for them, and re-layouts  1.81 us
    pallas_call x1, Pallas kernels, shards(): call(functools.partial(far_kernel, parts=parts), struct(GROUP * offsets,...  1.81 us
  transfers between devices with their start and end apart: 4, of which 1 were waited for; matrix products, arithmetic and copies ran while one was open for 0% of the time, Pallas kernels for 5%

profile of v7, /device:TPU:1, one launch (start us, length us, event | category | flops | bytes accessed | tf_op | source)
XLA Modules:
  0.0 54.5 jit_solution(3406214975495725847)
XLA Ops:
  0.0 0.0 copy-start.5
  0.0 0.0 copy-start.6
  0.0 2.1 %shard_map.119 = bf16[1024,128]{1,0:T(8,128)(2,1)} custom-call(s32[1,128]{1,0:T(1,128)} %bitcast.19, s32[1,128]{1,0:T(1,128)} %bins_ref.1, bf16[128,256]{1,0:T(8,128)(2,1)} %bitcast.18, bf16[256,128]{1,0:T(8,128)(2,1)} %constant.37.clone.high_ref, bf16[256,128]{1,0:T(8,128)(2,1)} %constant.38.clone.low_ref), custom_call_target="tpu_custom_call" | custom-call | bytes 1048576 | tf_op jit(solution)/shard_map/pallas_call | solution.py:370
  2.1 21.4 %all-to-all-start = ((bf16[64,16,128]{2,1,0:T(8,128)(2,1)}), bf16[64,16,128]{2,1,0:T(8,128)(2,1)S(1)}, u32[]{:S(2)}, u32[]{:S(2)}) async-start(bf16[64,16,128]{2,1,0:T(8,128)(2,1)} %bitcast.17), calls=%async_computation | async-start | bytes 524288 | tf_op jit(solution)/shard_map/all_to_all | solution.py:373
  23.5 0.0 copy-start.3
  23.5 0.9 %copy-done.3 = f32[1,1,7,16,256]{4,3,2,1,0:T(8,128)S(1)} copy-done((f32[1,1,7,16,256]{4,3,2,1,0:T(8,128)S(1)}, f32[1,1,7,16,256]{4,3,2,1,0:T(8,128)}, u32[]{:S(2)}) %copy-start.3) | copy-done | bytes 114712
  24.4 0.0 copy-start.4
  24.4 0.9 %copy-done.4 = f32[1,1,7,16,256]{4,3,2,1,0:T(8,128)S(1)} copy-done((f32[1,1,7,16,256]{4,3,2,1,0:T(8,128)S(1)}, f32[1,1,7,16,256]{4,3,2,1,0:T(8,128)}, u32[]{:S(2)}) %copy-start.4) | copy-done | bytes 114712
  25.3 0.0 copy-start
  25.3 0.0 copy-start.1
  25.3 0.0 copy-start.2
  25.3 0.8 %collective-permute-start = (f32[3,32,256]{2,1,0:T(8,128)S(1)}, f32[3,32,256]{2,1,0:T(8,128)S(1)}, u32[]{:S(2)}, u32[]{:S(2)}) collective-permute-start(f32[3,32,256]{2,1,0:T(8,128)S(1)} %get-tuple-element.17), channel_id=1, source_target_pairs={{5,2},{4,3},{3,4},{2,5},{9,6},{8,7},{7,8},{6,9},{13,10},{12,11},{1... | collective-permute-start | bytes 294920 | tf_op jit(solution)/shard_map/ppermute | solution.py:396
  26.1 5.8 %collective-permute-start.1 = (f32[32,256]{1,0:T(8,128)S(1)}, f32[32,256]{1,0:T(8,128)S(1)}, u32[]{:S(2)}, u32[]{:S(2)}) collective-permute-start(f32[32,256]{1,0:T(8,128)S(1)} %get-tuple-element.18), channel_id=1, source_target_pairs={{6,3},{1,4},{10,7},{5,8},{14,11},{9,12},{18,15},{13,16},{22,19},{1... | collective-permute-start | bytes 98312 | tf_op jit(solution)/shard_map/ppermute | solution.py:397
  31.9 4.3 %collective-permute-start.2 = (f32[32,256]{1,0:T(8,128)S(1)}, f32[32,256]{1,0:T(8,128)S(1)}, u32[]{:S(2)}, u32[]{:S(2)}) collective-permute-start(f32[32,256]{1,0:T(8,128)S(1)} %get-tuple-element.18), channel_id=1, source_target_pairs={{6,2},{1,5},{10,6},{5,9},{14,10},{9,13},{18,14},{13,17},{22,18},{1... | collective-permute-start | bytes 98312 | tf_op jit(solution)/shard_map/ppermute | solution.py:398
  36.3 0.4 shard_map.121.ready_ref
  36.7 0.0 copy-done.5
  36.7 0.0 copy-done.6
  36.7 0.1 shard_map.118
  36.8 1.3 %all-to-all-done = bf16[64,16,128]{2,1,0:T(8,128)(2,1)S(1)} async-done(((bf16[64,16,128]{2,1,0:T(8,128)(2,1)}), bf16[64,16,128]{2,1,0:T(8,128)(2,1)S(1)}, u32[]{:S(2)}, u32[]{:S(2)}) %all-to-all-start) | async-done | bytes 262176 | tf_op jit(solution)/shard_map/all_to_all | solution.py:373
  38.1 0.0 copy-done
  38.1 0.0 copy-done.1
  38.1 0.0 copy-done.2
  38.1 1.9 %shard_map.122 = (f32[4,128,256]{2,1,0:T(8,128)S(1)}, f32[4,1024]{1,0:T(4,128)S(1)}) custom-call(bf16[1024,128]{1,0:T(8,128)(2,1)S(1)} %bitcast.12, bf16[128,1024]{1,0:T(8,128)(2,1)S(1)} %copy-done, f32[16,1024]{1,0:T(8,128)S(1)} %copy-done.1, f32[16,1024]{1,0:T(8,128)S(1)} %copy-done.2, f32[4,32,256]{2,1,0:T(8,128)S(1)} %get-tuple-element.14.rays_ref, ...), custom_call_target="tpu_custom_call" | custom-call | bytes 1048576 | tf_op jit(solution)/shard_map/pallas_call | solution.py:414
  40.1 0.0 collective-permute-done.1.third_0_ref
  40.1 0.0 collective-permute-done.2.third_1_ref
  40.1 0.0 collective-permute-done.second_ref
  40.1 1.8 %shard_map.123 = bf16[32,32,128]{2,1,0:T(8,128)(2,1)S(1)} custom-call(f32[8,256]{1,0:T(8,128)S(1)} %get-tuple-element.12.flag_ref, f32[8,8,128]{2,1,0:T(8,128)S(1)} %get-tuple-element.13.tail_ref, f32[4,128,256]{2,1,0:T(8,128)S(1)} %get-tuple-element.15.near_ref, f32[4,1024]{1,0:T(4,128)S(1)} %get-tuple-element.16.beam_ref, ...), custom_call_target="tpu_custom_call" | custom-call | bytes 1048576 | tf_op jit(solution)/shard_map/pallas_call | solution.py:425
  41.9 12.0 %all_to_all.10.parts_ref = bf16[32,32,128]{2,1,0:T(8,128)(2,1)S(1)} all-to-all(bf16[32,32,128]{2,1,0:T(8,128)(2,1)S(1)} %shard_map.123), channel_id=1, replica_groups={{384,385,386,387,448,449,450,451,0,1,2,3,64,65,66,67,128,129,130,131,19..., dimensions={0} | all-to-all | bytes 524288 | tf_op jit(solution)/shard_map/all_to_all | solution.py:432
  53.9 0.7 %shard_map.124 = f32[32,128]{1,0:T(8,128)} custom-call(bf16[32,32,128]{2,1,0:T(8,128)(2,1)S(1)} %all_to_all.10.parts_ref), custom_call_target="tpu_custom_call" | custom-call | bytes 1048576 | tf_op jit(solution)/shard_map/pallas_call | solution.py:436
  (1 shorter events, 0.0 us)
Async XLA Ops:
  0.0 36.7 %copy-start.5 = (f32[1,64,7,16]{1,3,2,0:T(8,128)S(1)}, f32[1,64,7,16]{1,3,2,0:T(8,128)}, u32[]{:S(2)}) copy-start(f32[1,64,7,16]{1,3,2,0:T(8,128)} %param.17) | copy-start | bytes 86020
  0.0 36.7 %copy-start.6 = (s32[64,7,2]{0,2,1:T(2,128)S(1)}, s32[64,7,2]{0,2,1:T(2,128)}, u32[]{:S(2)}) copy-start(s32[64,7,2]{0,2,1:T(2,128)} %param.18) | copy-start | bytes 10756
  2.1 36.0 %all-to-all-start = ((bf16[64,16,128]{2,1,0:T(8,128)(2,1)}), bf16[64,16,128]{2,1,0:T(8,128)(2,1)S(1)}, u32[]{:S(2)}, u32[]{:S(2)}) async-start(bf16[64,16,128]{2,1,0:T(8,128)(2,1)} %bitcast.17), calls=%async_computation | async-start | bytes 524288 | tf_op jit(solution)/shard_map/all_to_all | solution.py:373
  23.5 0.9 %copy-start.3 = (f32[1,1,7,16,256]{4,3,2,1,0:T(8,128)S(1)}, f32[1,1,7,16,256]{4,3,2,1,0:T(8,128)}, u32[]{:S(2)}) copy-start(f32[1,1,7,16,256]{4,3,2,1,0:T(8,128)} %param.15) | copy-start | bytes 344068
  24.4 0.9 %copy-start.4 = (f32[1,1,7,16,256]{4,3,2,1,0:T(8,128)S(1)}, f32[1,1,7,16,256]{4,3,2,1,0:T(8,128)}, u32[]{:S(2)}) copy-start(f32[1,1,7,16,256]{4,3,2,1,0:T(8,128)} %param.16) | copy-start | bytes 344068
  25.3 12.8 %copy-start = (bf16[128,1024]{1,0:T(8,128)(2,1)S(1)}, bf16[128,1024]{1,0:T(8,128)(2,1)}, u32[]{:S(2)}) copy-start(bf16[128,1024]{1,0:T(8,128)(2,1)} %constant.39.clone.spread_ref) | copy-start | bytes 786436
  25.3 12.8 %copy-start.1 = (f32[16,1024]{1,0:T(8,128)S(1)}, f32[16,1024]{1,0:T(8,128)}, u32[]{:S(2)}) copy-start(f32[16,1024]{1,0:T(8,128)} %constant.40.clone.cos_ref) | copy-start | bytes 196612
  25.3 12.8 %copy-start.2 = (f32[16,1024]{1,0:T(8,128)S(1)}, f32[16,1024]{1,0:T(8,128)}, u32[]{:S(2)}) copy-start(f32[16,1024]{1,0:T(8,128)} %constant.41.clone.sin_ref) | copy-start | bytes 196612
  25.3 14.7 %collective-permute-start = (f32[3,32,256]{2,1,0:T(8,128)S(1)}, f32[3,32,256]{2,1,0:T(8,128)S(1)}, u32[]{:S(2)}, u32[]{:S(2)}) collective-permute-start(f32[3,32,256]{2,1,0:T(8,128)S(1)} %get-tuple-element.17), channel_id=1, source_target_pairs={{5,2},{4,3},{3,4},{2,5},{9,6},{8,7},{7,8},{6,9},{13,10},{12,11},{1... | collective-permute-start | bytes 294920 | tf_op jit(solution)/shard_map/ppermute | solution.py:396
  26.1 13.9 %collective-permute-start.1 = (f32[32,256]{1,0:T(8,128)S(1)}, f32[32,256]{1,0:T(8,128)S(1)}, u32[]{:S(2)}, u32[]{:S(2)}) collective-permute-start(f32[32,256]{1,0:T(8,128)S(1)} %get-tuple-element.18), channel_id=1, source_target_pairs={{6,3},{1,4},{10,7},{5,8},{14,11},{9,12},{18,15},{13,16},{22,19},{1... | collective-permute-start | bytes 98312 | tf_op jit(solution)/shard_map/ppermute | solution.py:397
  31.9 8.1 %collective-permute-start.2 = (f32[32,256]{1,0:T(8,128)S(1)}, f32[32,256]{1,0:T(8,128)S(1)}, u32[]{:S(2)}, u32[]{:S(2)}) collective-permute-start(f32[32,256]{1,0:T(8,128)S(1)} %get-tuple-element.18), channel_id=1, source_target_pairs={{6,2},{1,5},{10,6},{5,9},{14,10},{9,13},{18,14},{13,17},{22,18},{1... | collective-permute-start | bytes 98312 | tf_op jit(solution)/shard_map/ppermute | solution.py:398

commit v8 on v7

--- a/solution.py
+++ b/solution.py
@@ -23,7 +23,7 @@
 HALF = (WIN - 1) // 2
 GROUPS = P_SIZE * NF // LANES
 GROUP = 4
-FIRST_SLAB = 52
+FIRST_SLAB = 54
 READY = 2
 FIRST_OFFSET = 6
 SECOND_STEP = (-1, -3, 3, 1)
@@ -106,7 +106,11 @@
         jnp.where(wanted + group * GROUP * 8 == code_across, 1.0, 0.0).astype(bf16)
         for group in groups
     ]
-    picked = dot(jnp.concatenate(pick, axis=0), values).reshape(-1, ROWS, 2 * LANES)
+    pick = jnp.concatenate(pick, axis=0)
+    skip = FIRST_SLAB % GROUP * ROWS
+    if skip:
+        pick = jnp.concatenate([pick[skip:], pick[:skip]], axis=0)
+    picked = dot(pick, values).reshape(-1, ROWS, 2 * LANES)
     shape = picked.shape[:2] + (LANES,)
     places = jnp.where(iota(shape, 1) == iota(shape, 2), picked[:, :, LANES:], 0.0)
     places = jnp.broadcast_to(jnp.sum(places, axis=1, keepdims=True), shape)
@@ -169,26 +173,28 @@
     def times_of(a, b):
         return a[0] * b[0] - a[1] * b[1], a[0] * b[1] + a[1] * b[0]
 
-    one = cos_sin_turns(times * (1.0 / NT))
+    cos_1, sin_1 = cos_sin_turns(times * (1.0 / NT))
+    one = (cos_1, -sin_1)
     two = times_of(one, one)
     four = times_of(two, two)
     eight = times_of(four, four)
-    start = (amps * eight[0], amps * eight[1])
-    walk = [start, times_of(start, one), times_of(start, two)]
-    walk.append(times_of(walk[1], two))
-    values = [(c, -s) for c, s in walk]
-    factor = 2.0 * two[0]
-    for j in range(NF):
-        if j >= 4:
-            values.append(
-                tuple(factor * values[j - 2][i] - values[j - 4][i] for i in range(2))
-            )
-        group, inner = divmod(j, LANES // P_SIZE)
-        for i in range(2):
-            first = group * 2 * LANES + i * LANES + inner * P_SIZE
-            u_ref[pl.ds(first, P_SIZE), :] = values[j][i].astype(bf16)
-        if inner == LANES // P_SIZE - 1:
-            yield
+    first = (amps * eight[0], amps * eight[1])
+    second = times_of(first, one)
+    factor = 2.0 * cos_1
+    number = LANES // P_SIZE
+    for group in range(GROUPS):
+        if group:
+            first, second = times_of(first, eight), times_of(second, eight)
+        values = [first, second]
+        for inner in range(number):
+            if inner >= 2:
+                values.append(
+                    tuple(factor * values[-1][i] - values[-2][i] for i in range(2))
+                )
+            for i in range(2):
+                row = group * 2 * LANES + i * LANES + inner * P_SIZE
+                u_ref[pl.ds(row, P_SIZE), :] = values[inner][i].astype(bf16)
+        yield
 
 
 def v_groups(lateral, first, end, beam_re, beam_im):
@@ -366,7 +372,7 @@
     part = depth // offsets
     high, low = dft_tables()
     groups = [(FIRST_SLAB // GROUP + i) % (slabs // GROUP) for i in range(slabs // GROUP)]
-    order = [group * GROUP + i for group in groups for i in range(GROUP)]
+    order = [(FIRST_SLAB + i) % slabs for i in range(slabs)]
     routed = call(functools.partial(route_kernel, groups=groups), struct(slabs * ROWS, LANES), [vmem()] * 5)(
         centre_ids.reshape(1, count), midpoint_bins, traces[0], jnp.asarray(high), jnp.asarray(low)
     )

time: 54.9 us -> 54.4 us (level)
    all_to_all x1, starting transfers between devices: 21.4 us -> 20.5 us  [shards(): lax.all_to_all(routed.reshape(slabs, ROWS, LANES), slab_axes, split_axis=...]
    ppermute x1, starting transfers between devices: 4.3 us -> 5.2 us  [shards(): lax.ppermute(third_rays, slab_axes, to_those((0, THIRD_STEP[1], THIRD_STE...]
  transfers between devices with their start and end apart: 4 -> 4, of which waited for: 1 -> 1; matrix products, arithmetic and copies ran while one was open for 0% -> 0% of each run, Pallas kernels for 5% -> 4%
where the time goes in v8:
time: 54.4 us; the launch traced here: 54 us
  starting transfers between devices  32.3 us (59%)
  blocking collectives  11.7 us (22%)
  Pallas kernels  6.83 us (13%)
  local copies, waits for them, and re-layouts  1.81 us (3%)
  waiting for transfers between devices  1.29 us (2%)
    all_to_all x1, starting transfers between devices, shards(): lax.all_to_all(routed.reshape(slabs, ROWS, LANES), slab_axes, split_axis=...  20.5 us
    all_to_all x1, blocking collectives, shards(): lax.all_to_all(merged, ('offset', 'chip', 'core'), split_axis=0, concat_a...  11.7 us
    ppermute x1, starting transfers between devices, shards(): lax.ppermute(third_rays, slab_axes, to_those((THIRD_STEP[0], 0, 0, THIRD_...  5.79 us
    ppermute x1, starting transfers between devices, shards(): lax.ppermute(third_rays, slab_axes, to_those((0, THIRD_STEP[1], THIRD_STE...  5.2 us
    pallas_call x1, Pallas kernels, shards(): call(functools.partial(route_kernel, groups=groups), struct(slabs * ROWS,...  2.09 us
    pallas_call x1, Pallas kernels, shards(): call(functools.partial(near_kernel, scale=1.0 / math.sqrt(NT * count)), (...  1.87 us
    unnamed x14, local copies, waits for them, and re-layouts  1.81 us
    pallas_call x1, Pallas kernels, shards(): call(functools.partial(far_kernel, parts=parts), struct(GROUP * offsets,...  1.65 us
  transfers between devices with their start and end apart: 4, of which 1 were waited for; matrix products, arithmetic and copies ran while one was open for 0% of the time, Pallas kernels for 4%

profile of v8, /device:TPU:1, one launch (start us, length us, event | category | flops | bytes accessed | tf_op | source)
XLA Modules:
  0.0 54.0 jit_solution(5893390315127686370)
XLA Ops:
  0.0 0.0 copy-start.5
  0.0 0.0 copy-start.6
  0.0 2.1 %shard_map.119 = bf16[1024,128]{1,0:T(8,128)(2,1)} custom-call(s32[1,128]{1,0:T(1,128)} %bitcast.19, s32[1,128]{1,0:T(1,128)} %bins_ref.1, bf16[128,256]{1,0:T(8,128)(2,1)} %bitcast.18, bf16[256,128]{1,0:T(8,128)(2,1)} %constant.37.clone.high_ref, bf16[256,128]{1,0:T(8,128)(2,1)} %constant.38.clone.low_ref), custom_call_target="tpu_custom_call" | custom-call | bytes 1048576 | tf_op jit(solution)/shard_map/pallas_call | solution.py:376
  2.1 20.5 %all-to-all-start = ((bf16[64,16,128]{2,1,0:T(8,128)(2,1)}), bf16[64,16,128]{2,1,0:T(8,128)(2,1)S(1)}, u32[]{:S(2)}, u32[]{:S(2)}) async-start(bf16[64,16,128]{2,1,0:T(8,128)(2,1)} %bitcast.17), calls=%async_computation | async-start | bytes 524288 | tf_op jit(solution)/shard_map/all_to_all | solution.py:379
  22.6 0.0 copy-start.3
  22.6 0.9 %copy-done.3 = f32[1,1,7,16,256]{4,3,2,1,0:T(8,128)S(1)} copy-done((f32[1,1,7,16,256]{4,3,2,1,0:T(8,128)S(1)}, f32[1,1,7,16,256]{4,3,2,1,0:T(8,128)}, u32[]{:S(2)}) %copy-start.3) | copy-done | bytes 114712
  23.5 0.0 copy-start.4
  23.5 0.9 %copy-done.4 = f32[1,1,7,16,256]{4,3,2,1,0:T(8,128)S(1)} copy-done((f32[1,1,7,16,256]{4,3,2,1,0:T(8,128)S(1)}, f32[1,1,7,16,256]{4,3,2,1,0:T(8,128)}, u32[]{:S(2)}) %copy-start.4) | copy-done | bytes 114712
  24.4 0.0 copy-start
  24.4 0.0 copy-start.1
  24.4 0.0 copy-start.2
  24.4 0.8 %collective-permute-start = (f32[3,32,256]{2,1,0:T(8,128)S(1)}, f32[3,32,256]{2,1,0:T(8,128)S(1)}, u32[]{:S(2)}, u32[]{:S(2)}) collective-permute-start(f32[3,32,256]{2,1,0:T(8,128)S(1)} %get-tuple-element.17), channel_id=1, source_target_pairs={{5,2},{4,3},{3,4},{2,5},{9,6},{8,7},{7,8},{6,9},{13,10},{12,11},{1... | collective-permute-start | bytes 294920 | tf_op jit(solution)/shard_map/ppermute | solution.py:402
  25.2 5.8 %collective-permute-start.1 = (f32[32,256]{1,0:T(8,128)S(1)}, f32[32,256]{1,0:T(8,128)S(1)}, u32[]{:S(2)}, u32[]{:S(2)}) collective-permute-start(f32[32,256]{1,0:T(8,128)S(1)} %get-tuple-element.18), channel_id=1, source_target_pairs={{6,3},{1,4},{10,7},{5,8},{14,11},{9,12},{18,15},{13,16},{22,19},{1... | collective-permute-start | bytes 98312 | tf_op jit(solution)/shard_map/ppermute | solution.py:403
  31.0 5.2 %collective-permute-start.2 = (f32[32,256]{1,0:T(8,128)S(1)}, f32[32,256]{1,0:T(8,128)S(1)}, u32[]{:S(2)}, u32[]{:S(2)}) collective-permute-start(f32[32,256]{1,0:T(8,128)S(1)} %get-tuple-element.18), channel_id=1, source_target_pairs={{6,2},{1,5},{10,6},{5,9},{14,10},{9,13},{18,14},{13,17},{22,18},{1... | collective-permute-start | bytes 98312 | tf_op jit(solution)/shard_map/ppermute | solution.py:404
  36.3 0.4 shard_map.121.ready_ref
  36.7 0.0 copy-done.5
  36.7 0.0 copy-done.6
  36.7 0.1 shard_map.118
  36.8 1.3 %all-to-all-done = bf16[64,16,128]{2,1,0:T(8,128)(2,1)S(1)} async-done(((bf16[64,16,128]{2,1,0:T(8,128)(2,1)}), bf16[64,16,128]{2,1,0:T(8,128)(2,1)S(1)}, u32[]{:S(2)}, u32[]{:S(2)}) %all-to-all-start) | async-done | bytes 262176 | tf_op jit(solution)/shard_map/all_to_all | solution.py:379
  38.1 0.0 copy-done
  38.1 0.0 copy-done.1
  38.1 0.0 copy-done.2
  38.1 1.9 %shard_map.122 = (f32[4,128,256]{2,1,0:T(8,128)S(1)}, f32[4,1024]{1,0:T(4,128)S(1)}) custom-call(bf16[1024,128]{1,0:T(8,128)(2,1)S(1)} %bitcast.12, bf16[128,1024]{1,0:T(8,128)(2,1)S(1)} %copy-done, f32[16,1024]{1,0:T(8,128)S(1)} %copy-done.1, f32[16,1024]{1,0:T(8,128)S(1)} %copy-done.2, f32[4,32,256]{2,1,0:T(8,128)S(1)} %get-tuple-element.14.rays_ref, ...), custom_call_target="tpu_custom_call" | custom-call | bytes 1048576 | tf_op jit(solution)/shard_map/pallas_call | solution.py:420
  40.0 0.0 collective-permute-done.1.third_0_ref
  40.0 0.0 collective-permute-done.2.third_1_ref
  40.0 0.0 collective-permute-done.second_ref
  40.0 1.6 %shard_map.123 = bf16[32,32,128]{2,1,0:T(8,128)(2,1)S(1)} custom-call(f32[8,256]{1,0:T(8,128)S(1)} %get-tuple-element.12.flag_ref, f32[8,8,128]{2,1,0:T(8,128)S(1)} %get-tuple-element.13.tail_ref, f32[4,128,256]{2,1,0:T(8,128)S(1)} %get-tuple-element.15.near_ref, f32[4,1024]{1,0:T(4,128)S(1)} %get-tuple-element.16.beam_ref, ...), custom_call_target="tpu_custom_call" | custom-call | bytes 1048576 | tf_op jit(solution)/shard_map/pallas_call | solution.py:431
  41.7 11.7 %all_to_all.10.parts_ref = bf16[32,32,128]{2,1,0:T(8,128)(2,1)S(1)} all-to-all(bf16[32,32,128]{2,1,0:T(8,128)(2,1)S(1)} %shard_map.123), channel_id=1, replica_groups={{384,385,386,387,448,449,450,451,0,1,2,3,64,65,66,67,128,129,130,131,19..., dimensions={0} | all-to-all | bytes 524288 | tf_op jit(solution)/shard_map/all_to_all | solution.py:438
  53.4 0.7 %shard_map.124 = f32[32,128]{1,0:T(8,128)} custom-call(bf16[32,32,128]{2,1,0:T(8,128)(2,1)S(1)} %all_to_all.10.parts_ref), custom_call_target="tpu_custom_call" | custom-call | bytes 1048576 | tf_op jit(solution)/shard_map/pallas_call | solution.py:442
  (1 shorter events, 0.0 us)
Async XLA Ops:
  0.0 36.7 %copy-start.5 = (f32[1,64,7,16]{1,3,2,0:T(8,128)S(1)}, f32[1,64,7,16]{1,3,2,0:T(8,128)}, u32[]{:S(2)}) copy-start(f32[1,64,7,16]{1,3,2,0:T(8,128)} %param.17) | copy-start | bytes 86020
  0.0 36.7 %copy-start.6 = (s32[64,7,2]{0,2,1:T(2,128)S(1)}, s32[64,7,2]{0,2,1:T(2,128)}, u32[]{:S(2)}) copy-start(s32[64,7,2]{0,2,1:T(2,128)} %param.18) | copy-start | bytes 10756
  2.1 36.0 %all-to-all-start = ((bf16[64,16,128]{2,1,0:T(8,128)(2,1)}), bf16[64,16,128]{2,1,0:T(8,128)(2,1)S(1)}, u32[]{:S(2)}, u32[]{:S(2)}) async-start(bf16[64,16,128]{2,1,0:T(8,128)(2,1)} %bitcast.17), calls=%async_computation | async-start | bytes 524288 | tf_op jit(solution)/shard_map/all_to_all | solution.py:379
  22.6 0.9 %copy-start.3 = (f32[1,1,7,16,256]{4,3,2,1,0:T(8,128)S(1)}, f32[1,1,7,16,256]{4,3,2,1,0:T(8,128)}, u32[]{:S(2)}) copy-start(f32[1,1,7,16,256]{4,3,2,1,0:T(8,128)} %param.15) | copy-start | bytes 344068
  23.5 0.9 %copy-start.4 = (f32[1,1,7,16,256]{4,3,2,1,0:T(8,128)S(1)}, f32[1,1,7,16,256]{4,3,2,1,0:T(8,128)}, u32[]{:S(2)}) copy-start(f32[1,1,7,16,256]{4,3,2,1,0:T(8,128)} %param.16) | copy-start | bytes 344068
  24.4 13.7 %copy-start = (bf16[128,1024]{1,0:T(8,128)(2,1)S(1)}, bf16[128,1024]{1,0:T(8,128)(2,1)}, u32[]{:S(2)}) copy-start(bf16[128,1024]{1,0:T(8,128)(2,1)} %constant.39.clone.spread_ref) | copy-start | bytes 786436
  24.4 13.7 %copy-start.1 = (f32[16,1024]{1,0:T(8,128)S(1)}, f32[16,1024]{1,0:T(8,128)}, u32[]{:S(2)}) copy-start(f32[16,1024]{1,0:T(8,128)} %constant.40.clone.cos_ref) | copy-start | bytes 196612
  24.4 13.7 %copy-start.2 = (f32[16,1024]{1,0:T(8,128)S(1)}, f32[16,1024]{1,0:T(8,128)}, u32[]{:S(2)}) copy-start(f32[16,1024]{1,0:T(8,128)} %constant.41.clone.sin_ref) | copy-start | bytes 196612
  24.4 15.6 %collective-permute-start = (f32[3,32,256]{2,1,0:T(8,128)S(1)}, f32[3,32,256]{2,1,0:T(8,128)S(1)}, u32[]{:S(2)}, u32[]{:S(2)}) collective-permute-start(f32[3,32,256]{2,1,0:T(8,128)S(1)} %get-tuple-element.17), channel_id=1, source_target_pairs={{5,2},{4,3},{3,4},{2,5},{9,6},{8,7},{7,8},{6,9},{13,10},{12,11},{1... | collective-permute-start | bytes 294920 | tf_op jit(solution)/shard_map/ppermute | solution.py:402
  25.2 14.8 %collective-permute-start.1 = (f32[32,256]{1,0:T(8,128)S(1)}, f32[32,256]{1,0:T(8,128)S(1)}, u32[]{:S(2)}, u32[]{:S(2)}) collective-permute-start(f32[32,256]{1,0:T(8,128)S(1)} %get-tuple-element.18), channel_id=1, source_target_pairs={{6,3},{1,4},{10,7},{5,8},{14,11},{9,12},{18,15},{13,16},{22,19},{1... | collective-permute-start | bytes 98312 | tf_op jit(solution)/shard_map/ppermute | solution.py:403
  31.0 9.0 %collective-permute-start.2 = (f32[32,256]{1,0:T(8,128)S(1)}, f32[32,256]{1,0:T(8,128)S(1)}, u32[]{:S(2)}, u32[]{:S(2)}) collective-permute-start(f32[32,256]{1,0:T(8,128)S(1)} %get-tuple-element.18), channel_id=1, source_target_pairs={{6,2},{1,5},{10,6},{5,9},{14,10},{9,13},{18,14},{13,17},{22,18},{1... | collective-permute-start | bytes 98312 | tf_op jit(solution)/shard_map/ppermute | solution.py:404

commit v9 on v8

--- a/solution.py
+++ b/solution.py
@@ -77,7 +77,18 @@
     return value
 
 
-def route_kernel(ids_ref, bins_ref, traces_ref, high_ref, low_ref, out_ref, *, groups):
+def route_kernel(
+    ids_ref, bins_ref, traces_hbm, high_hbm, low_hbm, out_ref, traces_ref, high_ref, low_ref, sems,
+    *, groups,
+):
+    copies = [
+        pltpu.make_async_copy(source, target, sems.at[i])
+        for i, (source, target) in enumerate(
+            ((traces_hbm, traces_ref), (high_hbm, high_ref), (low_hbm, low_ref))
+        )
+    ]
+    for copy in copies:
+        copy.start()
     count = traces_ref.shape[0]
     square = (count, count)
     row, col = iota(square, 0), iota(square, 1)
@@ -90,9 +101,6 @@
     code_across = ids_across * 8 + rank_across.astype(jnp.int32)
     place_across = bins_ref[...].astype(f32) - (BINS - 1) / 2.0
     place_down = jnp.sum(jnp.where(row == col, place_across, 0.0), axis=1, keepdims=True)
-    traces = traces_ref[...]
-    spectrum = dot(traces, high_ref[...]) + dot(traces, low_ref[...])
-    values = jnp.concatenate([spectrum, jnp.broadcast_to(place_down, square)], axis=1).astype(bf16)
 
     group_rows = GROUP * ROWS
     slot = iota((group_rows, count), 0) % ROWS
@@ -110,6 +118,11 @@
     skip = FIRST_SLAB % GROUP * ROWS
     if skip:
         pick = jnp.concatenate([pick[skip:], pick[:skip]], axis=0)
+    for copy in copies:
+        copy.wait()
+    traces = traces_ref[...]
+    spectrum = dot(traces, high_ref[...]) + dot(traces, low_ref[...])
+    values = jnp.concatenate([spectrum, jnp.broadcast_to(place_down, square)], axis=1).astype(bf16)
     picked = dot(pick, values).reshape(-1, ROWS, 2 * LANES)
     shape = picked.shape[:2] + (LANES,)
     places = jnp.where(iota(shape, 1) == iota(shape, 2), picked[:, :, LANES:], 0.0)
@@ -373,7 +386,10 @@
     high, low = dft_tables()
     groups = [(FIRST_SLAB // GROUP + i) % (slabs // GROUP) for i in range(slabs // GROUP)]
     order = [(FIRST_SLAB + i) % slabs for i in range(slabs)]
-    routed = call(functools.partial(route_kernel, groups=groups), struct(slabs * ROWS, LANES), [vmem()] * 5)(
+    routed = call(functools.partial(route_kernel, groups=groups), struct(slabs * ROWS, LANES), [vmem()] * 2 + [pl.BlockSpec(memory_space=pl.ANY)] * 3, None, [
+        pltpu.VMEM((count, NT), bf16), pltpu.VMEM((NT, LANES), bf16),
+        pltpu.VMEM((NT, LANES), bf16), pltpu.SemaphoreType.DMA((3,)),
+    ])(
         centre_ids.reshape(1, count), midpoint_bins, traces[0], jnp.asarray(high), jnp.asarray(low)
     )
     arrived = lax.all_to_all(

time: 54.4 us -> 55.1 us (1.013)
  Pallas kernels: 6.83 us -> 7.49 us
    pallas_call x1, Pallas kernels: 2.09 us -> 2.77 us  [shards(): call(functools.partial(route_kernel, groups=groups), struct(slabs * ROWS,...]
where the time goes in v9:
time: 55.1 us; the launch traced here: 54.7 us
  starting transfers between devices  32.3 us (59%)
  blocking collectives  11.7 us (21%)
  Pallas kernels  7.49 us (14%)
  local copies, waits for them, and re-layouts  1.81 us (3%)
  waiting for transfers between devices  1.29 us (2%)
    all_to_all x1, starting transfers between devices, shards(): lax.all_to_all(routed.reshape(slabs, ROWS, LANES), slab_axes, split_axis=...  20.5 us
    all_to_all x1, blocking collectives, shards(): lax.all_to_all(merged, ('offset', 'chip', 'core'), split_axis=0, concat_a...  11.7 us
    ppermute x1, starting transfers between devices, shards(): lax.ppermute(third_rays, slab_axes, to_those((THIRD_STEP[0], 0, 0, THIRD_...  5.79 us
    ppermute x1, starting transfers between devices, shards(): lax.ppermute(third_rays, slab_axes, to_those((0, THIRD_STEP[1], THIRD_STE...  5.2 us
    pallas_call x1, Pallas kernels, shards(): call(functools.partial(route_kernel, groups=groups), struct(slabs * ROWS,...  2.77 us
    pallas_call x1, Pallas kernels, shards(): call(functools.partial(near_kernel, scale=1.0 / math.sqrt(NT * count)), (...  1.86 us
    unnamed x14, local copies, waits for them, and re-layouts  1.81 us
    pallas_call x1, Pallas kernels, shards(): call(functools.partial(far_kernel, parts=parts), struct(GROUP * offsets,...  1.65 us
  transfers between devices with their start and end apart: 4, of which 1 were waited for; matrix products, arithmetic and copies ran while one was open for 0% of the time, Pallas kernels for 4%

profile of v9, /device:TPU:1, one launch (start us, length us, event | category | flops | bytes accessed | tf_op | source)
XLA Modules:
  0.0 54.7 jit_solution(18204700160011623302)
XLA Ops:
  0.0 0.0 copy-start.5
  0.0 0.0 copy-start.6
  0.0 2.8 %shard_map.119 = bf16[1024,128]{1,0:T(8,128)(2,1)} custom-call(s32[1,128]{1,0:T(1,128)} %bitcast.19, s32[1,128]{1,0:T(1,128)} %bins_ref.1, bf16[128,256]{1,0:T(8,128)(2,1)} %bitcast.18, bf16[256,128]{1,0:T(8,128)(2,1)} %constant.37.clone.high_hbm, bf16[256,128]{1,0:T(8,128)(2,1)} %constant.38.clone.low_hbm), custom_call_target="tpu_custom_call" | custom-call | bytes 1048576 | tf_op jit(solution)/shard_map/pallas_call | solution.py:389
  2.8 20.5 %all-to-all-start = ((bf16[64,16,128]{2,1,0:T(8,128)(2,1)}), bf16[64,16,128]{2,1,0:T(8,128)(2,1)S(1)}, u32[]{:S(2)}, u32[]{:S(2)}) async-start(bf16[64,16,128]{2,1,0:T(8,128)(2,1)} %bitcast.17), calls=%async_computation | async-start | bytes 524288 | tf_op jit(solution)/shard_map/all_to_all | solution.py:395
  23.3 0.0 copy-start.3
  23.3 0.9 %copy-done.3 = f32[1,1,7,16,256]{4,3,2,1,0:T(8,128)S(1)} copy-done((f32[1,1,7,16,256]{4,3,2,1,0:T(8,128)S(1)}, f32[1,1,7,16,256]{4,3,2,1,0:T(8,128)}, u32[]{:S(2)}) %copy-start.3) | copy-done | bytes 114712
  24.2 0.0 copy-start.4
  24.2 0.9 %copy-done.4 = f32[1,1,7,16,256]{4,3,2,1,0:T(8,128)S(1)} copy-done((f32[1,1,7,16,256]{4,3,2,1,0:T(8,128)S(1)}, f32[1,1,7,16,256]{4,3,2,1,0:T(8,128)}, u32[]{:S(2)}) %copy-start.4) | copy-done | bytes 114712
  25.1 0.0 copy-start
  25.1 0.0 copy-start.1
  25.1 0.0 copy-start.2
  25.1 0.8 %collective-permute-start = (f32[3,32,256]{2,1,0:T(8,128)S(1)}, f32[3,32,256]{2,1,0:T(8,128)S(1)}, u32[]{:S(2)}, u32[]{:S(2)}) collective-permute-start(f32[3,32,256]{2,1,0:T(8,128)S(1)} %get-tuple-element.17), channel_id=1, source_target_pairs={{5,2},{4,3},{3,4},{2,5},{9,6},{8,7},{7,8},{6,9},{13,10},{12,11},{1... | collective-permute-start | bytes 294920 | tf_op jit(solution)/shard_map/ppermute | solution.py:418
  25.9 5.8 %collective-permute-start.1 = (f32[32,256]{1,0:T(8,128)S(1)}, f32[32,256]{1,0:T(8,128)S(1)}, u32[]{:S(2)}, u32[]{:S(2)}) collective-permute-start(f32[32,256]{1,0:T(8,128)S(1)} %get-tuple-element.18), channel_id=1, source_target_pairs={{6,3},{1,4},{10,7},{5,8},{14,11},{9,12},{18,15},{13,16},{22,19},{1... | collective-permute-start | bytes 98312 | tf_op jit(solution)/shard_map/ppermute | solution.py:419
  31.7 5.2 %collective-permute-start.2 = (f32[32,256]{1,0:T(8,128)S(1)}, f32[32,256]{1,0:T(8,128)S(1)}, u32[]{:S(2)}, u32[]{:S(2)}) collective-permute-start(f32[32,256]{1,0:T(8,128)S(1)} %get-tuple-element.18), channel_id=1, source_target_pairs={{6,2},{1,5},{10,6},{5,9},{14,10},{9,13},{18,14},{13,17},{22,18},{1... | collective-permute-start | bytes 98312 | tf_op jit(solution)/shard_map/ppermute | solution.py:420
  36.9 0.4 shard_map.121.ready_ref
  37.4 0.0 copy-done.5
  37.4 0.0 copy-done.6
  37.4 0.1 shard_map.118
  37.5 1.3 %all-to-all-done = bf16[64,16,128]{2,1,0:T(8,128)(2,1)S(1)} async-done(((bf16[64,16,128]{2,1,0:T(8,128)(2,1)}), bf16[64,16,128]{2,1,0:T(8,128)(2,1)S(1)}, u32[]{:S(2)}, u32[]{:S(2)}) %all-to-all-start) | async-done | bytes 262176 | tf_op jit(solution)/shard_map/all_to_all | solution.py:395
  38.8 0.0 copy-done
  38.8 0.0 copy-done.1
  38.8 0.0 copy-done.2
  38.8 1.9 %shard_map.122 = (f32[4,128,256]{2,1,0:T(8,128)S(1)}, f32[4,1024]{1,0:T(4,128)S(1)}) custom-call(bf16[1024,128]{1,0:T(8,128)(2,1)S(1)} %bitcast.12, bf16[128,1024]{1,0:T(8,128)(2,1)S(1)} %copy-done, f32[16,1024]{1,0:T(8,128)S(1)} %copy-done.1, f32[16,1024]{1,0:T(8,128)S(1)} %copy-done.2, f32[4,32,256]{2,1,0:T(8,128)S(1)} %get-tuple-element.14.rays_ref, ...), custom_call_target="tpu_custom_call" | custom-call | bytes 1048576 | tf_op jit(solution)/shard_map/pallas_call | solution.py:436
  40.7 0.0 collective-permute-done.1.third_0_ref
  40.7 0.0 collective-permute-done.2.third_1_ref
  40.7 0.0 collective-permute-done.second_ref
  40.7 1.6 %shard_map.123 = bf16[32,32,128]{2,1,0:T(8,128)(2,1)S(1)} custom-call(f32[8,256]{1,0:T(8,128)S(1)} %get-tuple-element.12.flag_ref, f32[8,8,128]{2,1,0:T(8,128)S(1)} %get-tuple-element.13.tail_ref, f32[4,128,256]{2,1,0:T(8,128)S(1)} %get-tuple-element.15.near_ref, f32[4,1024]{1,0:T(4,128)S(1)} %get-tuple-element.16.beam_ref, ...), custom_call_target="tpu_custom_call" | custom-call | bytes 1048576 | tf_op jit(solution)/shard_map/pallas_call | solution.py:447
  42.4 11.7 %all_to_all.10.parts_ref = bf16[32,32,128]{2,1,0:T(8,128)(2,1)S(1)} all-to-all(bf16[32,32,128]{2,1,0:T(8,128)(2,1)S(1)} %shard_map.123), channel_id=1, replica_groups={{384,385,386,387,448,449,450,451,0,1,2,3,64,65,66,67,128,129,130,131,19..., dimensions={0} | all-to-all | bytes 524288 | tf_op jit(solution)/shard_map/all_to_all | solution.py:454
  54.1 0.7 %shard_map.124 = f32[32,128]{1,0:T(8,128)} custom-call(bf16[32,32,128]{2,1,0:T(8,128)(2,1)S(1)} %all_to_all.10.parts_ref), custom_call_target="tpu_custom_call" | custom-call | bytes 1048576 | tf_op jit(solution)/shard_map/pallas_call | solution.py:458
  (1 shorter events, 0.0 us)
Async XLA Ops:
  0.0 37.4 %copy-start.5 = (f32[1,64,7,16]{1,3,2,0:T(8,128)S(1)}, f32[1,64,7,16]{1,3,2,0:T(8,128)}, u32[]{:S(2)}) copy-start(f32[1,64,7,16]{1,3,2,0:T(8,128)} %param.17) | copy-start | bytes 86020
  0.0 37.4 %copy-start.6 = (s32[64,7,2]{0,2,1:T(2,128)S(1)}, s32[64,7,2]{0,2,1:T(2,128)}, u32[]{:S(2)}) copy-start(s32[64,7,2]{0,2,1:T(2,128)} %param.18) | copy-start | bytes 10756
  2.8 36.0 %all-to-all-start = ((bf16[64,16,128]{2,1,0:T(8,128)(2,1)}), bf16[64,16,128]{2,1,0:T(8,128)(2,1)S(1)}, u32[]{:S(2)}, u32[]{:S(2)}) async-start(bf16[64,16,128]{2,1,0:T(8,128)(2,1)} %bitcast.17), calls=%async_computation | async-start | bytes 524288 | tf_op jit(solution)/shard_map/all_to_all | solution.py:395
  23.3 0.9 %copy-start.3 = (f32[1,1,7,16,256]{4,3,2,1,0:T(8,128)S(1)}, f32[1,1,7,16,256]{4,3,2,1,0:T(8,128)}, u32[]{:S(2)}) copy-start(f32[1,1,7,16,256]{4,3,2,1,0:T(8,128)} %param.15) | copy-start | bytes 344068
  24.2 0.9 %copy-start.4 = (f32[1,1,7,16,256]{4,3,2,1,0:T(8,128)S(1)}, f32[1,1,7,16,256]{4,3,2,1,0:T(8,128)}, u32[]{:S(2)}) copy-start(f32[1,1,7,16,256]{4,3,2,1,0:T(8,128)} %param.16) | copy-start | bytes 344068
  25.1 13.7 %copy-start = (bf16[128,1024]{1,0:T(8,128)(2,1)S(1)}, bf16[128,1024]{1,0:T(8,128)(2,1)}, u32[]{:S(2)}) copy-start(bf16[128,1024]{1,0:T(8,128)(2,1)} %constant.39.clone.spread_ref) | copy-start | bytes 786436
  25.1 13.7 %copy-start.1 = (f32[16,1024]{1,0:T(8,128)S(1)}, f32[16,1024]{1,0:T(8,128)}, u32[]{:S(2)}) copy-start(f32[16,1024]{1,0:T(8,128)} %constant.40.clone.cos_ref) | copy-start | bytes 196612
  25.1 13.7 %copy-start.2 = (f32[16,1024]{1,0:T(8,128)S(1)}, f32[16,1024]{1,0:T(8,128)}, u32[]{:S(2)}) copy-start(f32[16,1024]{1,0:T(8,128)} %constant.41.clone.sin_ref) | copy-start | bytes 196612
  25.1 15.6 %collective-permute-start = (f32[3,32,256]{2,1,0:T(8,128)S(1)}, f32[3,32,256]{2,1,0:T(8,128)S(1)}, u32[]{:S(2)}, u32[]{:S(2)}) collective-permute-start(f32[3,32,256]{2,1,0:T(8,128)S(1)} %get-tuple-element.17), channel_id=1, source_target_pairs={{5,2},{4,3},{3,4},{2,5},{9,6},{8,7},{7,8},{6,9},{13,10},{12,11},{1... | collective-permute-start | bytes 294920 | tf_op jit(solution)/shard_map/ppermute | solution.py:418
  25.9 14.8 %collective-permute-start.1 = (f32[32,256]{1,0:T(8,128)S(1)}, f32[32,256]{1,0:T(8,128)S(1)}, u32[]{:S(2)}, u32[]{:S(2)}) collective-permute-start(f32[32,256]{1,0:T(8,128)S(1)} %get-tuple-element.18), channel_id=1, source_target_pairs={{6,3},{1,4},{10,7},{5,8},{14,11},{9,12},{18,15},{13,16},{22,19},{1... | collective-permute-start | bytes 98312 | tf_op jit(solution)/shard_map/ppermute | solution.py:419
  31.7 9.0 %collective-permute-start.2 = (f32[32,256]{1,0:T(8,128)S(1)}, f32[32,256]{1,0:T(8,128)S(1)}, u32[]{:S(2)}, u32[]{:S(2)}) collective-permute-start(f32[32,256]{1,0:T(8,128)S(1)} %get-tuple-element.18), channel_id=1, source_target_pairs={{6,2},{1,5},{10,6},{5,9},{14,10},{9,13},{18,14},{13,17},{22,18},{1... | collective-permute-start | bytes 98312 | tf_op jit(solution)/shard_map/ppermute | solution.py:420
